TPU v7x, 32 devices: a whole 2x2x4 slice. The times are simulated.
32 devices in a mesh: band: 4 (over x, core), slab: 8 (over z, y).
Axes of the slice: x: 2, y: 2, z: 4, core: 2. Of those that a mesh axis runs over, the one named last changes fastest.
Arguments:
- current_image: float32 [8, 4, 2, 32, 384], P('band', None, None, 'slab'), may hold values from -6 to 6
- langevin_noise: float32 [8, 4, 2, 32, 384], P('band', None, None, 'slab'), may hold values from -6 to 6
- step_size: float32 [1], replicated, may hold values from 0.2 to 0.5
- coil_maps: bfloat16 [8, 4, 32, 2, 32, 384], P(None, None, 'band', None, 'slab'), may hold values from -1 to 1
- measured_kspace: float32 [4, 32, 2, 32, 384], P(None, 'band', None, 'slab'), may hold values from -6 to 6
- sample_mask: int32 [4, 384], replicated, may hold values 0 or 1
- caipi_steps: int32 [8], replicated, may hold values from 0 to 7
- band_order: int32 [8], replicated, may hold values from 0 to 7, each once
- weight_in: bfloat16 [64, 2, 3, 3, 3], replicated, may hold values from -0.875 to 0.875
- weight_mid: bfloat16 [64, 64, 3, 3, 3], replicated, may hold values from -0.15625 to 0.15625
- weight_out: bfloat16 [2, 64, 3, 3, 3], replicated, may hold values from -0.359375 to 0.359375
Outputs:
- next_image: float32 [8, 4, 2, 32, 384], P('band', None, None, 'slab')
Inputs may be any that keep to these rules, and one draw needn't show every extreme that they name: `sample_mask`: 1 where a phase-encode line of a slice group was sampled, else 0. `caipi_steps`: shift of a band in units of 48 columns. `band_order`: a permutation of 0 to 7.
All inputs are finite; a program needn't handle non-finite values.
Results may differ from a plain program's by a relative error of at most 0.0039.
Values may be sent and summed in bfloat16 or wider, within the bound.
No kernel may reach another device: no remote copies, remote signals or barrier semaphores. Data moves between devices by JAX's collectives and lax.ppermute only.
A program may use at most 128 MiB of HBM per device.

v0:
```python
import functools
import math

import jax
import jax.numpy as jnp
import numpy as np
from jax import lax
from jax.experimental import pallas as pl
from jax.experimental.pallas import tpu as pltpu
from jax.sharding import PartitionSpec as P


def from_behind(block, axis, distance):
    devices = range(lax.axis_size(axis))
    route = [(i - distance, i) for i in devices if i - distance in devices]
    return lax.ppermute(block, axis, route)


def split_table(table):
    high = table.astype(jnp.bfloat16)
    low = (table - high.astype(np.float64)).astype(jnp.bfloat16)
    return high, low


def dft_table(columns):
    index = np.arange(columns)
    phase = (np.outer(index, index) % columns) * (2.0 * math.pi / columns)
    factor = 1.0 / math.sqrt(columns)
    return np.concatenate([np.cos(phase), np.sin(phase)], axis=1) * factor


def moved_right(value):
    lanes = value.shape[-1]
    lane = lax.broadcasted_iota(jnp.int32, (1, lanes), 1)
    return jnp.where(lane == 0, 0.0, pltpu.roll(value, 1, 1))


def moved_left(value):
    lanes = value.shape[-1]
    lane = lax.broadcasted_iota(jnp.int32, (1, lanes), 1)
    return jnp.where(lane == lanes - 1, 0.0, pltpu.roll(value, lanes - 1, 1))


def half_silu(half):
    return half + half * jnp.tanh(half)


def table_product(source, high_ref, low_ref):
    rows = source.shape[0]
    high = source.astype(jnp.bfloat16)
    low = (source - high.astype(jnp.float32)).astype(jnp.bfloat16)
    both = jnp.dot(
        jnp.concatenate([high, low], axis=0), high_ref[...], preferred_element_type=jnp.float32
    )
    rest = jnp.dot(high, low_ref[...], preferred_element_type=jnp.float32)
    return both[:rows] + both[rows:] + rest


def consistency_kernel(
    steps_ref, order_ref, image_ref, coil_ref, kspace_ref, mask_ref, high_ref, low_ref,
    out_ref, field_ref, kdata_ref,
):
    all_positions, slices, coils, _, rows, columns = coil_ref.shape
    total = slices * coils * rows
    unit = columns // 8
    shifts = [steps_ref[order_ref[g]] * unit for g in range(all_positions)]
    chunk = 4

    for s in range(slices):
        for begin in range(0, coils, chunk):
            real_sum = jnp.zeros((chunk, rows, columns), jnp.float32)
            imag_sum = jnp.zeros((chunk, rows, columns), jnp.float32)
            for g in range(all_positions):
                coil = coil_ref[g, s, begin : begin + chunk].astype(jnp.float32)
                real_x = image_ref[g, s, 0].astype(jnp.float32)
                imag_x = image_ref[g, s, 1].astype(jnp.float32)
                real_c, imag_c = coil[:, 0], coil[:, 1]
                real_y = real_c * real_x - imag_c * imag_x
                imag_y = real_c * imag_x + imag_c * real_x
                real_sum += pltpu.roll(real_y, shifts[g], 2)
                imag_sum += pltpu.roll(imag_y, shifts[g], 2)
            for c in range(chunk):
                row = (s * coils + begin + c) * rows
                field_ref[row : row + rows, :] = real_sum[c]
                field_ref[total + row : total + row + rows, :] = imag_sum[c]
                kdata_ref[row : row + rows, :] = kspace_ref[s, begin + c, 0]
                kdata_ref[total + row : total + row + rows, :] = kspace_ref[s, begin + c, 1]

    product = table_product(field_ref[...], high_ref, low_ref)
    with_cos, with_sin = product[:, :columns], product[:, columns:]
    keep = jnp.concatenate(
        [
            jnp.broadcast_to(mask_ref[s : s + 1, :].astype(jnp.float32), (coils * rows, columns))
            for s in range(slices)
        ],
        axis=0,
    )
    real_r = keep * (with_cos[:total] + with_sin[total:] - kdata_ref[:total])
    imag_r = keep * (with_cos[total:] - with_sin[:total] - kdata_ref[total:])
    product = table_product(jnp.concatenate([real_r, imag_r], axis=0), high_ref, low_ref)
    with_cos, with_sin = product[:, :columns], product[:, columns:]
    field_ref[:total] = with_cos[:total] - with_sin[total:]
    field_ref[total:] = with_cos[total:] + with_sin[:total]

    for s in range(slices):
        real_b = []
        imag_b = []
        for c in range(coils):
            row = (s * coils + c) * rows
            real_b.append(field_ref[row : row + rows, :])
            imag_b.append(field_ref[total + row : total + row + rows, :])
        real_b = jnp.stack(real_b, axis=0)
        imag_b = jnp.stack(imag_b, axis=0)
        for g in range(all_positions):
            back = lax.rem(columns - shifts[g], columns)
            real_sum = jnp.zeros((rows, columns), jnp.float32)
            imag_sum = jnp.zeros((rows, columns), jnp.float32)
            for begin in range(0, coils, chunk):
                coil = coil_ref[g, s, begin : begin + chunk].astype(jnp.float32)
                real_c, imag_c = coil[:, 0], coil[:, 1]
                real_t = pltpu.roll(real_b[begin : begin + chunk], back, 2)
                imag_t = pltpu.roll(imag_b[begin : begin + chunk], back, 2)
                real_sum += jnp.sum(real_c * real_t + imag_c * imag_t, axis=0)
                imag_sum += jnp.sum(real_c * imag_t - imag_c * real_t, axis=0)
            out_ref[g, s, 0] = real_sum.astype(jnp.bfloat16)
            out_ref[g, s, 1] = imag_sum.astype(jnp.bfloat16)


def partial_consistency(everyone, coil_maps, measured_kspace, sample_mask, caipi_steps, band_order):
    columns = coil_maps.shape[-1]
    slices, coils, _, rows, _ = measured_kspace.shape
    total = slices * coils * rows
    high, low = split_table(dft_table(columns))
    smem = pl.BlockSpec(memory_space=pltpu.SMEM)
    vmem = pl.BlockSpec(memory_space=pltpu.VMEM)
    return pl.pallas_call(
        consistency_kernel,
        out_shape=jax.ShapeDtypeStruct(everyone.shape, jnp.bfloat16),
        in_specs=[smem, smem] + [vmem] * 6,
        out_specs=vmem,
        scratch_shapes=[
            pltpu.VMEM((2 * total, columns), jnp.float32),
            pltpu.VMEM((2 * total, columns), jnp.float32),
        ],
        compiler_params=pltpu.CompilerParams(vmem_limit_bytes=40 * 2**20),
        cost_estimate=pl.CostEstimate(flops=10**9, bytes_accessed=4 * 10**6, transcendentals=0),
    )(
        caipi_steps, band_order, everyone, coil_maps, measured_kspace, sample_mask,
        jnp.asarray(high), jnp.asarray(low),
    )


def network_kernel(
    place_ref, window_ref, first_ref, mid_ref, last_ref,
    out_ref, taps_ref, wide_ref, f1_ref, f2_ref, part_ref, score_ref,
):
    channels = mid_ref.shape[-1]
    out_slices, _, columns = out_ref.shape
    slices1, slices2 = out_slices + 4, out_slices + 2
    lower_slice, upper_slice = place_ref[0] == 0, place_ref[0] == place_ref[1] - 1
    lower_row, upper_row = place_ref[2] == 0, place_ref[2] == place_ref[3] - 1
    four, two = 4 * channels, 2 * channels

    for t in range(3):
        for a in range(2):
            for r in range(2):
                row = ((t * 2 + a) * 2 + r) * channels
                for d in range(4):
                    for pair in range(2):
                        blocks = []
                        for q in (2 * pair, 2 * pair + 1):
                            if 0 <= d - a <= 2 and 0 <= q - r <= 2:
                                blocks.append(mid_ref[d - a, q - r, t] * jnp.bfloat16(0.5))
                            else:
                                blocks.append(jnp.zeros((channels, channels), jnp.bfloat16))
                        col = (d * 4 + 2 * pair) * channels
                        wide_ref[row : row + channels, col : col + two] = jnp.concatenate(
                            blocks, axis=1
                        )

    for g in range(2):
        base = window_ref[g].astype(jnp.float32)
        taps_ref[g, 0] = moved_right(base).astype(jnp.bfloat16)
        taps_ref[g, 1] = window_ref[g]
        taps_ref[g, 2] = moved_left(base).astype(jnp.bfloat16)

    def first_layer(z, carry):
        for g in range(2):
            begin = pl.multiple_of(16 * z, 16)
            source = jnp.concatenate(
                [taps_ref[g, t, pl.ds(begin, 48), :] for t in range(3)], axis=0
            )
            half = jnp.dot(first_ref[...], source, preferred_element_type=jnp.float32)
            f1_ref[z, four * g : four * (g + 1), :] = half_silu(half).astype(jnp.bfloat16)
        return carry

    lax.fori_loop(0, slices1, first_layer, 0)

    @pl.when(lower_slice)
    def _():
        f1_ref[0:2] = jnp.zeros_like(f1_ref[0:2])

    @pl.when(upper_slice)
    def _():
        f1_ref[slices1 - 2 :] = jnp.zeros_like(f1_ref[slices1 - 2 :])

    @pl.when(lower_row)
    def _():
        f1_ref[:, :two, :] = jnp.zeros_like(f1_ref[:, :two, :])

    @pl.when(upper_row)
    def _():
        f1_ref[:, 3 * two :, :] = jnp.zeros_like(f1_ref[:, 3 * two :, :])

    def second_layer(step, carry):
        z = 2 * step
        for pair in range(3):
            source = f1_ref[pl.ds(z, 4), two * pair : two * pair + four, :]
            part_ref[...] = jnp.dot(
                wide_ref[...],
                source.reshape(4 * four, columns),
                preferred_element_type=jnp.float32,
            )
            for a in range(2):
                for r in range(2):
                    row = (a * 2 + r) * channels
                    half = (
                        moved_right(part_ref[row : row + channels])
                        + part_ref[four + row : four + row + channels]
                        + moved_left(part_ref[2 * four + row : 2 * four + row + channels])
                    )
                    place = two * pair + r * channels
                    f2_ref[z + a, place : place + channels, :] = half_silu(half).astype(
                        jnp.bfloat16
                    )
        return carry

    lax.fori_loop(0, slices2 // 2, second_layer, 0)

    @pl.when(lower_slice)
    def _():
        f2_ref[0] = jnp.zeros_like(f2_ref[0])

    @pl.when(upper_slice)
    def _():
        f2_ref[slices2 - 1] = jnp.zeros_like(f2_ref[slices2 - 1])

    @pl.when(lower_row)
    def _():
        f2_ref[:, :channels, :] = jnp.zeros_like(f2_ref[:, :channels, :])

    @pl.when(upper_row)
    def _():
        f2_ref[:, 5 * channels :, :] = jnp.zeros_like(f2_ref[:, 5 * channels :, :])

    for z in range(slices2):
        score_ref[z] = jnp.dot(last_ref[...], f2_ref[z], preferred_element_type=jnp.float32)

    for z in range(out_slices):
        taps = []
        for t in range(3):
            taps.append(
                sum(score_ref[z + d, (3 * d + t) * 8 : (3 * d + t + 1) * 8, :] for d in range(3))
            )
        out_ref[z] = moved_right(taps[0]) + taps[1] + moved_left(taps[2])


def score_network(place, windows, weight_in, weight_mid, weight_out):
    channels = weight_mid.shape[0]
    slices0, columns = windows.shape[1] // 16, windows.shape[-1]
    out_slices = slices0 - 6
    first = jnp.stack(
        [jnp.pad(weight_in, ((0, 0), (0, 0), (0, 0), (r, 5 - r), (0, 0))) for r in range(4)]
    )
    first = jnp.transpose(first, (0, 1, 5, 3, 2, 4)).reshape(4 * channels, 144)
    first = first * jnp.bfloat16(0.5)
    mid = jnp.transpose(weight_mid, (2, 3, 4, 0, 1))
    last = jnp.stack(
        [jnp.pad(weight_out, ((0, 0), (0, 0), (0, 0), (r, 3 - r), (0, 0))) for r in range(4)]
    )
    last = jnp.transpose(last, (3, 5, 1, 0, 4, 2)).reshape(72, 6 * channels)
    smem = pl.BlockSpec(memory_space=pltpu.SMEM)
    vmem = pl.BlockSpec(memory_space=pltpu.VMEM)
    return pl.pallas_call(
        network_kernel,
        out_shape=jax.ShapeDtypeStruct((out_slices, 8, columns), jnp.float32),
        in_specs=[smem] + [vmem] * 4,
        out_specs=vmem,
        scratch_shapes=[
            pltpu.VMEM((2, 3, slices0 * 16, columns), jnp.bfloat16),
            pltpu.VMEM((12 * channels, 16 * channels), jnp.bfloat16),
            pltpu.VMEM((out_slices + 4, 8 * channels, columns), jnp.bfloat16),
            pltpu.VMEM((out_slices + 2, 6 * channels, columns), jnp.bfloat16),
            pltpu.VMEM((12 * channels, columns), jnp.float32),
            pltpu.VMEM((out_slices + 2, 72, columns), jnp.float32),
        ],
        compiler_params=pltpu.CompilerParams(vmem_limit_bytes=40 * 2**20),
        cost_estimate=pl.CostEstimate(
            flops=10**10, bytes_accessed=2 * 10**6, transcendentals=4 * 10**6
        ),
    )(place, windows, first, mid, last)


def per_device(
    current_image, langevin_noise, step_size, coil_maps, measured_kspace, sample_mask,
    caipi_steps, band_order, weight_in, weight_mid, weight_out,
):
    positions, group_slices, _, row_count, columns = current_image.shape
    local_slices = positions * group_slices
    everyone = lax.all_gather(current_image.astype(jnp.bfloat16), "band", axis=0, tiled=True)

    volume = everyone.reshape(-1, 2, row_count, columns)
    volume = jnp.pad(volume, ((3, 3), (0, 0), (0, 0), (0, 0)))
    tall = lax.dynamic_slice_in_dim(
        volume, lax.axis_index("band") * local_slices, local_slices + 6, axis=0
    )
    below = from_behind(tall[:, :, row_count - 3 :, :], "slab", 1)
    above = from_behind(tall[:, :, :3, :], "slab", -1)
    field = jnp.concatenate([below, tall, above, jnp.zeros_like(above[:, :, :2])], axis=2)
    windows = jnp.stack(
        [field[:, :, 4 * g : 4 * g + 8].reshape(-1, columns) for g in range(2)], axis=0
    )
    place = jnp.stack(
        [
            lax.axis_index("band"),
            jnp.int32(lax.axis_size("band")),
            lax.axis_index("slab"),
            jnp.int32(lax.axis_size("slab")),
        ]
    ).astype(jnp.int32)

    partial_sums = partial_consistency(
        everyone, coil_maps, measured_kspace, sample_mask, caipi_steps, band_order
    )
    swapped = lax.all_to_all(partial_sums, "band", split_axis=0, concat_axis=0, tiled=True)
    score = score_network(place, windows, weight_in, weight_mid, weight_out)
    score_field = score.reshape(positions, group_slices, 2, row_count, columns)
    pieces = swapped.reshape((-1, positions) + swapped.shape[1:]).astype(jnp.float32)
    consistency = jnp.sum(pieces, axis=0)
    step_value = step_size[0]
    return (
        current_image
        + step_value * (score_field - consistency)
        + jnp.sqrt(2.0 * step_value) * langevin_noise
    )


def solution(mesh):
    band5 = P("band", None, None, "slab", None)
    in_specs = (
        band5,
        band5,
        P(),
        P(None, None, "band", None, "slab", None),
        P(None, "band", None, "slab", None),
        P(), P(), P(), P(), P(), P(),
    )
    return jax.shard_map(
        per_device, mesh=mesh, in_specs=in_specs, out_specs=band5, check_vma=False
    )
```

profile of v0, /device:TPU:0, one launch (start us, length us, event | category | flops | bytes accessed | tf_op | source)
XLA Modules:
  0.0 53.7 jit_solution(17191510269791492757)
XLA Ops:
  0.0 0.9 %convert_element_type.27 = bf16[2,4,2,4,384]{4,3,2,1,0:T(4,128)(2,1)S(1)} convert(f32[2,4,2,4,384]{4,3,2,1,0:T(4,128)} %param.13) | non-fusion elementwise | flops 24576 | bytes 147456 | tf_op jit(solution)/shard_map/convert_element_type | solution.py:310
  0.9 6.8 %all_gather.3.image_ref = bf16[8,4,2,4,384]{4,3,2,1,0:T(4,128)(2,1)S(1)} all-gather(bf16[2,4,2,4,384]{4,3,2,1,0:T(4,128)(2,1)S(1)} %convert_element_type.27), channel_id=1, replica_groups=mesh['band'=4,'slab'=8] {'band'}, dimensions={0}, use_global_device_ids=true | all-gather | bytes 245760 | tf_op jit(solution)/shard_map/all_gather | solution.py:310
  7.8 0.1 pad_dynamic-slice_fusion.1
  7.9 1.3 %collective-permute-start.1 = (bf16[14,2,3,384]{3,2,1,0:T(4,128)(2,1)S(1)}, bf16[14,2,3,384]{3,2,1,0:T(4,128)(2,1)S(1)}, u32[]{:S(2)}, u32[]{:S(2)}) collective-permute-start(bf16[14,2,3,384]{3,2,1,0:T(4,128)(2,1)S(1)} %get-tuple-element.6), channel_id=1, source_target_pairs={{1,0},{2,1},{3,2},{4,3},{5,4},{6,5},{7,6},{9,8},{10,9},{11,10},{12... | collective-permute-start | bytes 193544 | tf_op jit(solution)/shard_map/ppermute | solution.py:16
  9.2 4.6 %collective-permute-start = (bf16[14,2,3,384]{3,2,1,0:T(4,128)(2,1)S(1)}, bf16[14,2,3,384]{3,2,1,0:T(4,128)(2,1)S(1)}, u32[]{:S(2)}, u32[]{:S(2)}) collective-permute-start(bf16[14,2,3,384]{3,2,1,0:T(4,128)(2,1)S(1)} %get-tuple-element.5), channel_id=1, source_target_pairs={{0,1},{1,2},{2,3},{3,4},{4,5},{5,6},{6,7},{8,9},{9,10},{10,11},{11... | collective-permute-start | bytes 193544 | tf_op jit(solution)/shard_map/ppermute | solution.py:16
  13.7 0.0 copy-start
  13.7 1.4 %copy-done = bf16[8,4,8,2,4,384]{5,4,3,2,1,0:T(4,128)(2,1)S(1)} copy-done((bf16[8,4,8,2,4,384]{5,4,3,2,1,0:T(4,128)(2,1)S(1)}, bf16[8,4,8,2,4,384]{5,4,3,2,1,0:T(4,128)(2,1)}, u32[]{:S(2)}) %copy-start) | copy-done | bytes 1572888
  15.1 0.0 copy-start.2
  15.1 1.0 %copy-done.2 = f32[4,8,2,4,384]{4,3,2,1,0:T(4,128)S(1)} copy-done((f32[4,8,2,4,384]{4,3,2,1,0:T(4,128)S(1)}, f32[4,8,2,4,384]{4,3,2,1,0:T(4,128)}, u32[]{:S(2)}) %copy-start.2) | copy-done | bytes 393240
  16.1 0.0 copy-start.3
  16.1 0.7 %copy-done.3 = s32[4,384]{1,0:T(4,128)S(1)} copy-done((s32[4,384]{1,0:T(4,128)S(1)}, s32[4,384]{1,0:T(4,128)}, u32[]{:S(2)}) %copy-start.3) | copy-done | bytes 6168
  16.8 0.0 copy-start.4
  16.8 0.7 %copy-done.4 = s32[8]{0:T(128)S(1)} copy-done((s32[8]{0:T(128)S(1)}, s32[8]{0:T(128)}, u32[]{:S(2)}) %copy-start.4) | copy-done | bytes 56
  17.5 0.0 copy-start.5
  17.5 0.7 %copy-done.5 = s32[8]{0:T(128)S(1)} copy-done((s32[8]{0:T(128)S(1)}, s32[8]{0:T(128)}, u32[]{:S(2)}) %copy-start.5) | copy-done | bytes 56
  18.1 0.0 copy-start.6
  18.1 1.1 %copy-done.6 = bf16[384,768]{1,0:T(8,128)(2,1)S(1)} copy-done((bf16[384,768]{1,0:T(8,128)(2,1)S(1)}, bf16[384,768]{1,0:T(8,128)(2,1)}, u32[]{:S(2)}) %copy-start.6) | copy-done | bytes 589848
  19.2 0.0 copy-start.7
  19.2 1.1 %copy-done.7 = bf16[384,768]{1,0:T(8,128)(2,1)S(1)} copy-done((bf16[384,768]{1,0:T(8,128)(2,1)S(1)}, bf16[384,768]{1,0:T(8,128)(2,1)}, u32[]{:S(2)}) %copy-start.7) | copy-done | bytes 589848
  20.3 0.0 copy-start.10
  20.3 7.1 %shard_map.128 = bf16[8,4,2,4,384]{4,3,2,1,0:T(4,128)(2,1)} custom-call(s32[8]{0:T(128)S(1)} %copy-done.4, s32[8]{0:T(128)S(1)} %copy-done.5, bf16[8,4,2,4,384]{4,3,2,1,0:T(4,128)(2,1)S(1)} %all_gather.3.image_ref, bf16[8,4,8,2,4,384]{5,4,3,2,1,0:T(4,128)(2,1)S(1)} %copy-done, f32[4,8,2,4,384]{4,3,2,1,0:T(4,128)S(1)} %copy-done.2, s32[4,384]{1,0:T(4,128)S(1)} %copy-done.3, ...), custom_call_target="tpu_custom_call" | custom-call | flops 1000000000 | bytes 4000000 | tf_op jit(solution)/shard_map/pallas_call | solution.py:136
  27.4 0.0 copy-start.11
  27.4 3.5 %all-to-all-start = ((bf16[8,4,2,4,384]{4,3,2,1,0:T(4,128)(2,1)}), bf16[8,4,2,4,384]{4,3,2,1,0:T(4,128)(2,1)S(1)}, u32[]{:S(2)}, u32[]{:S(2)}) async-start(bf16[8,4,2,4,384]{4,3,2,1,0:T(4,128)(2,1)} %shard_map.128), calls=%async_computation | async-start | bytes 393216 | tf_op jit(solution)/shard_map/all_to_all | solution.py:335
  30.9 0.1 pad_dynamic-slice_fusion.2
  31.0 0.1 pad_slice_fusion
  31.0 0.0 copy-done.10
  31.0 0.1 pad_bitcast_fusion.3
  31.1 0.0 copy-start.1
  31.1 0.3 fusion.1
  31.5 0.1 copy.19
  31.5 0.2 mul.30
  31.7 0.1 copy.21.first_ref
  31.8 0.0 copy-done.11
  31.8 0.1 pad_bitcast_fusion.7
  31.9 0.2 maximum_bitcast_fusion
  32.1 0.2 reshape.16.last_ref
  33.0 0.1 pad_add_fusion.place_ref
  33.1 0.0 collective-permute-done.1
  33.1 0.0 collective-permute-done
  33.1 0.2 pad_maximum_fusion.2
  33.4 0.0 copy-done.1
  33.4 0.0 copy-start.8
  33.4 0.0 copy-start.9
  33.4 19.4 %shard_map.127 = f32[8,8,384]{2,1,0:T(8,128)S(1)} custom-call(s32[4]{0:T(128)S(1)} %pad_add_fusion.place_ref, bf16[2,224,384]{2,1,0:T(8,128)(2,1)S(1)} %pad_maximum_fusion.window_ref, bf16[256,144]{1,0:T(8,128)(2,1)S(1)} %copy.21.first_ref, bf16[3,3,3,64,64]{4,3,2,1,0:T(8,128)(2,1)S(1)} %bitcast.40, bf16[72,384]{1,0:T(8,128)(2,1)S(1)} %reshape.16.last_ref), custom_call_target="tpu_custom_call" | custom-call | flops 10000000000 | bytes 2000000 | tf_op jit(solution)/shard_map/pallas_call | solution.py:284
  52.9 0.0 all-to-all-done
  52.9 0.1 convert_reduce_fusion
  53.0 0.0 copy-done.8
  53.0 0.0 copy-done.9
  53.0 0.7 %multiply_add_fusion = f32[2,4,1,8,384]{4,3,2,1,0:T(8,128)} fusion(f32[2,4,1,8,384]{4,3,2,1,0:T(8,128)S(1)} %bitcast.47, f32[2,4,1,8,384]{4,3,2,1,0:T(8,128)S(1)} %bitcast.44, f32[2,4,1,8,384]{4,3,2,1,0:T(8,128)S(1)} %bitcast.45, f32[2,4,1,8,384]{4,3,2,1,0:T(8,128)S(1)} %bitcast.46, f32[]{:T(128)S(6)} %sqrt.3, f32[]{:T(128)} %bitcast.36), kind=kLoop, calls=%fused_computation.12 | loop fusion | flops 122880 | bytes 491528 | tf_op jit(solution)/shard_map/add | solution.py:342
  (4 shorter events, 0.1 us)
Async XLA Ops:
  7.9 25.2 %collective-permute-start.1 = (bf16[14,2,3,384]{3,2,1,0:T(4,128)(2,1)S(1)}, bf16[14,2,3,384]{3,2,1,0:T(4,128)(2,1)S(1)}, u32[]{:S(2)}, u32[]{:S(2)}) collective-permute-start(bf16[14,2,3,384]{3,2,1,0:T(4,128)(2,1)S(1)} %get-tuple-element.6), channel_id=1, source_target_pairs={{1,0},{2,1},{3,2},{4,3},{5,4},{6,5},{7,6},{9,8},{10,9},{11,10},{12... | collective-permute-start | bytes 193544 | tf_op jit(solution)/shard_map/ppermute | solution.py:16
  9.2 23.9 %collective-permute-start = (bf16[14,2,3,384]{3,2,1,0:T(4,128)(2,1)S(1)}, bf16[14,2,3,384]{3,2,1,0:T(4,128)(2,1)S(1)}, u32[]{:S(2)}, u32[]{:S(2)}) collective-permute-start(bf16[14,2,3,384]{3,2,1,0:T(4,128)(2,1)S(1)} %get-tuple-element.5), channel_id=1, source_target_pairs={{0,1},{1,2},{2,3},{3,4},{4,5},{5,6},{6,7},{8,9},{9,10},{10,11},{11... | collective-permute-start | bytes 193544 | tf_op jit(solution)/shard_map/ppermute | solution.py:16
  13.7 1.4 %copy-start = (bf16[8,4,8,2,4,384]{5,4,3,2,1,0:T(4,128)(2,1)S(1)}, bf16[8,4,8,2,4,384]{5,4,3,2,1,0:T(4,128)(2,1)}, u32[]{:S(2)}) copy-start(bf16[8,4,8,2,4,384]{5,4,3,2,1,0:T(4,128)(2,1)} %coil_ref.1) | copy-start | bytes 4718596
  15.1 1.0 %copy-start.2 = (f32[4,8,2,4,384]{4,3,2,1,0:T(4,128)S(1)}, f32[4,8,2,4,384]{4,3,2,1,0:T(4,128)}, u32[]{:S(2)}) copy-start(f32[4,8,2,4,384]{4,3,2,1,0:T(4,128)} %kspace_ref.1) | copy-start | bytes 1179652
  16.1 0.7 %copy-start.3 = (s32[4,384]{1,0:T(4,128)S(1)}, s32[4,384]{1,0:T(4,128)}, u32[]{:S(2)}) copy-start(s32[4,384]{1,0:T(4,128)} %mask_ref.1) | copy-start | bytes 18436
  16.8 0.7 %copy-start.4 = (s32[8]{0:T(128)S(1)}, s32[8]{0:T(128)}, u32[]{:S(2)}) copy-start(s32[8]{0:T(128)} %steps_ref.1) | copy-start | bytes 100
  17.5 0.7 %copy-start.5 = (s32[8]{0:T(128)S(1)}, s32[8]{0:T(128)}, u32[]{:S(2)}) copy-start(s32[8]{0:T(128)} %order_ref.1) | copy-start | bytes 100
  18.1 1.1 %copy-start.6 = (bf16[384,768]{1,0:T(8,128)(2,1)S(1)}, bf16[384,768]{1,0:T(8,128)(2,1)}, u32[]{:S(2)}) copy-start(bf16[384,768]{1,0:T(8,128)(2,1)} %constant.31.clone.high_ref) | copy-start | bytes 1769476
  19.2 1.1 %copy-start.7 = (bf16[384,768]{1,0:T(8,128)(2,1)S(1)}, bf16[384,768]{1,0:T(8,128)(2,1)}, u32[]{:S(2)}) copy-start(bf16[384,768]{1,0:T(8,128)(2,1)} %constant.32.clone.low_ref) | copy-start | bytes 1769476
  20.3 10.8 %copy-start.10 = (bf16[64,2,3,3,3]{0,1,4,3,2:T(2,128)(2,1)S(1)}, bf16[64,2,3,3,3]{0,1,4,3,2:T(2,128)(2,1)}, u32[]{:S(2)}) copy-start(bf16[64,2,3,3,3]{0,1,4,3,2:T(2,128)(2,1)} %param.21) | copy-start | bytes 20740
  27.4 4.4 %copy-start.11 = (bf16[2,64,3,3,3]{1,0,4,3,2:T(2,128)(2,1)S(1)}, bf16[2,64,3,3,3]{1,0,4,3,2:T(2,128)(2,1)}, u32[]{:S(2)}) copy-start(bf16[2,64,3,3,3]{1,0,4,3,2:T(2,128)(2,1)} %param.23) | copy-start | bytes 20740
  27.4 25.5 %all-to-all-start = ((bf16[8,4,2,4,384]{4,3,2,1,0:T(4,128)(2,1)}), bf16[8,4,2,4,384]{4,3,2,1,0:T(4,128)(2,1)S(1)}, u32[]{:S(2)}, u32[]{:S(2)}) async-start(bf16[8,4,2,4,384]{4,3,2,1,0:T(4,128)(2,1)} %shard_map.128), calls=%async_computation | async-start | bytes 393216 | tf_op jit(solution)/shard_map/all_to_all | solution.py:335
  31.1 2.2 %copy-start.1 = (bf16[64,64,3,3,3]{1,0,4,3,2:T(8,128)(2,1)S(1)}, bf16[64,64,3,3,3]{1,0,4,3,2:T(8,128)(2,1)}, u32[]{:S(2)}) copy-start(bf16[64,64,3,3,3]{1,0,4,3,2:T(8,128)(2,1)} %param.22) | copy-start | bytes 663556
  33.4 19.6 %copy-start.8 = (f32[2,4,2,4,384]{4,3,2,1,0:T(4,128)S(1)}, f32[2,4,2,4,384]{4,3,2,1,0:T(4,128)}, u32[]{:S(2)}) copy-start(f32[2,4,2,4,384]{4,3,2,1,0:T(4,128)} %param.13) | copy-start | bytes 294916
  33.4 19.6 %copy-start.9 = (f32[2,4,2,4,384]{4,3,2,1,0:T(4,128)S(1)}, f32[2,4,2,4,384]{4,3,2,1,0:T(4,128)}, u32[]{:S(2)}) copy-start(f32[2,4,2,4,384]{4,3,2,1,0:T(4,128)} %param.14) | copy-start | bytes 294916
where the time goes:
time: 54.6 us; the launch traced here: 53.7 us
  Pallas kernels  26.5 us (49%)
  starting transfers between devices  9.34 us (17%)
  local copies, waits for them, and re-layouts  7.47 us (14%)
  blocking collectives  6.84 us (13%)
  other arithmetic  2.57 us (5%)
  between operations  0.9 us (2%)
    pallas_call x1, Pallas kernels, score_network(): pl.pallas_call(network_kernel, out_shape=jax.ShapeDtypeStruct((out_slices...  19.4 us
    pallas_call x1, Pallas kernels, partial_consistency(): pl.pallas_call(consistency_kernel, out_shape=jax.ShapeDtypeStruct(everyon...  7.11 us
    all_gather x1, blocking collectives, per_device(): lax.all_gather(current_image.astype(jnp.bfloat16), 'band', axis=0, tiled=...  6.84 us
    unnamed x24, local copies, waits for them, and re-layouts  6.55 us
    ppermute x2, starting transfers between devices, from_behind(): return lax.ppermute(block, axis, route)  5.84 us
    all_to_all x1, starting transfers between devices, per_device(): lax.all_to_all(partial_sums, 'band', split_axis=0, concat_axis=0, tiled=T...  3.5 us
  transfers between devices with their start and end apart: 3, of which 0 were waited for; matrix products, arithmetic and copies ran while one was open for 3% of the time, Pallas kernels for 49%

commit v1 on v0

v1 whole, which is shorter than its diff:
```python
import functools
import math

import jax
import jax.numpy as jnp
import numpy as np
from jax import lax
from jax.experimental import pallas as pl
from jax.experimental.pallas import tpu as pltpu
from jax.sharding import PartitionSpec as P


def from_behind(block, axis, distance):
    devices = range(lax.axis_size(axis))
    route = [(i - distance, i) for i in devices if i - distance in devices]
    return lax.ppermute(block, axis, route)


def split_table(table):
    high = table.astype(jnp.bfloat16)
    low = (table - high.astype(np.float64)).astype(jnp.bfloat16)
    return high, low


def dft_table(columns):
    index = np.arange(columns)
    phase = (np.outer(index, index) % columns) * (2.0 * math.pi / columns)
    factor = 1.0 / math.sqrt(columns)
    return np.concatenate([np.cos(phase), np.sin(phase)], axis=1) * factor


def moved_right(value):
    lanes = value.shape[-1]
    lane = lax.broadcasted_iota(jnp.int32, (1, lanes), 1)
    return jnp.where(lane == 0, 0.0, pltpu.roll(value, 1, 1))


def moved_left(value):
    lanes = value.shape[-1]
    lane = lax.broadcasted_iota(jnp.int32, (1, lanes), 1)
    return jnp.where(lane == lanes - 1, 0.0, pltpu.roll(value, lanes - 1, 1))


def half_silu(half):
    return half + half * jnp.tanh(half)


def table_product(source, high_ref, low_ref):
    rows = source.shape[0]
    high = source.astype(jnp.bfloat16)
    low = (source - high.astype(jnp.float32)).astype(jnp.bfloat16)
    both = jnp.dot(
        jnp.concatenate([high, low], axis=0), high_ref[...], preferred_element_type=jnp.float32
    )
    rest = jnp.dot(high, low_ref[...], preferred_element_type=jnp.float32)
    return both[:rows] + both[rows:] + rest


def halves_swapped(value):
    return pltpu.roll(value, 4, value.ndim - 2)


def upper_half(value):
    return lax.broadcasted_iota(jnp.int32, value.shape, value.ndim - 2) < 4


def signed_swap(value, top, bottom):
    sign = jnp.where(upper_half(value), top, bottom)
    return sign * halves_swapped(value)


def stacked_parts(value):
    return jnp.concatenate([value[..., 0, :, :], value[..., 1, :, :]], axis=-2)


def turned_tiles(value, shift, store):
    tiles = value.shape[-1] // 128
    whole, part = shift // 128, lax.rem(shift, 128)
    moved = [
        pltpu.roll(value[..., 128 * j : 128 * (j + 1)], part, value.ndim - 1) for j in range(tiles)
    ]
    lane = lax.broadcasted_iota(jnp.int32, moved[0].shape, value.ndim - 1)
    for j in range(tiles):
        store(lax.rem(j + whole, tiles), jnp.where(lane < part, moved[j - 1], moved[j]))


def consistency_kernel(
    image_ref, steps_hbm, order_hbm, size_hbm, coil_hbm, kspace_hbm, mask_hbm, high_hbm, low_hbm,
    out_ref,
    steps_ref, order_ref, size_ref, coil_ref, kspace_ref, mask_ref, high_ref, low_ref,
    turned_ref, real_ref, imag_ref, field_ref, swap_ref, sum_ref, sems, coil_sems,
):
    all_positions, slices, coils, _, rows, columns = coil_ref.shape
    tiles = columns // 128
    unit = columns // 8
    pairs = (
        (steps_hbm, steps_ref), (order_hbm, order_ref), (size_hbm, size_ref),
        (kspace_hbm, kspace_ref), (mask_hbm, mask_ref), (high_hbm, high_ref), (low_hbm, low_ref),
    )
    copies = [pltpu.make_async_copy(src, dst, sems.at[i]) for i, (src, dst) in enumerate(pairs)]
    for copy in copies[:3]:
        copy.start()
    for g in range(all_positions):
        pltpu.make_async_copy(coil_hbm.at[g], coil_ref.at[g], coil_sems.at[g]).start()
    for copy in copies[3:]:
        copy.start()
    for copy in copies[:3]:
        copy.wait()

    def shift_of(g):
        return steps_ref[order_ref[g]] * unit

    def turn_coils(g, carry):
        shift = shift_of(g)
        image = image_ref[g].astype(jnp.float32)

        def store_image(j, value):
            other = halves_swapped(value)
            top = upper_half(value)
            real_ref[j, g] = jnp.where(top, value, other)
            imag_ref[j, g] = jnp.where(top, other, value)

        turned_tiles(image, shift, store_image)
        pltpu.make_async_copy(coil_hbm.at[g], coil_ref.at[g], coil_sems.at[g]).wait()
        for s in range(slices):
            coil = stacked_parts(coil_ref[g, s].astype(jnp.float32))

            def store_coil(j, value, s=s):
                turned_ref[j, g, s] = value

            turned_tiles(coil, shift, store_coil)
        return carry

    lax.fori_loop(0, all_positions, turn_coils, 0)

    block = coils * 2 * rows
    for j in range(tiles):
        for s in range(slices):
            with_real = jnp.zeros((coils, 2 * rows, 128), jnp.float32)
            with_imag = jnp.zeros((coils, 2 * rows, 128), jnp.float32)
            for g in range(all_positions):
                coil = turned_ref[j, g, s]
                with_real += coil * real_ref[j, g, s]
                with_imag += coil * imag_ref[j, g, s]
            total = with_real + signed_swap(with_imag, -1.0, 1.0)
            field_ref[s * block : (s + 1) * block, 128 * j : 128 * (j + 1)] = total.reshape(
                block, 128
            )

    for copy in copies[3:]:
        copy.wait()
    product = table_product(field_ref[...], high_ref, low_ref)
    grouped = (slices, coils, 2 * rows, columns)
    with_cos = product[:, :columns].reshape(grouped)
    with_sin = product[:, columns:].reshape(grouped)
    spectrum = with_cos + signed_swap(with_sin, 1.0, -1.0)
    keep = mask_ref[...].astype(jnp.float32).reshape(slices, 1, 1, columns)
    residual = keep * (spectrum - stacked_parts(kspace_ref[...]))
    product = table_product(residual.reshape(slices * block, columns), high_ref, low_ref)
    with_cos = product[:, :columns].reshape(grouped)
    with_sin = product[:, columns:].reshape(grouped)
    back = with_cos + signed_swap(with_sin, -1.0, 1.0)
    field_ref[...] = back.reshape(slices * block, columns)
    swap_ref[...] = halves_swapped(back).reshape(slices * block, columns)

    size = size_ref[0]
    for j in range(tiles):
        for s in range(slices):
            place = (slice(s * block, (s + 1) * block), slice(128 * j, 128 * (j + 1)))
            field = field_ref[place].reshape(coils, 2 * rows, 128)
            swapped = swap_ref[place].reshape(coils, 2 * rows, 128)
            for g in range(all_positions):
                coil = turned_ref[j, g, s]
                straight = jnp.sum(coil * field, axis=0)
                crossed = jnp.sum(coil * swapped, axis=0)
                straight = straight + halves_swapped(straight)
                crossed = halves_swapped(crossed) - crossed
                sum_ref[g, s, :, 128 * j : 128 * (j + 1)] = size * jnp.where(
                    upper_half(straight), straight, crossed
                )

    def turn_sums(g, carry):
        back_shift = lax.rem(columns - shift_of(g), columns)
        turned = pltpu.roll(sum_ref[g], back_shift, 2).astype(jnp.bfloat16)
        out_ref[g, :, 0] = turned[:, :rows]
        out_ref[g, :, 1] = turned[:, rows:]
        return carry

    lax.fori_loop(0, all_positions, turn_sums, 0)


def partial_consistency(
    everyone, step_size, coil_maps, measured_kspace, sample_mask, caipi_steps, band_order
):
    all_positions, slices, coils, _, rows, columns = coil_maps.shape
    total = slices * coils * 2 * rows
    high, low = split_table(dft_table(columns))
    hbm = pl.BlockSpec(memory_space=pltpu.HBM)
    vmem = pl.BlockSpec(memory_space=pltpu.VMEM)
    tile_shape = (columns // 128, all_positions, slices)
    return pl.pallas_call(
        consistency_kernel,
        out_shape=jax.ShapeDtypeStruct((all_positions, slices, 2, rows, columns), jnp.bfloat16),
        in_specs=[vmem] + [hbm] * 8,
        out_specs=vmem,
        scratch_shapes=[
            pltpu.SMEM(caipi_steps.shape, jnp.int32),
            pltpu.SMEM(band_order.shape, jnp.int32),
            pltpu.SMEM(step_size.shape, jnp.float32),
            pltpu.VMEM(coil_maps.shape, jnp.bfloat16),
            pltpu.VMEM(measured_kspace.shape, jnp.float32),
            pltpu.VMEM(sample_mask.shape, jnp.int32),
            pltpu.VMEM(high.shape, jnp.bfloat16),
            pltpu.VMEM(low.shape, jnp.bfloat16),
            pltpu.VMEM(tile_shape + (coils, 2 * rows, 128), jnp.float32),
            pltpu.VMEM(tile_shape + (2 * rows, 128), jnp.float32),
            pltpu.VMEM(tile_shape + (2 * rows, 128), jnp.float32),
            pltpu.VMEM((total, columns), jnp.float32),
            pltpu.VMEM((total, columns), jnp.float32),
            pltpu.VMEM((all_positions, slices, 2 * rows, columns), jnp.float32),
            pltpu.SemaphoreType.DMA((7,)),
            pltpu.SemaphoreType.DMA((all_positions,)),
        ],
        compiler_params=pltpu.CompilerParams(vmem_limit_bytes=48 * 2**20),
        cost_estimate=pl.CostEstimate(flops=10**9, bytes_accessed=4 * 10**6, transcendentals=0),
    )(
        everyone, caipi_steps, band_order, step_size, coil_maps, measured_kspace, sample_mask,
        jnp.asarray(high), jnp.asarray(low),
    )


def network_kernel(
    window_ref, size_hbm, first_hbm, mid_hbm, last_hbm, image_hbm, noise_hbm,
    out_ref,
    size_ref, first_raw, mid_raw, last_raw, image_ref, noise_ref,
    first_sum, last_sum, first_ref, wide_ref, last_ref,
    taps_ref, f1_ref, f2_ref, part_a, part_b, score_ref, sems,
):
    channels = mid_raw.shape[-1]
    out_slices, _, rows, columns = out_ref.shape
    slices1, slices2 = out_slices + 4, out_slices + 2
    pairs = (
        (first_hbm, first_raw), (mid_hbm, mid_raw), (last_hbm, last_raw),
        (size_hbm, size_ref), (image_hbm, image_ref), (noise_hbm, noise_ref),
    )
    copies = [pltpu.make_async_copy(src, dst, sems.at[i]) for i, (src, dst) in enumerate(pairs)]
    for copy in copies:
        copy.start()

    def inside(axis, end):
        edge = lax.axis_size(axis) - 1 if end else 0
        return jnp.where(lax.axis_index(axis) == edge, 0.0, 1.0).astype(jnp.float32)

    low_slice, high_slice = inside("band", False), inside("band", True)
    low_row, high_row = inside("slab", False), inside("slab", True)
    four, two = 4 * channels, 2 * channels

    for g in range(2):
        base = window_ref[g].astype(jnp.float32)
        taps_ref[g, 0] = moved_right(base).astype(jnp.bfloat16)
        taps_ref[g, 1] = window_ref[g]
        taps_ref[g, 2] = moved_left(base).astype(jnp.bfloat16)

    first_sum[...] = jnp.zeros_like(first_sum)
    copies[0].wait()
    for d in range(3):
        for u in range(3):
            for t in range(3):
                block = first_raw[d, u, t].astype(jnp.float32) * 0.5
                for i in range(2):
                    for r in range(4):
                        row = (t * 3 + d) * 16 + i * 8 + u + r
                        first_sum[row : row + 1, r * channels : (r + 1) * channels] = block[
                            i : i + 1
                        ]
    first_ref[...] = first_sum[...].T[:, : first_ref.shape[1]].astype(jnp.bfloat16)

    copies[1].wait()
    half_weight = jnp.bfloat16(0.5)
    for t in range(3):
        for r in range(2):
            row = (t * 2 + r) * channels
            for d in range(3):
                for pair in range(2):
                    blocks = []
                    for q in (2 * pair, 2 * pair + 1):
                        if 0 <= q - r <= 2:
                            blocks.append(mid_raw[d, q - r, t] * half_weight)
                        else:
                            blocks.append(jnp.zeros((channels, channels), jnp.bfloat16))
                    col = (d * 4 + 2 * pair) * channels
                    wide_ref[row : row + channels, col : col + two] = jnp.concatenate(
                        blocks, axis=1
                    )

    last_sum[...] = jnp.zeros_like(last_sum)
    copies[2].wait()
    for d in range(3):
        for u in range(3):
            for t in range(3):
                block = last_raw[d, u, t].astype(jnp.float32)
                for o in range(2):
                    for r in range(4):
                        row = (d * 3 + t) * 8 + o * 4 + r
                        col = (r + u) * channels
                        last_sum[row : row + 1, col : col + channels] = block[o : o + 1]
    last_ref[...] = last_sum[...].astype(jnp.bfloat16)

    def first_layer(z):
        source = jnp.concatenate(
            [
                jnp.concatenate([taps_ref[g, t, 16 * z : 16 * z + 48, :] for t in range(3)], axis=0)
                for g in range(2)
            ],
            axis=1,
        )
        half = jnp.dot(first_ref[...], source, preferred_element_type=jnp.float32)
        for r in range(8):
            begin = (r % 4) * channels
            first = columns * (r // 4)
            value = half_silu(half[begin : begin + channels, first : first + columns])
            factors = []
            if z < 2:
                factors.append(low_slice)
            if z >= slices1 - 2:
                factors.append(high_slice)
            if r < 2:
                factors.append(low_row)
            if r >= 6:
                factors.append(high_row)
            for factor in factors:
                value = value * factor
            f1_ref[z, r * channels : (r + 1) * channels, :] = value.astype(jnp.bfloat16)

    def second_product(z, pair, part_ref):
        source = jnp.concatenate(
            [
                f1_ref[z + a : z + a + 3, two * pair : two * pair + four, :].reshape(
                    3 * four, columns
                )
                for a in range(2)
            ],
            axis=1,
        )
        part_ref[...] = jnp.dot(wide_ref[...], source, preferred_element_type=jnp.float32)

    def second_layer(z, pair, part_ref):
        for a in range(2):
            first = columns * a
            for r in range(2):
                row = r * channels
                half = (
                    moved_right(part_ref[row : row + channels, first : first + columns])
                    + part_ref[two + row : two + row + channels, first : first + columns]
                    + moved_left(
                        part_ref[four + row : four + row + channels, first : first + columns]
                    )
                )
                value = half_silu(half)
                factors = []
                if z + a == 0:
                    factors.append(low_slice)
                if z + a == slices2 - 1:
                    factors.append(high_slice)
                if pair == 0 and r == 0:
                    factors.append(low_row)
                if pair == 2 and r == 1:
                    factors.append(high_row)
                for factor in factors:
                    value = value * factor
                place = two * pair + r * channels
                f2_ref[z + a, place : place + channels, :] = value.astype(jnp.bfloat16)

    def third_product(z):
        source = jnp.concatenate([f2_ref[z], f2_ref[z + 1]], axis=1)
        score_ref[z // 2] = jnp.dot(last_ref[...], source, preferred_element_type=jnp.float32)

    for z in range(4):
        first_layer(z)
    waiting = None
    parts = (part_a, part_b)
    count = 0
    for z in range(0, slices2, 2):
        for pair in range(3):
            second_product(z, pair, parts[count % 2])
            if pair < 2 and z + 4 + pair < slices1:
                first_layer(z + 4 + pair)
            if waiting is not None:
                second_layer(*waiting)
                if waiting[1] == 2:
                    third_product(waiting[0])
            waiting = (z, pair, parts[count % 2])
            count += 1
    second_layer(*waiting)
    third_product(waiting[0])

    for copy in copies[3:]:
        copy.wait()
    size = size_ref[0]
    noise_scale = jnp.sqrt(jnp.full((1, columns), 2.0 * size, jnp.float32))
    for z in range(out_slices):
        taps = []
        for t in range(3):
            total = None
            for d in range(3):
                row, first = (3 * d + t) * 8, columns * ((z + d) % 2)
                piece = score_ref[(z + d) // 2, row : row + 8, first : first + columns]
                total = piece if total is None else total + piece
            taps.append(total)
        score = size * (moved_right(taps[0]) + taps[1] + moved_left(taps[2]))
        for part in range(2):
            out_ref[z, part] = (
                image_ref[z, part]
                + score[part * rows : (part + 1) * rows]
                + noise_scale * noise_ref[z, part]
            )


def stepped_without_data(
    windows, current_image, langevin_noise, step_size, weight_in, weight_mid, weight_out
):
    channels = weight_mid.shape[0]
    slices0, columns = windows.shape[1] // 16, windows.shape[-1]
    out_slices = slices0 - 6
    local = (out_slices,) + current_image.shape[2:]
    first = jnp.transpose(weight_in, (2, 3, 4, 1, 0))
    mid = jnp.transpose(weight_mid, (2, 3, 4, 0, 1))
    last = jnp.transpose(weight_out, (2, 3, 4, 0, 1))
    hbm = pl.BlockSpec(memory_space=pltpu.HBM)
    vmem = pl.BlockSpec(memory_space=pltpu.VMEM)
    return pl.pallas_call(
        network_kernel,
        out_shape=jax.ShapeDtypeStruct(local, jnp.float32),
        in_specs=[vmem] + [hbm] * 6,
        out_specs=vmem,
        scratch_shapes=[
            pltpu.SMEM(step_size.shape, jnp.float32),
            pltpu.VMEM(first.shape, jnp.bfloat16),
            pltpu.VMEM(mid.shape, jnp.bfloat16),
            pltpu.VMEM(last.shape, jnp.bfloat16),
            pltpu.VMEM(local, jnp.float32),
            pltpu.VMEM(local, jnp.float32),
            pltpu.VMEM((256, 4 * channels), jnp.float32),
            pltpu.VMEM((72, 6 * channels), jnp.float32),
            pltpu.VMEM((4 * channels, 144), jnp.bfloat16),
            pltpu.VMEM((6 * channels, 12 * channels), jnp.bfloat16),
            pltpu.VMEM((72, 6 * channels), jnp.bfloat16),
            pltpu.VMEM((2, 3, slices0 * 16, columns), jnp.bfloat16),
            pltpu.VMEM((out_slices + 4, 8 * channels, columns), jnp.bfloat16),
            pltpu.VMEM((out_slices + 2, 6 * channels, columns), jnp.bfloat16),
            pltpu.VMEM((6 * channels, 2 * columns), jnp.float32),
            pltpu.VMEM((6 * channels, 2 * columns), jnp.float32),
            pltpu.VMEM((out_slices // 2 + 1, 72, 2 * columns), jnp.float32),
            pltpu.SemaphoreType.DMA((6,)),
        ],
        compiler_params=pltpu.CompilerParams(vmem_limit_bytes=48 * 2**20),
        cost_estimate=pl.CostEstimate(
            flops=10**10, bytes_accessed=2 * 10**6, transcendentals=4 * 10**6
        ),
    )(
        windows, step_size, first, mid, last,
        current_image.reshape(local), langevin_noise.reshape(local),
    ).reshape(current_image.shape)


def per_device(
    current_image, langevin_noise, step_size, coil_maps, measured_kspace, sample_mask,
    caipi_steps, band_order, weight_in, weight_mid, weight_out,
):
    positions, group_slices, _, row_count, columns = current_image.shape
    local_slices = positions * group_slices
    own = current_image.astype(jnp.bfloat16).reshape(
        positions, group_slices, 2 * row_count, columns
    )
    everyone = lax.all_gather(own, "band", axis=0, tiled=True)

    volume = everyone.reshape(-1, 2, row_count, columns)
    volume = jnp.pad(volume, ((3, 3), (0, 0), (0, 0), (0, 0)))
    tall = lax.dynamic_slice_in_dim(
        volume, lax.axis_index("band") * local_slices, local_slices + 6, axis=0
    )
    below = from_behind(tall[:, :, row_count - 3 :, :], "slab", 1)
    above = from_behind(tall[:, :, :3, :], "slab", -1)
    field = jnp.concatenate([below, tall, above, jnp.zeros_like(above[:, :, :2])], axis=2)
    windows = jnp.stack(
        [field[:, :, 4 * g : 4 * g + 8].reshape(-1, columns) for g in range(2)], axis=0
    )
    partial_sums = partial_consistency(
        everyone, step_size, coil_maps, measured_kspace, sample_mask, caipi_steps, band_order
    )
    swapped = lax.all_to_all(partial_sums, "band", split_axis=0, concat_axis=0, tiled=True)
    base = stepped_without_data(
        windows, current_image, langevin_noise, step_size, weight_in, weight_mid, weight_out
    )
    pieces = swapped.reshape((-1, positions) + swapped.shape[1:]).astype(jnp.float32)
    return base - jnp.sum(pieces, axis=0)


def solution(mesh):
    band5 = P("band", None, None, "slab", None)
    in_specs = (
        band5,
        band5,
        P(),
        P(None, None, "band", None, "slab", None),
        P(None, "band", None, "slab", None),
        P(), P(), P(), P(), P(), P(),
    )
    return jax.shard_map(
        per_device, mesh=mesh, in_specs=in_specs, out_specs=band5, check_vma=False
    )
```

time: 54.6 us -> 49.7 us (0.910)
  Pallas kernels: 26.5 us -> 19.2 us
  waiting for transfers between devices: 0.01 us -> 4.89 us
  starting transfers between devices: 9.34 us -> 8.63 us
  other arithmetic: 2.57 us -> 1.95 us
  local copies, waits for them, and re-layouts: 7.47 us -> 6.88 us
    pallas_call x2, Pallas kernels: 26.5 us -> 19.2 us  [the longest x1 10.7 us: stepped_without_data(): pl.pallas_call(network_kernel, out_shape=jax.ShapeDtypeStruct(local, jnp....]
    ppermute x2, waiting for transfers between devices: 0.01 us -> 4.88 us  [from_behind(): return lax.ppermute(block, axis, route)]
    ppermute x2, starting transfers between devices: 5.84 us -> 5.12 us  [from_behind(): return lax.ppermute(block, axis, route)]
    add x1 -> x0, other arithmetic: 0.67 us -> none  [per_device(): current_image + step_value * (score_field - consistency)]
    sub x0 -> x1, other arithmetic: none -> 0.67 us  [per_device(): return base - jnp.sum(pieces, axis=0)]
  transfers between devices with their start and end apart: 3 -> 3, of which waited for: 0 -> 2; matrix products, arithmetic and copies ran while one was open for 3% -> 1% of each run, Pallas kernels for 49% -> 22%
where the time goes in v1:
time: 49.7 us; the launch traced here: 49.2 us
  Pallas kernels  19.2 us (39%)
  starting transfers between devices  8.63 us (17%)
  local copies, waits for them, and re-layouts  6.88 us (14%)
  blocking collectives  6.84 us (14%)
  waiting for transfers between devices  4.89 us (10%)
  other arithmetic  1.95 us (4%)
  between operations  0.85 us (2%)
    pallas_call x1, Pallas kernels, stepped_without_data(): pl.pallas_call(network_kernel, out_shape=jax.ShapeDtypeStruct(local, jnp....  10.7 us
    pallas_call x1, Pallas kernels, partial_consistency(): pl.pallas_call(consistency_kernel, out_shape=jax.ShapeDtypeStruct((all_po...  8.42 us
    all_gather x1, blocking collectives, per_device(): everyone = lax.all_gather(own, 'band', axis=0, tiled=True)  6.84 us
    unnamed x24, local copies, waits for them, and re-layouts  6.56 us
    ppermute x2, starting transfers between devices, from_behind(): return lax.ppermute(block, axis, route)  5.12 us
    ppermute x2, waiting for transfers between devices, from_behind(): return lax.ppermute(block, axis, route)  4.88 us
    all_to_all x1, starting transfers between devices, per_device(): lax.all_to_all(partial_sums, 'band', split_axis=0, concat_axis=0, tiled=T...  3.51 us
  transfers between devices with their start and end apart: 3, of which 2 were waited for; matrix products, arithmetic and copies ran while one was open for 1% of the time, Pallas kernels for 22%

profile of v1, /device:TPU:0, one launch (start us, length us, event | category | flops | bytes accessed | tf_op | source)
XLA Modules:
  0.0 49.2 jit_solution(5774899671380237595)
XLA Ops:
  0.7 0.9 %convert_element_type.11 = bf16[2,4,2,4,384]{4,3,2,1,0:T(4,128)(2,1)S(1)} convert(f32[2,4,2,4,384]{4,3,2,1,0:T(4,128)} %param.13) | non-fusion elementwise | flops 24576 | bytes 147456 | tf_op jit(solution)/shard_map/convert_element_type | solution.py:472
  1.6 6.8 %all_gather.3.image_ref = bf16[8,4,8,384]{3,2,1,0:T(8,128)(2,1)S(1)} all-gather(bf16[2,4,8,384]{3,2,1,0:T(8,128)(2,1)S(1)} %reshape.18), channel_id=1, replica_groups=mesh['band'=4,'slab'=8] {'band'}, dimensions={0}, use_global_device_ids=true | all-gather | bytes 245760 | tf_op jit(solution)/shard_map/all_gather | solution.py:475
  8.4 0.0 copy-start.1
  8.4 1.4 %copy-done.1 = bf16[8,4,8,2,4,384]{5,4,3,2,1,0:T(4,128)(2,1)S(1)} copy-done((bf16[8,4,8,2,4,384]{5,4,3,2,1,0:T(4,128)(2,1)S(1)}, bf16[8,4,8,2,4,384]{5,4,3,2,1,0:T(4,128)(2,1)}, u32[]{:S(2)}) %copy-start.1) | copy-done | bytes 1572888
  9.8 0.0 copy-start.3
  9.8 1.0 %copy-done.3 = f32[4,8,2,4,384]{4,3,2,1,0:T(4,128)S(1)} copy-done((f32[4,8,2,4,384]{4,3,2,1,0:T(4,128)S(1)}, f32[4,8,2,4,384]{4,3,2,1,0:T(4,128)}, u32[]{:S(2)}) %copy-start.3) | copy-done | bytes 393240
  10.8 0.0 copy-start.7
  10.8 0.7 %copy-done.7 = s32[4,384]{1,0:T(4,128)S(1)} copy-done((s32[4,384]{1,0:T(4,128)S(1)}, s32[4,384]{1,0:T(4,128)}, u32[]{:S(2)}) %copy-start.7) | copy-done | bytes 6168
  11.5 0.0 copy-start.8
  11.5 0.7 %copy-done.8 = s32[8]{0:T(128)S(1)} copy-done((s32[8]{0:T(128)S(1)}, s32[8]{0:T(128)}, u32[]{:S(2)}) %copy-start.8) | copy-done | bytes 56
  12.2 0.0 copy-start.9
  12.2 0.7 %copy-done.9 = s32[8]{0:T(128)S(1)} copy-done((s32[8]{0:T(128)S(1)}, s32[8]{0:T(128)}, u32[]{:S(2)}) %copy-start.9) | copy-done | bytes 56
  12.8 0.0 copy-start.10
  12.8 1.1 %copy-done.10 = bf16[384,768]{1,0:T(8,128)(2,1)S(1)} copy-done((bf16[384,768]{1,0:T(8,128)(2,1)S(1)}, bf16[384,768]{1,0:T(8,128)(2,1)}, u32[]{:S(2)}) %copy-start.10) | copy-done | bytes 589848
  13.9 0.0 copy-start.11
  13.9 1.1 %copy-done.11 = bf16[384,768]{1,0:T(8,128)(2,1)S(1)} copy-done((bf16[384,768]{1,0:T(8,128)(2,1)S(1)}, bf16[384,768]{1,0:T(8,128)(2,1)}, u32[]{:S(2)}) %copy-start.11) | copy-done | bytes 589848
  15.0 8.4 %shard_map.128 = bf16[8,4,2,4,384]{4,3,2,1,0:T(4,128)(2,1)} custom-call(bf16[8,4,8,384]{3,2,1,0:T(8,128)(2,1)S(1)} %all_gather.3.image_ref, s32[8]{0:T(128)S(1)} %copy-done.8, s32[8]{0:T(128)S(1)} %copy-done.9, f32[1]{0:T(128)S(6)} %copy.14.size_hbm, bf16[8,4,8,2,4,384]{5,4,3,2,1,0:T(4,128)(2,1)S(1)} %copy-done.1, f32[4,8,2,4,384]{4,3,2,1,0:T(4,128)S(1)} %copy-done.3, ...), custom_call_target="tpu_custom_call" | custom-call | flops 1000000000 | bytes 4000000 | tf_op jit(solution)/shard_map/pallas_call | solution.py:201
  23.4 0.0 copy-start
  23.4 0.0 copy-start.2
  23.4 0.0 copy-start.4
  23.4 0.0 copy-start.5
  23.4 0.0 copy-start.6
  23.5 3.5 %all-to-all-start = ((bf16[8,4,2,4,384]{4,3,2,1,0:T(4,128)(2,1)}), bf16[8,4,2,4,384]{4,3,2,1,0:T(4,128)(2,1)S(1)}, u32[]{:S(2)}, u32[]{:S(2)}) async-start(bf16[8,4,2,4,384]{4,3,2,1,0:T(4,128)(2,1)} %shard_map.128), calls=%async_computation | async-start | bytes 393216 | tf_op jit(solution)/shard_map/all_to_all | solution.py:491
  27.0 0.1 reshape.19
  27.0 0.1 pad_dynamic-slice_fusion.1
  27.2 3.6 %collective-permute-start = (bf16[14,2,3,384]{3,2,1,0:T(4,128)(2,1)S(1)}, bf16[14,2,3,384]{3,2,1,0:T(4,128)(2,1)S(1)}, u32[]{:S(2)}, u32[]{:S(2)}) collective-permute-start(bf16[14,2,3,384]{3,2,1,0:T(4,128)(2,1)S(1)} %get-tuple-element.5), channel_id=1, source_target_pairs={{0,1},{1,2},{2,3},{3,4},{4,5},{5,6},{6,7},{8,9},{9,10},{10,11},{11... | collective-permute-start | bytes 193544 | tf_op jit(solution)/shard_map/ppermute | solution.py:16
  30.8 1.5 %collective-permute-start.1 = (bf16[14,2,3,384]{3,2,1,0:T(4,128)(2,1)S(1)}, bf16[14,2,3,384]{3,2,1,0:T(4,128)(2,1)S(1)}, u32[]{:S(2)}, u32[]{:S(2)}) collective-permute-start(bf16[14,2,3,384]{3,2,1,0:T(4,128)(2,1)S(1)} %get-tuple-element.6), channel_id=1, source_target_pairs={{1,0},{2,1},{3,2},{4,3},{5,4},{6,5},{7,6},{9,8},{10,9},{11,10},{12... | collective-permute-start | bytes 193544 | tf_op jit(solution)/shard_map/ppermute | solution.py:16
  32.3 0.1 pad_dynamic-slice_fusion.2
  32.4 0.1 pad_slice_fusion
  32.4 0.8 %collective-permute-done = bf16[14,2,3,384]{3,2,1,0:T(4,128)(2,1)S(1)} collective-permute-done((bf16[14,2,3,384]{3,2,1,0:T(4,128)(2,1)S(1)}, bf16[14,2,3,384]{3,2,1,0:T(4,128)(2,1)S(1)}, u32[]{:S(2)}, u32[]{:S(2)}) %collective-permute-start) | collective-permute-done | bytes 64544 | tf_op jit(solution)/shard_map/ppermute | solution.py:16
  33.2 4.1 %collective-permute-done.1 = bf16[14,2,3,384]{3,2,1,0:T(4,128)(2,1)S(1)} collective-permute-done((bf16[14,2,3,384]{3,2,1,0:T(4,128)(2,1)S(1)}, bf16[14,2,3,384]{3,2,1,0:T(4,128)(2,1)S(1)}, u32[]{:S(2)}, u32[]{:S(2)}) %collective-permute-start.1) | collective-permute-done | bytes 64544 | tf_op jit(solution)/shard_map/ppermute | solution.py:16
  37.3 0.2 pad_maximum_fusion.2
  37.6 0.0 copy-done
  37.6 0.0 copy-done.2
  37.6 0.0 copy-done.4
  37.6 0.0 copy-done.5
  37.6 0.0 copy-done.6
  37.7 10.7 %shard_map.127 = f32[8,2,4,384]{3,2,1,0:T(4,128)S(1)} custom-call(bf16[2,224,384]{2,1,0:T(8,128)(2,1)S(1)} %pad_maximum_fusion.window_ref, f32[1]{0:T(128)S(6)} %copy.14.size_hbm, bf16[3,3,3,2,64]{4,3,2,1,0:T(2,128)(2,1)S(1)} %bitcast.16, bf16[3,3,3,64,64]{4,3,2,1,0:T(8,128)(2,1)S(1)} %bitcast.14, bf16[3,3,3,2,64]{4,3,2,1,0:T(2,128)(2,1)S(1)} %bitcast.17, ...), custom_call_target="tpu_custom_call" | custom-call | flops 10000000000 | bytes 2000000 | tf_op jit(solution)/shard_map/pallas_call | solution.py:431
  48.4 0.0 all-to-all-done
  48.4 0.1 convert_reduce_fusion
  48.5 0.7 %sub.3 = f32[2,4,2,4,384]{4,3,2,1,0:T(4,128)} subtract(f32[2,4,2,4,384]{4,3,2,1,0:T(4,128)S(1)} %bitcast.13, f32[2,4,2,4,384]{4,3,2,1,0:T(4,128)S(1)} %convert_reduce_fusion) | non-fusion elementwise | flops 24576 | bytes 294912 | tf_op jit(solution)/shard_map/sub | solution.py:496
  (3 shorter events, 0.1 us)
Async XLA Ops:
  8.4 1.4 %copy-start.1 = (bf16[8,4,8,2,4,384]{5,4,3,2,1,0:T(4,128)(2,1)S(1)}, bf16[8,4,8,2,4,384]{5,4,3,2,1,0:T(4,128)(2,1)}, u32[]{:S(2)}) copy-start(bf16[8,4,8,2,4,384]{5,4,3,2,1,0:T(4,128)(2,1)} %coil_hbm.1) | copy-start | bytes 4718596
  9.8 1.0 %copy-start.3 = (f32[4,8,2,4,384]{4,3,2,1,0:T(4,128)S(1)}, f32[4,8,2,4,384]{4,3,2,1,0:T(4,128)}, u32[]{:S(2)}) copy-start(f32[4,8,2,4,384]{4,3,2,1,0:T(4,128)} %kspace_hbm.1) | copy-start | bytes 1179652
  10.8 0.7 %copy-start.7 = (s32[4,384]{1,0:T(4,128)S(1)}, s32[4,384]{1,0:T(4,128)}, u32[]{:S(2)}) copy-start(s32[4,384]{1,0:T(4,128)} %mask_hbm.1) | copy-start | bytes 18436
  11.5 0.7 %copy-start.8 = (s32[8]{0:T(128)S(1)}, s32[8]{0:T(128)}, u32[]{:S(2)}) copy-start(s32[8]{0:T(128)} %steps_hbm.1) | copy-start | bytes 100
  12.2 0.7 %copy-start.9 = (s32[8]{0:T(128)S(1)}, s32[8]{0:T(128)}, u32[]{:S(2)}) copy-start(s32[8]{0:T(128)} %order_hbm.1) | copy-start | bytes 100
  12.8 1.1 %copy-start.10 = (bf16[384,768]{1,0:T(8,128)(2,1)S(1)}, bf16[384,768]{1,0:T(8,128)(2,1)}, u32[]{:S(2)}) copy-start(bf16[384,768]{1,0:T(8,128)(2,1)} %constant.21.clone.low_hbm) | copy-start | bytes 1769476
  13.9 1.1 %copy-start.11 = (bf16[384,768]{1,0:T(8,128)(2,1)S(1)}, bf16[384,768]{1,0:T(8,128)(2,1)}, u32[]{:S(2)}) copy-start(bf16[384,768]{1,0:T(8,128)(2,1)} %constant.20.clone.high_hbm) | copy-start | bytes 1769476
  23.4 14.2 %copy-start = (f32[2,4,2,4,384]{4,3,2,1,0:T(4,128)S(1)}, f32[2,4,2,4,384]{4,3,2,1,0:T(4,128)}, u32[]{:S(2)}) copy-start(f32[2,4,2,4,384]{4,3,2,1,0:T(4,128)} %param.13) | copy-start | bytes 294916
  23.4 14.2 %copy-start.2 = (bf16[64,64,3,3,3]{1,0,4,3,2:T(8,128)(2,1)S(1)}, bf16[64,64,3,3,3]{1,0,4,3,2:T(8,128)(2,1)}, u32[]{:S(2)}) copy-start(bf16[64,64,3,3,3]{1,0,4,3,2:T(8,128)(2,1)} %param.22) | copy-start | bytes 663556
  23.4 14.2 %copy-start.4 = (f32[2,4,2,4,384]{4,3,2,1,0:T(4,128)S(1)}, f32[2,4,2,4,384]{4,3,2,1,0:T(4,128)}, u32[]{:S(2)}) copy-start(f32[2,4,2,4,384]{4,3,2,1,0:T(4,128)} %param.14) | copy-start | bytes 294916
  23.4 14.2 %copy-start.5 = (bf16[64,2,3,3,3]{0,1,4,3,2:T(2,128)(2,1)S(1)}, bf16[64,2,3,3,3]{0,1,4,3,2:T(2,128)(2,1)}, u32[]{:S(2)}) copy-start(bf16[64,2,3,3,3]{0,1,4,3,2:T(2,128)(2,1)} %param.21) | copy-start | bytes 20740
  23.4 14.2 %copy-start.6 = (bf16[2,64,3,3,3]{1,0,4,3,2:T(2,128)(2,1)S(1)}, bf16[2,64,3,3,3]{1,0,4,3,2:T(2,128)(2,1)}, u32[]{:S(2)}) copy-start(bf16[2,64,3,3,3]{1,0,4,3,2:T(2,128)(2,1)} %param.23) | copy-start | bytes 20740
  23.5 25.0 %all-to-all-start = ((bf16[8,4,2,4,384]{4,3,2,1,0:T(4,128)(2,1)}), bf16[8,4,2,4,384]{4,3,2,1,0:T(4,128)(2,1)S(1)}, u32[]{:S(2)}, u32[]{:S(2)}) async-start(bf16[8,4,2,4,384]{4,3,2,1,0:T(4,128)(2,1)} %shard_map.128), calls=%async_computation | async-start | bytes 393216 | tf_op jit(solution)/shard_map/all_to_all | solution.py:491
  27.2 6.0 %collective-permute-start = (bf16[14,2,3,384]{3,2,1,0:T(4,128)(2,1)S(1)}, bf16[14,2,3,384]{3,2,1,0:T(4,128)(2,1)S(1)}, u32[]{:S(2)}, u32[]{:S(2)}) collective-permute-start(bf16[14,2,3,384]{3,2,1,0:T(4,128)(2,1)S(1)} %get-tuple-element.5), channel_id=1, source_target_pairs={{0,1},{1,2},{2,3},{3,4},{4,5},{5,6},{6,7},{8,9},{9,10},{10,11},{11... | collective-permute-start | bytes 193544 | tf_op jit(solution)/shard_map/ppermute | solution.py:16
  30.8 6.5 %collective-permute-start.1 = (bf16[14,2,3,384]{3,2,1,0:T(4,128)(2,1)S(1)}, bf16[14,2,3,384]{3,2,1,0:T(4,128)(2,1)S(1)}, u32[]{:S(2)}, u32[]{:S(2)}) collective-permute-start(bf16[14,2,3,384]{3,2,1,0:T(4,128)(2,1)S(1)} %get-tuple-element.6), channel_id=1, source_target_pairs={{1,0},{2,1},{3,2},{4,3},{5,4},{6,5},{7,6},{9,8},{10,9},{11,10},{12... | collective-permute-start | bytes 193544 | tf_op jit(solution)/shard_map/ppermute | solution.py:16

commit v2 on v1

--- a/solution.py
+++ b/solution.py
@@ -10,23 +10,53 @@
 from jax.sharding import PartitionSpec as P
 
 
-def from_behind(block, axis, distance):
-    devices = range(lax.axis_size(axis))
-    route = [(i - distance, i) for i in devices if i - distance in devices]
-    return lax.ppermute(block, axis, route)
-
-
-def split_table(table):
-    high = table.astype(jnp.bfloat16)
-    low = (table - high.astype(np.float64)).astype(jnp.bfloat16)
-    return high, low
-
-
-def dft_table(columns):
+def exchanged_rows(tall, width):
+    count = lax.axis_size("slab")
+    odd = lax.axis_index("slab") % 2 == 1
+    head, tail = tall[:, :, :width, :], tall[:, :, tall.shape[2] - width :, :]
+    arrived = []
+    for first in range(2):
+        route = []
+        for i in range(first, count - 1, 2):
+            route += [(i, i + 1), (i + 1, i)]
+        sent = jnp.where(odd, head, tail) if first == 0 else jnp.where(odd, tail, head)
+        arrived.append(lax.ppermute(sent, "slab", route))
+    below = jnp.where(odd, arrived[0], arrived[1])
+    above = jnp.where(odd, arrived[1], arrived[0])
+    return below, above
+
+
+def in_hbm(*arrays):
+    return [pltpu.with_memory_space_constraint(array, pltpu.HBM) for array in arrays]
+
+
+def dft_factors(columns):
+    near = 16
     index = np.arange(columns)
-    phase = (np.outer(index, index) % columns) * (2.0 * math.pi / columns)
-    factor = 1.0 / math.sqrt(columns)
-    return np.concatenate([np.cos(phase), np.sin(phase)], axis=1) * factor
+    pieces = []
+    for rows in (near * np.arange(columns // near), np.arange(near)):
+        phase = (np.outer(rows, index) % columns) * (2.0 * math.pi / columns)
+        pieces += [np.cos(phase), np.sin(phase)]
+    far = np.concatenate(pieces[:2], axis=0) / math.sqrt(columns)
+    return np.concatenate([far] + pieces[2:], axis=0).astype(np.float32)
+
+
+def build_tables(factors_ref, high_ref, low_ref):
+    columns = factors_ref.shape[1]
+    near = 16
+    count = columns // near
+    near_cos = factors_ref[2 * count : 2 * count + near, :]
+    near_sin = factors_ref[2 * count + near :, :]
+    for a in range(count):
+        far_cos = factors_ref[a : a + 1, :]
+        far_sin = factors_ref[count + a : count + a + 1, :]
+        tables = (far_cos * near_cos - far_sin * near_sin, far_sin * near_cos + far_cos * near_sin)
+        rows = slice(near * a, near * (a + 1))
+        for part, table in enumerate(tables):
+            high = table.astype(jnp.bfloat16)
+            lanes = slice(columns * part, columns * (part + 1))
+            high_ref[rows, lanes] = high
+            low_ref[rows, lanes] = (table - high.astype(jnp.float32)).astype(jnp.bfloat16)
 
 
 def moved_right(value):
@@ -85,32 +115,32 @@
 
 
 def consistency_kernel(
-    image_ref, steps_hbm, order_hbm, size_hbm, coil_hbm, kspace_hbm, mask_hbm, high_hbm, low_hbm,
+    image_ref, steps_hbm, order_hbm, size_ref, coil_hbm, kspace_hbm, mask_hbm, factors_hbm,
     out_ref,
-    steps_ref, order_ref, size_ref, coil_ref, kspace_ref, mask_ref, high_ref, low_ref,
+    steps_ref, order_ref, coil_ref, kspace_ref, mask_ref, factors_ref, high_ref, low_ref,
     turned_ref, real_ref, imag_ref, field_ref, swap_ref, sum_ref, sems, coil_sems,
 ):
     all_positions, slices, coils, _, rows, columns = coil_ref.shape
     tiles = columns // 128
     unit = columns // 8
     pairs = (
-        (steps_hbm, steps_ref), (order_hbm, order_ref), (size_hbm, size_ref),
-        (kspace_hbm, kspace_ref), (mask_hbm, mask_ref), (high_hbm, high_ref), (low_hbm, low_ref),
+        (steps_hbm, steps_ref), (order_hbm, order_ref),
+        (kspace_hbm, kspace_ref), (mask_hbm, mask_ref), (factors_hbm, factors_ref),
     )
     copies = [pltpu.make_async_copy(src, dst, sems.at[i]) for i, (src, dst) in enumerate(pairs)]
-    for copy in copies[:3]:
+    for copy in copies[:2]:
         copy.start()
     for g in range(all_positions):
         pltpu.make_async_copy(coil_hbm.at[g], coil_ref.at[g], coil_sems.at[g]).start()
-    for copy in copies[3:]:
+    for copy in copies[2:]:
         copy.start()
-    for copy in copies[:3]:
+    for copy in copies[:2]:
         copy.wait()
 
     def shift_of(g):
         return steps_ref[order_ref[g]] * unit
 
-    def turn_coils(g, carry):
+    def turn_coils(g):
         shift = shift_of(g)
         image = image_ref[g].astype(jnp.float32)
 
@@ -129,9 +159,9 @@
                 turned_ref[j, g, s] = value
 
             turned_tiles(coil, shift, store_coil)
-        return carry
-
-    lax.fori_loop(0, all_positions, turn_coils, 0)
+
+    for g in range(all_positions):
+        turn_coils(g)
 
     block = coils * 2 * rows
     for j in range(tiles):
@@ -147,8 +177,9 @@
                 block, 128
             )
 
-    for copy in copies[3:]:
+    for copy in copies[2:]:
         copy.wait()
+    build_tables(factors_ref, high_ref, low_ref)
     product = table_product(field_ref[...], high_ref, low_ref)
     grouped = (slices, coils, 2 * rows, columns)
     with_cos = product[:, :columns].reshape(grouped)
@@ -179,14 +210,11 @@
                     upper_half(straight), straight, crossed
                 )
 
-    def turn_sums(g, carry):
+    for g in range(all_positions):
         back_shift = lax.rem(columns - shift_of(g), columns)
         turned = pltpu.roll(sum_ref[g], back_shift, 2).astype(jnp.bfloat16)
         out_ref[g, :, 0] = turned[:, :rows]
         out_ref[g, :, 1] = turned[:, rows:]
-        return carry
-
-    lax.fori_loop(0, all_positions, turn_sums, 0)
 
 
 def partial_consistency(
@@ -194,45 +222,51 @@
 ):
     all_positions, slices, coils, _, rows, columns = coil_maps.shape
     total = slices * coils * 2 * rows
-    high, low = split_table(dft_table(columns))
+    factors = jnp.asarray(dft_factors(columns))
+    table = (columns, 2 * columns)
     hbm = pl.BlockSpec(memory_space=pltpu.HBM)
     vmem = pl.BlockSpec(memory_space=pltpu.VMEM)
     tile_shape = (columns // 128, all_positions, slices)
     return pl.pallas_call(
         consistency_kernel,
         out_shape=jax.ShapeDtypeStruct((all_positions, slices, 2, rows, columns), jnp.bfloat16),
-        in_specs=[vmem] + [hbm] * 8,
+        in_specs=[vmem, hbm, hbm, pl.BlockSpec(memory_space=pltpu.SMEM)] + [hbm] * 4,
         out_specs=vmem,
         scratch_shapes=[
             pltpu.SMEM(caipi_steps.shape, jnp.int32),
             pltpu.SMEM(band_order.shape, jnp.int32),
-            pltpu.SMEM(step_size.shape, jnp.float32),
             pltpu.VMEM(coil_maps.shape, jnp.bfloat16),
             pltpu.VMEM(measured_kspace.shape, jnp.float32),
             pltpu.VMEM(sample_mask.shape, jnp.int32),
-            pltpu.VMEM(high.shape, jnp.bfloat16),
-            pltpu.VMEM(low.shape, jnp.bfloat16),
+            pltpu.VMEM(factors.shape, jnp.float32),
+            pltpu.VMEM(table, jnp.bfloat16),
+            pltpu.VMEM(table, jnp.bfloat16),
             pltpu.VMEM(tile_shape + (coils, 2 * rows, 128), jnp.float32),
             pltpu.VMEM(tile_shape + (2 * rows, 128), jnp.float32),
             pltpu.VMEM(tile_shape + (2 * rows, 128), jnp.float32),
             pltpu.VMEM((total, columns), jnp.float32),
             pltpu.VMEM((total, columns), jnp.float32),
             pltpu.VMEM((all_positions, slices, 2 * rows, columns), jnp.float32),
-            pltpu.SemaphoreType.DMA((7,)),
+            pltpu.SemaphoreType.DMA((5,)),
             pltpu.SemaphoreType.DMA((all_positions,)),
         ],
         compiler_params=pltpu.CompilerParams(vmem_limit_bytes=48 * 2**20),
-        cost_estimate=pl.CostEstimate(flops=10**9, bytes_accessed=4 * 10**6, transcendentals=0),
+        cost_estimate=pl.CostEstimate(
+            flops=8 * 10**9, bytes_accessed=4 * 10**6, transcendentals=0
+        ),
     )(
-        everyone, caipi_steps, band_order, step_size, coil_maps, measured_kspace, sample_mask,
-        jnp.asarray(high), jnp.asarray(low),
+        everyone,
+        *in_hbm(caipi_steps, band_order),
+        step_size,
+        *in_hbm(coil_maps, measured_kspace, sample_mask),
+        factors,
     )
 
 
 def network_kernel(
-    window_ref, size_hbm, first_hbm, mid_hbm, last_hbm, image_hbm, noise_hbm,
+    window_ref, size_ref, first_hbm, mid_hbm, last_hbm, image_hbm, noise_hbm,
     out_ref,
-    size_ref, first_raw, mid_raw, last_raw, image_ref, noise_ref,
+    first_raw, mid_raw, last_raw, image_ref, noise_ref,
     first_sum, last_sum, first_ref, wide_ref, last_ref,
     taps_ref, f1_ref, f2_ref, part_a, part_b, score_ref, sems,
 ):
@@ -241,7 +275,7 @@
     slices1, slices2 = out_slices + 4, out_slices + 2
     pairs = (
         (first_hbm, first_raw), (mid_hbm, mid_raw), (last_hbm, last_raw),
-        (size_hbm, size_ref), (image_hbm, image_ref), (noise_hbm, noise_ref),
+        (image_hbm, image_ref), (noise_hbm, noise_ref),
     )
     copies = [pltpu.make_async_copy(src, dst, sems.at[i]) for i, (src, dst) in enumerate(pairs)]
     for copy in copies:
@@ -431,10 +465,9 @@
     return pl.pallas_call(
         network_kernel,
         out_shape=jax.ShapeDtypeStruct(local, jnp.float32),
-        in_specs=[vmem] + [hbm] * 6,
+        in_specs=[vmem, pl.BlockSpec(memory_space=pltpu.SMEM)] + [hbm] * 5,
         out_specs=vmem,
         scratch_shapes=[
-            pltpu.SMEM(step_size.shape, jnp.float32),
             pltpu.VMEM(first.shape, jnp.bfloat16),
             pltpu.VMEM(mid.shape, jnp.bfloat16),
             pltpu.VMEM(last.shape, jnp.bfloat16),
@@ -451,15 +484,17 @@
             pltpu.VMEM((6 * channels, 2 * columns), jnp.float32),
             pltpu.VMEM((6 * channels, 2 * columns), jnp.float32),
             pltpu.VMEM((out_slices // 2 + 1, 72, 2 * columns), jnp.float32),
-            pltpu.SemaphoreType.DMA((6,)),
+            pltpu.SemaphoreType.DMA((5,)),
         ],
         compiler_params=pltpu.CompilerParams(vmem_limit_bytes=48 * 2**20),
         cost_estimate=pl.CostEstimate(
             flops=10**10, bytes_accessed=2 * 10**6, transcendentals=4 * 10**6
         ),
     )(
-        windows, step_size, first, mid, last,
-        current_image.reshape(local), langevin_noise.reshape(local),
+        windows,
+        step_size,
+        *in_hbm(first, mid, last),
+        *in_hbm(current_image.reshape(local), langevin_noise.reshape(local)),
     ).reshape(current_image.shape)
 
 
@@ -479,8 +514,7 @@
     tall = lax.dynamic_slice_in_dim(
         volume, lax.axis_index("band") * local_slices, local_slices + 6, axis=0
     )
-    below = from_behind(tall[:, :, row_count - 3 :, :], "slab", 1)
-    above = from_behind(tall[:, :, :3, :], "slab", -1)
+    below, above = exchanged_rows(tall, 3)
     field = jnp.concatenate([below, tall, above, jnp.zeros_like(above[:, :, :2])], axis=2)
     windows = jnp.stack(
         [field[:, :, 4 * g : 4 * g + 8].reshape(-1, columns) for g in range(2)], axis=0

time: 49.7 us -> 38.7 us (0.78)
  the two profiles are of different devices: /device:TPU:0 before, /device:TPU:26 now
where the time goes in v2:
time: 38.7 us; the launch traced here: 38.4 us
  Pallas kernels  16.2 us (42%)
  starting transfers between devices  7.93 us (20%)
  blocking collectives  5.61 us (14%)
  waiting for transfers between devices  4.64 us (12%)
  other arithmetic  2.15 us (6%)
  local copies, waits for them, and re-layouts  1.1 us (3%)
  between operations  0.76 us (2%)
    pallas_call x1, Pallas kernels, stepped_without_data(): pl.pallas_call(network_kernel, out_shape=jax.ShapeDtypeStruct(local, jnp....  10.7 us
    all_gather x1, blocking collectives, per_device(): everyone = lax.all_gather(own, 'band', axis=0, tiled=True)  5.61 us
    pallas_call x1, Pallas kernels, partial_consistency(): pl.pallas_call(consistency_kernel, out_shape=jax.ShapeDtypeStruct((all_po...  5.56 us
    ppermute x2, waiting for transfers between devices, exchanged_rows(): arrived.append(lax.ppermute(sent, 'slab', route))  4.64 us
    ppermute x2, starting transfers between devices, exchanged_rows(): arrived.append(lax.ppermute(sent, 'slab', route))  4.05 us
    all_to_all x1, starting transfers between devices, per_device(): lax.all_to_all(partial_sums, 'band', split_axis=0, concat_axis=0, tiled=T...  3.88 us
    convert_element_type x1, other arithmetic, per_device(): current_image.astype(jnp.bfloat16)  0.91 us
    unnamed x2, local copies, waits for them, and re-layouts  0.9 us
  transfers between devices with their start and end apart: 3, of which 2 were waited for; matrix products, arithmetic and copies ran while one was open for 2% of the time, Pallas kernels for 28%

profile of v2, /device:TPU:26, one launch (start us, length us, event | category | flops | bytes accessed | tf_op | source)
XLA Modules:
  0.0 38.4 jit_solution(8440117432288094755)
XLA Ops:
  0.7 0.9 %convert_element_type.11 = bf16[2,4,2,4,384]{4,3,2,1,0:T(4,128)(2,1)S(1)} convert(f32[2,4,2,4,384]{4,3,2,1,0:T(4,128)} %param.12) | non-fusion elementwise | flops 24576 | bytes 147456 | tf_op jit(solution)/shard_map/convert_element_type | solution.py:507
  1.6 5.6 %all_gather.3.image_ref = bf16[8,4,8,384]{3,2,1,0:T(8,128)(2,1)S(1)} all-gather(bf16[2,4,8,384]{3,2,1,0:T(8,128)(2,1)S(1)} %reshape.18), channel_id=1, replica_groups=mesh['band'=4,'slab'=8] {'band'}, dimensions={0}, use_global_device_ids=true | all-gather | bytes 245760 | tf_op jit(solution)/shard_map/all_gather | solution.py:510
  7.2 0.0 copy-start
  7.2 0.9 %copy-done = f32[80,384]{1,0:T(8,128)S(1)} copy-done((f32[80,384]{1,0:T(8,128)S(1)}, f32[80,384]{1,0:T(8,128)}, u32[]{:S(2)}) %copy-start) | copy-done | bytes 122904
  8.1 5.6 %shard_map.119 = bf16[8,4,2,4,384]{4,3,2,1,0:T(4,128)(2,1)} custom-call(bf16[8,4,8,384]{3,2,1,0:T(8,128)(2,1)S(1)} %all_gather.3.image_ref, s32[8]{0:T(128)} %steps_hbm.1, s32[8]{0:T(128)} %order_hbm.1, f32[1]{0:T(128)S(6)} %copy.13.size_ref, bf16[8,4,8,2,4,384]{5,4,3,2,1,0:T(4,128)(2,1)} %coil_hbm.1, f32[4,8,2,4,384]{4,3,2,1,0:T(4,128)} %kspace_hbm.1, ...), custom_call_target="tpu_custom_call" | custom-call | flops 8000000000 | bytes 4000000 | tf_op jit(solution)/shard_map/pallas_call | solution.py:230
  13.7 3.9 %all-to-all-start = ((bf16[8,4,2,4,384]{4,3,2,1,0:T(4,128)(2,1)}), bf16[8,4,2,4,384]{4,3,2,1,0:T(4,128)(2,1)S(1)}, u32[]{:S(2)}, u32[]{:S(2)}) async-start(bf16[8,4,2,4,384]{4,3,2,1,0:T(4,128)(2,1)} %shard_map.119), calls=%async_computation | async-start | bytes 393216 | tf_op jit(solution)/shard_map/all_to_all | solution.py:525
  17.6 0.1 reshape.19
  17.6 0.1 broadcast_select_fusion.3
  17.8 1.6 %collective-permute-start = (bf16[14,2,3,384]{3,2,1,0:T(4,128)(2,1)S(1)}, bf16[14,2,3,384]{3,2,1,0:T(4,128)(2,1)S(1)}, u32[]{:S(2)}, u32[]{:S(2)}) collective-permute-start(bf16[14,2,3,384]{3,2,1,0:T(4,128)(2,1)S(1)} %get-tuple-element.5), channel_id=1, source_target_pairs={{0,1},{1,0},{2,3},{3,2},{4,5},{5,4},{6,7},{7,6},{8,9},{9,8},{10,11... | collective-permute-start | bytes 193544 | tf_op jit(solution)/shard_map/ppermute | solution.py:23
  19.3 2.5 %collective-permute-start.1 = (bf16[14,2,3,384]{3,2,1,0:T(4,128)(2,1)S(1)}, bf16[14,2,3,384]{3,2,1,0:T(4,128)(2,1)S(1)}, u32[]{:S(2)}, u32[]{:S(2)}) collective-permute-start(bf16[14,2,3,384]{3,2,1,0:T(4,128)(2,1)S(1)} %get-tuple-element.6), channel_id=1, source_target_pairs={{1,2},{2,1},{3,4},{4,3},{5,6},{6,5},{9,10},{10,9},{11,12},{12,11},... | collective-permute-start | bytes 193544 | tf_op jit(solution)/shard_map/ppermute | solution.py:23
  21.8 0.1 pad_dynamic-slice_fusion.2
  21.9 0.1 pad_slice_fusion
  22.0 0.4 %collective-permute-done = bf16[14,2,3,384]{3,2,1,0:T(4,128)(2,1)S(1)} collective-permute-done((bf16[14,2,3,384]{3,2,1,0:T(4,128)(2,1)S(1)}, bf16[14,2,3,384]{3,2,1,0:T(4,128)(2,1)S(1)}, u32[]{:S(2)}, u32[]{:S(2)}) %collective-permute-start) | collective-permute-done | bytes 64544 | tf_op jit(solution)/shard_map/ppermute | solution.py:23
  22.4 4.2 %collective-permute-done.1 = bf16[14,2,3,384]{3,2,1,0:T(4,128)(2,1)S(1)} collective-permute-done((bf16[14,2,3,384]{3,2,1,0:T(4,128)(2,1)S(1)}, bf16[14,2,3,384]{3,2,1,0:T(4,128)(2,1)S(1)}, u32[]{:S(2)}, u32[]{:S(2)}) %collective-permute-start.1) | collective-permute-done | bytes 64544 | tf_op jit(solution)/shard_map/ppermute | solution.py:23
  26.6 0.1 broadcast_select_fusion.1
  26.7 0.2 pad_maximum_fusion.2
  27.0 10.7 %shard_map.118 = f32[8,2,4,384]{3,2,1,0:T(4,128)S(1)} custom-call(bf16[2,224,384]{2,1,0:T(8,128)(2,1)S(1)} %pad_maximum_fusion.window_ref, f32[1]{0:T(128)S(6)} %copy.13.size_ref, bf16[3,3,3,2,64]{4,3,2,1,0:T(2,128)(2,1)} %bitcast.19, bf16[3,3,3,64,64]{4,3,2,1,0:T(8,128)(2,1)} %bitcast.17, bf16[3,3,3,2,64]{4,3,2,1,0:T(2,128)(2,1)} %bitcast.20, ...), custom_call_target="tpu_custom_call" | custom-call | flops 10000000000 | bytes 2000000 | tf_op jit(solution)/shard_map/pallas_call | solution.py:465
  37.6 0.0 all-to-all-done
  37.7 0.1 convert_reduce_fusion
  37.8 0.7 %sub.3 = f32[2,4,2,4,384]{4,3,2,1,0:T(4,128)} subtract(f32[2,4,2,4,384]{4,3,2,1,0:T(4,128)S(1)} %bitcast.12, f32[2,4,2,4,384]{4,3,2,1,0:T(4,128)S(1)} %convert_reduce_fusion) | non-fusion elementwise | flops 24576 | bytes 294912 | tf_op jit(solution)/shard_map/sub | solution.py:530
  (3 shorter events, 0.1 us)
Async XLA Ops:
  7.2 0.9 %copy-start = (f32[80,384]{1,0:T(8,128)S(1)}, f32[80,384]{1,0:T(8,128)}, u32[]{:S(2)}) copy-start(f32[80,384]{1,0:T(8,128)} %constant.34.clone.factors_hbm) | copy-start | bytes 368644
  13.7 24.0 %all-to-all-start = ((bf16[8,4,2,4,384]{4,3,2,1,0:T(4,128)(2,1)}), bf16[8,4,2,4,384]{4,3,2,1,0:T(4,128)(2,1)S(1)}, u32[]{:S(2)}, u32[]{:S(2)}) async-start(bf16[8,4,2,4,384]{4,3,2,1,0:T(4,128)(2,1)} %shard_map.119), calls=%async_computation | async-start | bytes 393216 | tf_op jit(solution)/shard_map/all_to_all | solution.py:525
  17.8 4.7 %collective-permute-start = (bf16[14,2,3,384]{3,2,1,0:T(4,128)(2,1)S(1)}, bf16[14,2,3,384]{3,2,1,0:T(4,128)(2,1)S(1)}, u32[]{:S(2)}, u32[]{:S(2)}) collective-permute-start(bf16[14,2,3,384]{3,2,1,0:T(4,128)(2,1)S(1)} %get-tuple-element.5), channel_id=1, source_target_pairs={{0,1},{1,0},{2,3},{3,2},{4,5},{5,4},{6,7},{7,6},{8,9},{9,8},{10,11... | collective-permute-start | bytes 193544 | tf_op jit(solution)/shard_map/ppermute | solution.py:23
  19.3 7.3 %collective-permute-start.1 = (bf16[14,2,3,384]{3,2,1,0:T(4,128)(2,1)S(1)}, bf16[14,2,3,384]{3,2,1,0:T(4,128)(2,1)S(1)}, u32[]{:S(2)}, u32[]{:S(2)}) collective-permute-start(bf16[14,2,3,384]{3,2,1,0:T(4,128)(2,1)S(1)} %get-tuple-element.6), channel_id=1, source_target_pairs={{1,2},{2,1},{3,4},{4,3},{5,6},{6,5},{9,10},{10,9},{11,12},{12,11},... | collective-permute-start | bytes 193544 | tf_op jit(solution)/shard_map/ppermute | solution.py:23

commit v3 on v2

--- a/solution.py
+++ b/solution.py
@@ -60,15 +60,25 @@
 
 
 def moved_right(value):
-    lanes = value.shape[-1]
-    lane = lax.broadcasted_iota(jnp.int32, (1, lanes), 1)
-    return jnp.where(lane == 0, 0.0, pltpu.roll(value, 1, 1))
+    tiles = value.shape[-1] // 128
+    moved = [pltpu.roll(value[:, 128 * j : 128 * (j + 1)], 1, 1) for j in range(tiles)]
+    edge = lax.broadcasted_iota(jnp.int32, moved[0].shape, 1) == 0
+    return jnp.concatenate(
+        [jnp.where(edge, moved[j - 1] if j > 0 else 0.0, moved[j]) for j in range(tiles)], axis=1
+    )
 
 
 def moved_left(value):
-    lanes = value.shape[-1]
-    lane = lax.broadcasted_iota(jnp.int32, (1, lanes), 1)
-    return jnp.where(lane == lanes - 1, 0.0, pltpu.roll(value, lanes - 1, 1))
+    tiles = value.shape[-1] // 128
+    moved = [pltpu.roll(value[:, 128 * j : 128 * (j + 1)], 127, 1) for j in range(tiles)]
+    edge = lax.broadcasted_iota(jnp.int32, moved[0].shape, 1) == 127
+    return jnp.concatenate(
+        [
+            jnp.where(edge, moved[j + 1] if j < tiles - 1 else 0.0, moved[j])
+            for j in range(tiles)
+        ],
+        axis=1,
+    )
 
 
 def half_silu(half):
@@ -115,26 +125,29 @@
 
 
 def consistency_kernel(
-    image_ref, steps_hbm, order_hbm, size_ref, coil_hbm, kspace_hbm, mask_hbm, factors_hbm,
+    image_hbm, steps_hbm, order_hbm, size_ref, coil_hbm, kspace_hbm, mask_hbm, factors_hbm,
     out_ref,
-    steps_ref, order_ref, coil_ref, kspace_ref, mask_ref, factors_ref, high_ref, low_ref,
-    turned_ref, real_ref, imag_ref, field_ref, swap_ref, sum_ref, sems, coil_sems,
+    image_ref, steps_ref, order_ref, coil_ref, kspace_ref, mask_ref, factors_ref,
+    high_ref, low_ref, turned_ref, real_ref, imag_ref, field_ref, swap_ref, sum_ref,
+    sems, coil_sems,
 ):
     all_positions, slices, coils, _, rows, columns = coil_ref.shape
     tiles = columns // 128
     unit = columns // 8
     pairs = (
-        (steps_hbm, steps_ref), (order_hbm, order_ref),
-        (kspace_hbm, kspace_ref), (mask_hbm, mask_ref), (factors_hbm, factors_ref),
+        (factors_hbm, factors_ref), (steps_hbm, steps_ref), (order_hbm, order_ref),
+        (image_hbm, image_ref), (kspace_hbm, kspace_ref), (mask_hbm, mask_ref),
     )
     copies = [pltpu.make_async_copy(src, dst, sems.at[i]) for i, (src, dst) in enumerate(pairs)]
-    for copy in copies[:2]:
+    for copy in copies[:3]:
         copy.start()
     for g in range(all_positions):
         pltpu.make_async_copy(coil_hbm.at[g], coil_ref.at[g], coil_sems.at[g]).start()
-    for copy in copies[2:]:
+    for copy in copies[3:]:
         copy.start()
-    for copy in copies[:2]:
+    copies[0].wait()
+    build_tables(factors_ref, high_ref, low_ref)
+    for copy in copies[1:3]:
         copy.wait()
 
     def shift_of(g):
@@ -142,26 +155,28 @@
 
     def turn_coils(g):
         shift = shift_of(g)
-        image = image_ref[g].astype(jnp.float32)
-
-        def store_image(j, value):
+        pltpu.make_async_copy(coil_hbm.at[g], coil_ref.at[g], coil_sems.at[g]).wait()
+        for s in range(slices):
+            coil = stacked_parts(coil_ref[g, s].astype(jnp.float32))
+
+            def store_coil(j, value, s=s):
+                turned_ref[j, g, s] = value
+
+            turned_tiles(coil, shift, store_coil)
+
+    for g in range(all_positions):
+        turn_coils(g)
+    for copy in copies[3:]:
+        copy.wait()
+    for g in range(all_positions):
+
+        def store_image(j, value, g=g):
             other = halves_swapped(value)
             top = upper_half(value)
             real_ref[j, g] = jnp.where(top, value, other)
             imag_ref[j, g] = jnp.where(top, other, value)
 
-        turned_tiles(image, shift, store_image)
-        pltpu.make_async_copy(coil_hbm.at[g], coil_ref.at[g], coil_sems.at[g]).wait()
-        for s in range(slices):
-            coil = stacked_parts(coil_ref[g, s].astype(jnp.float32))
-
-            def store_coil(j, value, s=s):
-                turned_ref[j, g, s] = value
-
-            turned_tiles(coil, shift, store_coil)
-
-    for g in range(all_positions):
-        turn_coils(g)
+        turned_tiles(image_ref[g].astype(jnp.float32), shift_of(g), store_image)
 
     block = coils * 2 * rows
     for j in range(tiles):
@@ -177,9 +192,6 @@
                 block, 128
             )
 
-    for copy in copies[2:]:
-        copy.wait()
-    build_tables(factors_ref, high_ref, low_ref)
     product = table_product(field_ref[...], high_ref, low_ref)
     grouped = (slices, coils, 2 * rows, columns)
     with_cos = product[:, :columns].reshape(grouped)
@@ -230,9 +242,10 @@
     return pl.pallas_call(
         consistency_kernel,
         out_shape=jax.ShapeDtypeStruct((all_positions, slices, 2, rows, columns), jnp.bfloat16),
-        in_specs=[vmem, hbm, hbm, pl.BlockSpec(memory_space=pltpu.SMEM)] + [hbm] * 4,
+        in_specs=[hbm] * 3 + [pl.BlockSpec(memory_space=pltpu.SMEM)] + [hbm] * 4,
         out_specs=vmem,
         scratch_shapes=[
+            pltpu.VMEM(everyone.shape, jnp.bfloat16),
             pltpu.SMEM(caipi_steps.shape, jnp.int32),
             pltpu.SMEM(band_order.shape, jnp.int32),
             pltpu.VMEM(coil_maps.shape, jnp.bfloat16),
@@ -247,7 +260,7 @@
             pltpu.VMEM((total, columns), jnp.float32),
             pltpu.VMEM((total, columns), jnp.float32),
             pltpu.VMEM((all_positions, slices, 2 * rows, columns), jnp.float32),
-            pltpu.SemaphoreType.DMA((5,)),
+            pltpu.SemaphoreType.DMA((6,)),
             pltpu.SemaphoreType.DMA((all_positions,)),
         ],
         compiler_params=pltpu.CompilerParams(vmem_limit_bytes=48 * 2**20),
@@ -255,8 +268,7 @@
             flops=8 * 10**9, bytes_accessed=4 * 10**6, transcendentals=0
         ),
     )(
-        everyone,
-        *in_hbm(caipi_steps, band_order),
+        *in_hbm(everyone, caipi_steps, band_order),
         step_size,
         *in_hbm(coil_maps, measured_kspace, sample_mask),
         factors,
@@ -515,14 +527,15 @@
         volume, lax.axis_index("band") * local_slices, local_slices + 6, axis=0
     )
     below, above = exchanged_rows(tall, 3)
+    partial_sums = partial_consistency(
+        everyone, step_size, coil_maps, measured_kspace, sample_mask, caipi_steps, band_order
+    )
+    partial_sums, below, above = lax.optimization_barrier((partial_sums, below, above))
+    swapped = lax.all_to_all(partial_sums, "band", split_axis=0, concat_axis=0, tiled=True)
     field = jnp.concatenate([below, tall, above, jnp.zeros_like(above[:, :, :2])], axis=2)
     windows = jnp.stack(
         [field[:, :, 4 * g : 4 * g + 8].reshape(-1, columns) for g in range(2)], axis=0
     )
-    partial_sums = partial_consistency(
-        everyone, step_size, coil_maps, measured_kspace, sample_mask, caipi_steps, band_order
-    )
-    swapped = lax.all_to_all(partial_sums, "band", split_axis=0, concat_axis=0, tiled=True)
     base = stepped_without_data(
         windows, current_image, langevin_noise, step_size, weight_in, weight_mid, weight_out
     )

time: 38.7 us -> 35.4 us (0.915)
  the two profiles are of different devices: /device:TPU:26 before, /device:TPU:0 now
where the time goes in v3:
time: 35.4 us; the launch traced here: 35.2 us
  Pallas kernels  16.4 us (46%)
  starting transfers between devices  8.79 us (25%)
  blocking collectives  6.84 us (19%)
  other arithmetic  2.19 us (6%)
  between operations  0.76 us (2%)
    pallas_call x1, Pallas kernels, stepped_without_data(): pl.pallas_call(network_kernel, out_shape=jax.ShapeDtypeStruct(local, jnp....  10.6 us
    all_gather x1, blocking collectives, per_device(): everyone = lax.all_gather(own, 'band', axis=0, tiled=True)  6.84 us
    pallas_call x1, Pallas kernels, partial_consistency(): pl.pallas_call(consistency_kernel, out_shape=jax.ShapeDtypeStruct((all_po...  5.74 us
    ppermute x2, starting transfers between devices, exchanged_rows(): arrived.append(lax.ppermute(sent, 'slab', route))  5.23 us
    all_to_all x1, starting transfers between devices, per_device(): lax.all_to_all(partial_sums, 'band', split_axis=0, concat_axis=0, tiled=T...  3.56 us
    convert_element_type x1, other arithmetic, per_device(): current_image.astype(jnp.bfloat16)  0.95 us
  transfers between devices with their start and end apart: 3, of which 0 were waited for; matrix products, arithmetic and copies ran while one was open for 1% of the time, Pallas kernels for 46%

profile of v3, /device:TPU:0, one launch (start us, length us, event | category | flops | bytes accessed | tf_op | source)
XLA Modules:
  0.0 35.2 jit_solution(6694070525976350842)
XLA Ops:
  0.0 0.0 copy-start
  0.0 0.9 %convert_element_type.11 = bf16[2,4,2,4,384]{4,3,2,1,0:T(4,128)(2,1)S(1)} convert(f32[2,4,2,4,384]{4,3,2,1,0:T(4,128)} %param.12) | non-fusion elementwise | flops 24576 | bytes 147456 | tf_op jit(solution)/shard_map/convert_element_type | solution.py:519
  1.0 6.8 %all_gather.3.image_hbm = bf16[8,4,8,384]{3,2,1,0:T(8,128)(2,1)S(1)} all-gather(bf16[2,4,8,384]{3,2,1,0:T(8,128)(2,1)S(1)} %reshape.18), channel_id=1, replica_groups=mesh['band'=4,'slab'=8] {'band'}, dimensions={0}, use_global_device_ids=true | all-gather | bytes 245760 | tf_op jit(solution)/shard_map/all_gather | solution.py:522
  7.8 0.0 copy-start.1
  7.8 0.1 reshape.19
  7.9 0.1 broadcast_select_fusion.2
  8.0 0.7 %collective-permute-start.1 = (bf16[14,2,3,384]{3,2,1,0:T(4,128)(2,1)S(1)}, bf16[14,2,3,384]{3,2,1,0:T(4,128)(2,1)S(1)}, u32[]{:S(2)}, u32[]{:S(2)}) collective-permute-start(bf16[14,2,3,384]{3,2,1,0:T(4,128)(2,1)S(1)} %get-tuple-element.11), channel_id=1, source_target_pairs={{1,2},{2,1},{3,4},{4,3},{5,6},{6,5},{9,10},{10,9},{11,12},{12,11},... | collective-permute-start | bytes 193544 | tf_op jit(solution)/shard_map/ppermute | solution.py:23
  8.7 4.6 %collective-permute-start = (bf16[14,2,3,384]{3,2,1,0:T(4,128)(2,1)S(1)}, bf16[14,2,3,384]{3,2,1,0:T(4,128)(2,1)S(1)}, u32[]{:S(2)}, u32[]{:S(2)}) collective-permute-start(bf16[14,2,3,384]{3,2,1,0:T(4,128)(2,1)S(1)} %get-tuple-element.12), channel_id=1, source_target_pairs={{0,1},{1,0},{2,3},{3,2},{4,5},{5,4},{6,7},{7,6},{8,9},{9,8},{10,11... | collective-permute-start | bytes 193544 | tf_op jit(solution)/shard_map/ppermute | solution.py:23
  14.0 0.0 copy-done.1
  14.0 0.0 copy-done
  14.0 5.7 %shard_map.118 = bf16[8,4,2,4,384]{4,3,2,1,0:T(4,128)(2,1)} custom-call(bf16[8,4,8,384]{3,2,1,0:T(8,128)(2,1)} %copy-done.1, s32[8]{0:T(128)} %steps_hbm.1, s32[8]{0:T(128)} %order_hbm.1, f32[1]{0:T(128)S(6)} %copy.13.size_ref, bf16[8,4,8,2,4,384]{5,4,3,2,1,0:T(4,128)(2,1)} %coil_hbm.1, f32[4,8,2,4,384]{4,3,2,1,0:T(4,128)} %kspace_hbm.1, s32[4,384]{1,0:T(4,128)} %mask_hbm.1, ...), custom_call_target="tpu_custom_call" | custom-call | flops 8000000000 | bytes 4000000 | tf_op jit(solution)/shard_map/pallas_call | solution.py:242
  19.7 0.1 pad_slice_fusion
  19.8 0.0 collective-permute-done.1
  19.8 0.0 collective-permute-done
  19.8 0.1 broadcast_select_fusion
  19.9 3.6 %all-to-all-start = ((bf16[8,4,2,4,384]{4,3,2,1,0:T(4,128)(2,1)}), bf16[8,4,2,4,384]{4,3,2,1,0:T(4,128)(2,1)S(1)}, u32[]{:S(2)}, u32[]{:S(2)}) async-start(bf16[8,4,2,4,384]{4,3,2,1,0:T(4,128)(2,1)} %shard_map.118), calls=%async_computation | async-start | bytes 393216 | tf_op jit(solution)/shard_map/all_to_all | solution.py:534
  23.5 0.2 pad_maximum_fusion.2
  23.7 10.6 %shard_map.119 = f32[8,2,4,384]{3,2,1,0:T(4,128)S(1)} custom-call(bf16[2,224,384]{2,1,0:T(8,128)(2,1)S(1)} %pad_maximum_fusion.window_ref, f32[1]{0:T(128)S(6)} %copy.13.size_ref, bf16[3,3,3,2,64]{4,3,2,1,0:T(2,128)(2,1)} %bitcast.19, bf16[3,3,3,64,64]{4,3,2,1,0:T(8,128)(2,1)} %bitcast.17, bf16[3,3,3,2,64]{4,3,2,1,0:T(2,128)(2,1)} %bitcast.20, ...), custom_call_target="tpu_custom_call" | custom-call | flops 10000000000 | bytes 2000000 | tf_op jit(solution)/shard_map/pallas_call | solution.py:477
  34.4 0.0 all-to-all-done
  34.4 0.1 convert_reduce_fusion
  34.5 0.7 %sub.3 = f32[2,4,2,4,384]{4,3,2,1,0:T(4,128)} subtract(f32[2,4,2,4,384]{4,3,2,1,0:T(4,128)S(1)} %bitcast.12, f32[2,4,2,4,384]{4,3,2,1,0:T(4,128)S(1)} %convert_reduce_fusion) | non-fusion elementwise | flops 24576 | bytes 294912 | tf_op jit(solution)/shard_map/sub | solution.py:543
  (4 shorter events, 0.1 us)
Async XLA Ops:
  0.0 14.0 %copy-start = (f32[80,384]{1,0:T(8,128)S(1)}, f32[80,384]{1,0:T(8,128)}, u32[]{:S(2)}) copy-start(f32[80,384]{1,0:T(8,128)} %constant.34.clone.factors_hbm) | copy-start | bytes 368644
  7.8 6.1 %copy-start.1 = (bf16[8,4,8,384]{3,2,1,0:T(8,128)(2,1)}, bf16[8,4,8,384]{3,2,1,0:T(8,128)(2,1)S(1)}, u32[]{:S(2)}) copy-start(bf16[8,4,8,384]{3,2,1,0:T(8,128)(2,1)S(1)} %all_gather.3.image_hbm) | copy-start | bytes 589828
  8.0 11.8 %collective-permute-start.1 = (bf16[14,2,3,384]{3,2,1,0:T(4,128)(2,1)S(1)}, bf16[14,2,3,384]{3,2,1,0:T(4,128)(2,1)S(1)}, u32[]{:S(2)}, u32[]{:S(2)}) collective-permute-start(bf16[14,2,3,384]{3,2,1,0:T(4,128)(2,1)S(1)} %get-tuple-element.11), channel_id=1, source_target_pairs={{1,2},{2,1},{3,4},{4,3},{5,6},{6,5},{9,10},{10,9},{11,12},{12,11},... | collective-permute-start | bytes 193544 | tf_op jit(solution)/shard_map/ppermute | solution.py:23
  8.7 11.1 %collective-permute-start = (bf16[14,2,3,384]{3,2,1,0:T(4,128)(2,1)S(1)}, bf16[14,2,3,384]{3,2,1,0:T(4,128)(2,1)S(1)}, u32[]{:S(2)}, u32[]{:S(2)}) collective-permute-start(bf16[14,2,3,384]{3,2,1,0:T(4,128)(2,1)S(1)} %get-tuple-element.12), channel_id=1, source_target_pairs={{0,1},{1,0},{2,3},{3,2},{4,5},{5,4},{6,7},{7,6},{8,9},{9,8},{10,11... | collective-permute-start | bytes 193544 | tf_op jit(solution)/shard_map/ppermute | solution.py:23
  19.9 14.5 %all-to-all-start = ((bf16[8,4,2,4,384]{4,3,2,1,0:T(4,128)(2,1)}), bf16[8,4,2,4,384]{4,3,2,1,0:T(4,128)(2,1)S(1)}, u32[]{:S(2)}, u32[]{:S(2)}) async-start(bf16[8,4,2,4,384]{4,3,2,1,0:T(4,128)(2,1)} %shard_map.118), calls=%async_computation | async-start | bytes 393216 | tf_op jit(solution)/shard_map/all_to_all | solution.py:534

commit v4 on v3

v4 whole, which is shorter than its diff:
```python
import functools
import math

import jax
import jax.numpy as jnp
import numpy as np
from jax import lax
from jax.experimental import pallas as pl
from jax.experimental.pallas import tpu as pltpu
from jax.sharding import PartitionSpec as P


def exchanged_rows(tall, width):
    count = lax.axis_size("slab")
    odd = lax.axis_index("slab") % 2 == 1
    head, tail = tall[:, :, :width, :], tall[:, :, tall.shape[2] - width :, :]
    arrived = []
    for first in range(2):
        route = []
        for i in range(first, count - 1, 2):
            route += [(i, i + 1), (i + 1, i)]
        sent = jnp.where(odd, head, tail) if first == 0 else jnp.where(odd, tail, head)
        arrived.append(lax.ppermute(sent, "slab", route))
    below = jnp.where(odd, arrived[0], arrived[1])
    above = jnp.where(odd, arrived[1], arrived[0])
    return below, above


def in_hbm(*arrays):
    return [pltpu.with_memory_space_constraint(array, pltpu.HBM) for array in arrays]


def dft_factors(columns):
    near = 16
    index = np.arange(columns)
    pieces = []
    for rows in (near * np.arange(columns // near), np.arange(near)):
        phase = (np.outer(rows, index) % columns) * (2.0 * math.pi / columns)
        pieces += [np.cos(phase), np.sin(phase)]
    far = np.concatenate(pieces[:2], axis=0) / math.sqrt(columns)
    return np.concatenate([far] + pieces[2:], axis=0).astype(np.float32)


def build_tables(factors_ref, high_ref, low_ref):
    columns = factors_ref.shape[1]
    near = 16
    count = columns // near
    near_cos = factors_ref[2 * count : 2 * count + near, :]
    near_sin = factors_ref[2 * count + near :, :]
    for a in range(count):
        far_cos = factors_ref[a : a + 1, :]
        far_sin = factors_ref[count + a : count + a + 1, :]
        tables = (far_cos * near_cos - far_sin * near_sin, far_sin * near_cos + far_cos * near_sin)
        rows = slice(near * a, near * (a + 1))
        for part, table in enumerate(tables):
            high = table.astype(jnp.bfloat16)
            lanes = slice(columns * part, columns * (part + 1))
            high_ref[rows, lanes] = high
            low_ref[rows, lanes] = (table - high.astype(jnp.float32)).astype(jnp.bfloat16)


def moved_right(value):
    tiles = value.shape[-1] // 128
    moved = [pltpu.roll(value[:, 128 * j : 128 * (j + 1)], 1, 1) for j in range(tiles)]
    edge = lax.broadcasted_iota(jnp.int32, moved[0].shape, 1) == 0
    return jnp.concatenate(
        [jnp.where(edge, moved[j - 1] if j > 0 else 0.0, moved[j]) for j in range(tiles)], axis=1
    )


def moved_left(value):
    tiles = value.shape[-1] // 128
    moved = [pltpu.roll(value[:, 128 * j : 128 * (j + 1)], 127, 1) for j in range(tiles)]
    edge = lax.broadcasted_iota(jnp.int32, moved[0].shape, 1) == 127
    return jnp.concatenate(
        [
            jnp.where(edge, moved[j + 1] if j < tiles - 1 else 0.0, moved[j])
            for j in range(tiles)
        ],
        axis=1,
    )


def half_silu(half):
    return half + half * jnp.tanh(half)


def table_product(source, high_ref, low_ref):
    rows = source.shape[0]
    high = source.astype(jnp.bfloat16)
    low = (source - high.astype(jnp.float32)).astype(jnp.bfloat16)
    both = jnp.dot(
        jnp.concatenate([high, low], axis=0), high_ref[...], preferred_element_type=jnp.float32
    )
    rest = jnp.dot(high, low_ref[...], preferred_element_type=jnp.float32)
    return both[:rows] + both[rows:] + rest


def halves_swapped(value):
    return pltpu.roll(value, 4, value.ndim - 2)


def upper_half(value):
    return lax.broadcasted_iota(jnp.int32, value.shape, value.ndim - 2) < 4


def signed_swap(value, top, bottom):
    sign = jnp.where(upper_half(value), top, bottom)
    return sign * halves_swapped(value)


def stacked_parts(value):
    return jnp.concatenate([value[..., 0, :, :], value[..., 1, :, :]], axis=-2)


def turned_tiles(value, shift, store):
    tiles = value.shape[-1] // 128
    whole, part = shift // 128, lax.rem(shift, 128)
    moved = [
        pltpu.roll(value[..., 128 * j : 128 * (j + 1)], part, value.ndim - 1) for j in range(tiles)
    ]
    lane = lax.broadcasted_iota(jnp.int32, moved[0].shape, value.ndim - 1)
    for j in range(tiles):
        store(lax.rem(j + whole, tiles), jnp.where(lane < part, moved[j - 1], moved[j]))


def fill_weights(first_raw, mid_raw, last_raw, first_sum, last_sum, first_ref, wide_ref, last_ref):
    channels = mid_raw.shape[-1]
    two = 2 * channels
    first_sum[...] = jnp.zeros_like(first_sum)
    last_sum[...] = jnp.zeros_like(last_sum)
    for d in range(3):
        for u in range(3):
            for t in range(3):
                block = first_raw[d, u, t].astype(jnp.float32) * 0.5
                for i in range(2):
                    for r in range(4):
                        row = (t * 3 + d) * 16 + i * 8 + u + r
                        first_sum[row : row + 1, r * channels : (r + 1) * channels] = block[
                            i : i + 1
                        ]
                block = last_raw[d, u, t].astype(jnp.float32)
                for o in range(2):
                    for r in range(4):
                        row = (d * 3 + t) * 8 + o * 4 + r
                        col = (r + u) * channels
                        last_sum[row : row + 1, col : col + channels] = block[o : o + 1]
    first_ref[...] = first_sum[...].T[:, : first_ref.shape[1]].astype(jnp.bfloat16)
    last_ref[...] = last_sum[...].astype(jnp.bfloat16)
    half_weight = jnp.bfloat16(0.5)
    for t in range(3):
        for r in range(2):
            row = (t * 2 + r) * channels
            for d in range(3):
                for pair in range(2):
                    blocks = []
                    for q in (2 * pair, 2 * pair + 1):
                        if 0 <= q - r <= 2:
                            blocks.append(mid_raw[d, q - r, t] * half_weight)
                        else:
                            blocks.append(jnp.zeros((channels, channels), jnp.bfloat16))
                    col = (d * 4 + 2 * pair) * channels
                    wide_ref[row : row + channels, col : col + two] = jnp.concatenate(
                        blocks, axis=1
                    )


def preparation_kernel(
    steps_hbm, order_hbm, coil_hbm, kspace_hbm, factors_hbm, first_hbm, mid_hbm, last_hbm,
    turned_ref, stacked_ref, high_ref, low_ref, first_ref, wide_ref, last_ref,
    steps_ref, order_ref, coil_ref, kspace_ref, factors_ref, first_raw, mid_raw, last_raw,
    first_sum, last_sum, sems, coil_sems,
):
    all_positions, slices, coils, _, rows, columns = coil_ref.shape
    unit = columns // 8
    pairs = (
        (first_hbm, first_raw), (mid_hbm, mid_raw), (last_hbm, last_raw),
        (factors_hbm, factors_ref), (steps_hbm, steps_ref), (order_hbm, order_ref),
        (kspace_hbm, kspace_ref),
    )
    copies = [pltpu.make_async_copy(src, dst, sems.at[i]) for i, (src, dst) in enumerate(pairs)]
    coil_copies = [
        pltpu.make_async_copy(coil_hbm.at[g], coil_ref.at[g], coil_sems.at[g])
        for g in range(all_positions)
    ]
    for copy in copies[:6] + coil_copies + copies[6:]:
        copy.start()
    for copy in copies[:3]:
        copy.wait()
    fill_weights(
        first_raw, mid_raw, last_raw, first_sum, last_sum, first_ref, wide_ref, last_ref
    )
    copies[3].wait()
    build_tables(factors_ref, high_ref, low_ref)
    for copy in copies[4:6]:
        copy.wait()
    for g in range(all_positions):
        shift = steps_ref[order_ref[g]] * unit
        coil_copies[g].wait()
        for s in range(slices):

            def store_coil(j, value, s=s, g=g):
                turned_ref[j, g, s] = value

            turned_tiles(stacked_parts(coil_ref[g, s].astype(jnp.float32)), shift, store_coil)
    copies[6].wait()
    for s in range(slices):
        stacked_ref[s] = stacked_parts(kspace_ref[s])


def preparation(
    coil_maps, measured_kspace, caipi_steps, band_order, weight_in, weight_mid, weight_out
):
    all_positions, slices, coils, _, rows, columns = coil_maps.shape
    channels = weight_mid.shape[0]
    factors = jnp.asarray(dft_factors(columns))
    first = jnp.transpose(weight_in, (2, 3, 4, 1, 0))
    mid = jnp.transpose(weight_mid, (2, 3, 4, 0, 1))
    last = jnp.transpose(weight_out, (2, 3, 4, 0, 1))
    f32, bf16 = jnp.float32, jnp.bfloat16
    hbm = pl.BlockSpec(memory_space=pltpu.HBM)
    vmem = pl.BlockSpec(memory_space=pltpu.VMEM)
    return pl.pallas_call(
        preparation_kernel,
        out_shape=(
            jax.ShapeDtypeStruct((columns // 128, all_positions, slices, coils, 2 * rows, 128), f32),
            jax.ShapeDtypeStruct((slices, coils, 2 * rows, columns), f32),
            jax.ShapeDtypeStruct((columns, 2 * columns), bf16),
            jax.ShapeDtypeStruct((columns, 2 * columns), bf16),
            jax.ShapeDtypeStruct((4 * channels, 144), bf16),
            jax.ShapeDtypeStruct((6 * channels, 12 * channels), bf16),
            jax.ShapeDtypeStruct((72, 6 * channels), bf16),
        ),
        in_specs=[hbm] * 8,
        out_specs=(vmem,) * 7,
        scratch_shapes=[
            pltpu.SMEM(caipi_steps.shape, jnp.int32),
            pltpu.SMEM(band_order.shape, jnp.int32),
            pltpu.VMEM(coil_maps.shape, bf16),
            pltpu.VMEM(measured_kspace.shape, f32),
            pltpu.VMEM(factors.shape, f32),
            pltpu.VMEM(first.shape, bf16),
            pltpu.VMEM(mid.shape, bf16),
            pltpu.VMEM(last.shape, bf16),
            pltpu.VMEM((256, 4 * channels), f32),
            pltpu.VMEM((72, 6 * channels), f32),
            pltpu.SemaphoreType.DMA((7,)),
            pltpu.SemaphoreType.DMA((all_positions,)),
        ],
        compiler_params=pltpu.CompilerParams(vmem_limit_bytes=40 * 2**20),
        cost_estimate=pl.CostEstimate(
            flops=4 * 10**9, bytes_accessed=4 * 10**6, transcendentals=0
        ),
    )(
        *in_hbm(caipi_steps, band_order, coil_maps, measured_kspace),
        factors,
        *in_hbm(first, mid, last),
    )


def consistency_kernel(
    own_ref, one_ref, two_ref, three_ref, turned_ref, stacked_ref, high_ref, low_ref,
    size_ref, steps_hbm, order_hbm, mask_hbm,
    out_ref,
    steps_ref, order_ref, mask_ref, real_ref, imag_ref, field_ref, swap_ref, sum_ref,
    sems,
):
    tiles, all_positions, slices, coils, doubled, _ = turned_ref.shape
    rows, columns = doubled // 2, stacked_ref.shape[-1]
    positions = all_positions // 4
    unit = columns // 8
    pairs = (
        (steps_hbm, steps_ref), (order_hbm, order_ref), (mask_hbm, mask_ref),
    )
    copies = [pltpu.make_async_copy(src, dst, sems.at[i]) for i, (src, dst) in enumerate(pairs)]
    for copy in copies:
        copy.start()
    for copy in copies:
        copy.wait()

    def shift_of(g):
        return steps_ref[order_ref[g]] * unit

    for x, ref in enumerate((own_ref, one_ref, two_ref, three_ref)):
        for p in range(positions):
            g = lax.bitwise_xor(lax.axis_index("band"), jnp.int32(x)) * positions + p

            def store_image(j, value, g=g):
                other = halves_swapped(value)
                top = upper_half(value)
                real_ref[j, g] = jnp.where(top, value, other)
                imag_ref[j, g] = jnp.where(top, other, value)

            image = ref[p * slices : (p + 1) * slices].astype(jnp.float32)
            turned_tiles(image, shift_of(g), store_image)

    block = coils * 2 * rows
    for j in range(tiles):
        for s in range(slices):
            with_real = jnp.zeros((coils, 2 * rows, 128), jnp.float32)
            with_imag = jnp.zeros((coils, 2 * rows, 128), jnp.float32)
            for g in range(all_positions):
                coil = turned_ref[j, g, s]
                with_real += coil * real_ref[j, g, s]
                with_imag += coil * imag_ref[j, g, s]
            total = with_real + signed_swap(with_imag, -1.0, 1.0)
            field_ref[s * block : (s + 1) * block, 128 * j : 128 * (j + 1)] = total.reshape(
                block, 128
            )

    product = table_product(field_ref[...], high_ref, low_ref)
    grouped = (slices, coils, 2 * rows, columns)
    with_cos = product[:, :columns].reshape(grouped)
    with_sin = product[:, columns:].reshape(grouped)
    spectrum = with_cos + signed_swap(with_sin, 1.0, -1.0)
    keep = mask_ref[...].astype(jnp.float32).reshape(slices, 1, 1, columns)
    residual = keep * (spectrum - stacked_ref[...])
    product = table_product(residual.reshape(slices * block, columns), high_ref, low_ref)
    with_cos = product[:, :columns].reshape(grouped)
    with_sin = product[:, columns:].reshape(grouped)
    back = with_cos + signed_swap(with_sin, -1.0, 1.0)
    field_ref[...] = back.reshape(slices * block, columns)
    swap_ref[...] = halves_swapped(back).reshape(slices * block, columns)

    size = size_ref[0]
    for j in range(tiles):
        for s in range(slices):
            place = (slice(s * block, (s + 1) * block), slice(128 * j, 128 * (j + 1)))
            field = field_ref[place].reshape(coils, 2 * rows, 128)
            swapped = swap_ref[place].reshape(coils, 2 * rows, 128)
            for g in range(all_positions):
                coil = turned_ref[j, g, s]
                straight = jnp.sum(coil * field, axis=0)
                crossed = jnp.sum(coil * swapped, axis=0)
                straight = straight + halves_swapped(straight)
                crossed = halves_swapped(crossed) - crossed
                sum_ref[g, s, :, 128 * j : 128 * (j + 1)] = size * jnp.where(
                    upper_half(straight), straight, crossed
                )

    for g in range(all_positions):
        back_shift = lax.rem(columns - shift_of(g), columns)
        turned = pltpu.roll(sum_ref[g], back_shift, 2).astype(jnp.bfloat16)
        out_ref[g, :, 0] = turned[:, :rows]
        out_ref[g, :, 1] = turned[:, rows:]


def partial_consistency(images, prepared, size, sample_mask, caipi_steps, band_order):
    tiles, all_positions, slices, coils, doubled, _ = prepared[0].shape
    columns = sample_mask.shape[-1]
    total = slices * coils * doubled
    hbm = pl.BlockSpec(memory_space=pltpu.HBM)
    vmem = pl.BlockSpec(memory_space=pltpu.VMEM)
    image_shape = (tiles, all_positions, slices, doubled, 128)
    return pl.pallas_call(
        consistency_kernel,
        out_shape=jax.ShapeDtypeStruct(
            (all_positions, slices, 2, doubled // 2, columns), jnp.bfloat16
        ),
        in_specs=[vmem] * 8 + [pl.BlockSpec(memory_space=pltpu.SMEM)] + [hbm] * 3,
        out_specs=vmem,
        scratch_shapes=[
            pltpu.SMEM(caipi_steps.shape, jnp.int32),
            pltpu.SMEM(band_order.shape, jnp.int32),
            pltpu.VMEM(sample_mask.shape, jnp.int32),
            pltpu.VMEM(image_shape, jnp.float32),
            pltpu.VMEM(image_shape, jnp.float32),
            pltpu.VMEM((total, columns), jnp.float32),
            pltpu.VMEM((total, columns), jnp.float32),
            pltpu.VMEM((all_positions, slices, doubled, columns), jnp.float32),
            pltpu.SemaphoreType.DMA((3,)),
        ],
        compiler_params=pltpu.CompilerParams(vmem_limit_bytes=40 * 2**20),
        cost_estimate=pl.CostEstimate(
            flops=4 * 10**9, bytes_accessed=4 * 10**6, transcendentals=0
        ),
    )(*images, *prepared, size, *in_hbm(caipi_steps, band_order, sample_mask))


def network_kernel(
    window_ref, first_ref, wide_ref, last_ref, size_ref, image_hbm, noise_hbm,
    out_ref,
    image_ref, noise_ref, taps_ref, f1_ref, f2_ref, part_a, part_b, score_ref, sems,
):
    channels = first_ref.shape[0] // 4
    out_slices, _, rows, columns = out_ref.shape
    slices1, slices2 = out_slices + 4, out_slices + 2
    pairs = (
        (image_hbm, image_ref), (noise_hbm, noise_ref),
    )
    copies = [pltpu.make_async_copy(src, dst, sems.at[i]) for i, (src, dst) in enumerate(pairs)]
    for copy in copies:
        copy.start()

    def inside(axis, end):
        edge = lax.axis_size(axis) - 1 if end else 0
        return jnp.where(lax.axis_index(axis) == edge, 0.0, 1.0).astype(jnp.float32)

    low_slice, high_slice = inside("band", False), inside("band", True)
    low_row, high_row = inside("slab", False), inside("slab", True)
    four, two = 4 * channels, 2 * channels

    for g in range(2):
        base = window_ref[g].astype(jnp.float32)
        taps_ref[g, 0] = moved_right(base).astype(jnp.bfloat16)
        taps_ref[g, 1] = window_ref[g]
        taps_ref[g, 2] = moved_left(base).astype(jnp.bfloat16)

    def first_layer(z):
        source = jnp.concatenate(
            [
                jnp.concatenate([taps_ref[g, t, 16 * z : 16 * z + 48, :] for t in range(3)], axis=0)
                for g in range(2)
            ],
            axis=1,
        )
        half = jnp.dot(first_ref[...], source, preferred_element_type=jnp.float32)
        for r in range(8):
            begin = (r % 4) * channels
            first = columns * (r // 4)
            value = half_silu(half[begin : begin + channels, first : first + columns])
            factors = []
            if z < 2:
                factors.append(low_slice)
            if z >= slices1 - 2:
                factors.append(high_slice)
            if r < 2:
                factors.append(low_row)
            if r >= 6:
                factors.append(high_row)
            for factor in factors:
                value = value * factor
            f1_ref[z, r * channels : (r + 1) * channels, :] = value.astype(jnp.bfloat16)

    def second_product(z, pair, part_ref):
        source = jnp.concatenate(
            [
                f1_ref[z + a : z + a + 3, two * pair : two * pair + four, :].reshape(
                    3 * four, columns
                )
                for a in range(2)
            ],
            axis=1,
        )
        part_ref[...] = jnp.dot(wide_ref[...], source, preferred_element_type=jnp.float32)

    def second_layer(z, pair, part_ref):
        for a in range(2):
            first = columns * a
            for r in range(2):
                row = r * channels
                half = (
                    moved_right(part_ref[row : row + channels, first : first + columns])
                    + part_ref[two + row : two + row + channels, first : first + columns]
                    + moved_left(
                        part_ref[four + row : four + row + channels, first : first + columns]
                    )
                )
                value = half_silu(half)
                factors = []
                if z + a == 0:
                    factors.append(low_slice)
                if z + a == slices2 - 1:
                    factors.append(high_slice)
                if pair == 0 and r == 0:
                    factors.append(low_row)
                if pair == 2 and r == 1:
                    factors.append(high_row)
                for factor in factors:
                    value = value * factor
                place = two * pair + r * channels
                f2_ref[z + a, place : place + channels, :] = value.astype(jnp.bfloat16)

    def third_product(z):
        source = jnp.concatenate([f2_ref[z], f2_ref[z + 1]], axis=1)
        score_ref[z // 2] = jnp.dot(last_ref[...], source, preferred_element_type=jnp.float32)

    for z in range(4):
        first_layer(z)
    waiting = None
    parts = (part_a, part_b)
    count = 0
    for z in range(0, slices2, 2):
        for pair in range(3):
            second_product(z, pair, parts[count % 2])
            if pair < 2 and z + 4 + pair < slices1:
                first_layer(z + 4 + pair)
            if waiting is not None:
                second_layer(*waiting)
                if waiting[1] == 2:
                    third_product(waiting[0])
            waiting = (z, pair, parts[count % 2])
            count += 1
    second_layer(*waiting)
    third_product(waiting[0])

    for copy in copies:
        copy.wait()
    size = size_ref[0]
    noise_scale = jnp.sqrt(jnp.full((1, columns), 2.0 * size, jnp.float32))
    for z in range(out_slices):
        taps = []
        for t in range(3):
            total = None
            for d in range(3):
                row, first = (3 * d + t) * 8, columns * ((z + d) % 2)
                piece = score_ref[(z + d) // 2, row : row + 8, first : first + columns]
                total = piece if total is None else total + piece
            taps.append(total)
        score = size * (moved_right(taps[0]) + taps[1] + moved_left(taps[2]))
        for part in range(2):
            out_ref[z, part] = (
                image_ref[z, part]
                + score[part * rows : (part + 1) * rows]
                + noise_scale * noise_ref[z, part]
            )


def stepped_without_data(windows, weights, size, current_image, langevin_noise):
    channels = weights[0].shape[0] // 4
    slices0, columns = windows.shape[1] // 16, windows.shape[-1]
    out_slices = slices0 - 6
    local = (out_slices,) + current_image.shape[2:]
    hbm = pl.BlockSpec(memory_space=pltpu.HBM)
    vmem = pl.BlockSpec(memory_space=pltpu.VMEM)
    return pl.pallas_call(
        network_kernel,
        out_shape=jax.ShapeDtypeStruct(local, jnp.float32),
        in_specs=[vmem] * 4 + [pl.BlockSpec(memory_space=pltpu.SMEM)] + [hbm] * 2,
        out_specs=vmem,
        scratch_shapes=[
            pltpu.VMEM(local, jnp.float32),
            pltpu.VMEM(local, jnp.float32),
            pltpu.VMEM((2, 3, slices0 * 16, columns), jnp.bfloat16),
            pltpu.VMEM((out_slices + 4, 8 * channels, columns), jnp.bfloat16),
            pltpu.VMEM((out_slices + 2, 6 * channels, columns), jnp.bfloat16),
            pltpu.VMEM((6 * channels, 2 * columns), jnp.float32),
            pltpu.VMEM((6 * channels, 2 * columns), jnp.float32),
            pltpu.VMEM((out_slices // 2 + 1, 72, 2 * columns), jnp.float32),
            pltpu.SemaphoreType.DMA((2,)),
        ],
        compiler_params=pltpu.CompilerParams(vmem_limit_bytes=40 * 2**20),
        cost_estimate=pl.CostEstimate(
            flops=10**10, bytes_accessed=2 * 10**6, transcendentals=4 * 10**6
        ),
    )(
        windows,
        *weights,
        size,
        *in_hbm(current_image.reshape(local), langevin_noise.reshape(local)),
    ).reshape(current_image.shape)


def per_device(
    current_image, langevin_noise, step_size, coil_maps, measured_kspace, sample_mask,
    caipi_steps, band_order, weight_in, weight_mid, weight_out,
):
    positions, group_slices, _, row_count, columns = current_image.shape
    local_slices = positions * group_slices
    band, bands = lax.axis_index("band"), lax.axis_size("band")
    own = current_image.astype(jnp.bfloat16).reshape(local_slices, 2 * row_count, columns)
    images = [own] + [
        lax.ppermute(own, "band", [(i, i ^ x) for i in range(bands)]) for x in range(1, 4)
    ]
    turned, stacked, high, low, *weights = preparation(
        coil_maps, measured_kspace, caipi_steps, band_order, weight_in, weight_mid, weight_out
    )

    odd = band % 2 == 1
    under = jnp.where(odd, images[1], images[3])[local_slices - 3 :]
    over = jnp.where(odd, images[3], images[1])[:3]
    under = jnp.where(band == 0, jnp.zeros_like(under), under)
    over = jnp.where(band == bands - 1, jnp.zeros_like(over), over)
    tall = jnp.concatenate([under, own, over], axis=0)
    tall = tall.reshape(-1, 2, row_count, columns)
    below, above = exchanged_rows(tall, 3)
    partial_sums = partial_consistency(
        images, (turned, stacked, high, low), step_size, sample_mask, caipi_steps, band_order
    )
    partial_sums, below, above = lax.optimization_barrier((partial_sums, below, above))
    swapped = lax.all_to_all(partial_sums, "band", split_axis=0, concat_axis=0, tiled=True)
    field = jnp.concatenate([below, tall, above, jnp.zeros_like(above[:, :, :2])], axis=2)
    windows = jnp.stack(
        [field[:, :, 4 * g : 4 * g + 8].reshape(-1, columns) for g in range(2)], axis=0
    )
    base = stepped_without_data(windows, weights, step_size, current_image, langevin_noise)
    pieces = swapped.reshape((-1, positions) + swapped.shape[1:]).astype(jnp.float32)
    return base - jnp.sum(pieces, axis=0)


def solution(mesh):
    band5 = P("band", None, None, "slab", None)
    in_specs = (
        band5,
        band5,
        P(),
        P(None, None, "band", None, "slab", None),
        P(None, "band", None, "slab", None),
        P(), P(), P(), P(), P(), P(),
    )
    return jax.shard_map(
        per_device, mesh=mesh, in_specs=in_specs, out_specs=band5, check_vma=False
    )
```

time: 35.4 us -> 46.9 us (1.32); the launches traced: 35.2 us -> 46.2 us
  local copies, waits for them, and re-layouts: 0.2 us -> 10.5 us
  blocking collectives: 6.84 us -> 0 us
  starting transfers between devices: 8.79 us -> 12 us
  other arithmetic: 2.19 us -> 4.5 us
  Pallas kernels: 16.4 us -> 18.4 us
    unnamed x4 -> x20, local copies, waits for them, and re-layouts: 0.01 us -> 8.33 us
    all_gather x1 -> x0, blocking collectives: 6.84 us -> none  [per_device(): everyone = lax.all_gather(own, 'band', axis=0, tiled=True)]
    ppermute x0 -> x3, starting transfers between devices: none -> 3.15 us  [per_device(): lax.ppermute(own, 'band', [(i, i ^ x) for i in range(bands)])]
    pallas_call x0 -> x1, Pallas kernels: none -> 3.13 us  [preparation(): pl.pallas_call(preparation_kernel, out_shape=(jax.ShapeDtypeStruct((colum...]
    concatenate x0 -> x2, local copies, waits for them, and re-layouts: none -> 2.06 us  [per_device(): tall = jnp.concatenate([under, own, over], axis=0)]
    pallas_call x1, Pallas kernels: 5.74 us -> 4.48 us  [partial_consistency(): pl.pallas_call(consistency_kernel, out_shape=jax.ShapeDtypeStruct((all_po...]
    concatenate x1, other arithmetic: 0.23 us -> 1.12 us  [per_device(): jnp.concatenate([below, tall, above, jnp.zeros_like(above[:, :, :2])], ax...]
    concatenate x0 -> x1, other arithmetic: none -> 0.86 us  [per_device(): tall = jnp.concatenate([under, own, over], axis=0)]
  transfers between devices with their start and end apart: 3 -> 6, of which waited for: 0 -> 0; matrix products, arithmetic and copies ran while one was open for 1% -> 11% of each run, Pallas kernels for 46% -> 40%
where the time goes in v4:
time: 46.9 us; the launch traced here: 46.2 us
  Pallas kernels  18.4 us (39%)
  starting transfers between devices  12 us (26%)
  local copies, waits for them, and re-layouts  10.5 us (22%)
  other arithmetic  4.5 us (10%)
  between operations  0.82 us (2%)
    pallas_call x1, Pallas kernels, stepped_without_data(): pl.pallas_call(network_kernel, out_shape=jax.ShapeDtypeStruct(local, jnp....  10.8 us
    unnamed x20, local copies, waits for them, and re-layouts  8.33 us
    ppermute x2, starting transfers between devices, exchanged_rows(): arrived.append(lax.ppermute(sent, 'slab', route))  5.25 us
    pallas_call x1, Pallas kernels, partial_consistency(): pl.pallas_call(consistency_kernel, out_shape=jax.ShapeDtypeStruct((all_po...  4.48 us
    all_to_all x1, starting transfers between devices, per_device(): lax.all_to_all(partial_sums, 'band', split_axis=0, concat_axis=0, tiled=T...  3.56 us
    ppermute x3, starting transfers between devices, per_device(): lax.ppermute(own, 'band', [(i, i ^ x) for i in range(bands)])  3.15 us
    pallas_call x1, Pallas kernels, preparation(): pl.pallas_call(preparation_kernel, out_shape=(jax.ShapeDtypeStruct((colum...  3.13 us
    concatenate x2, local copies, waits for them, and re-layouts, per_device(): tall = jnp.concatenate([under, own, over], axis=0)  2.06 us
  transfers between devices with their start and end apart: 6, of which 0 were waited for; matrix products, arithmetic and copies ran while one was open for 11% of the time, Pallas kernels for 40%

profile of v4, /device:TPU:0, one launch (start us, length us, event | category | flops | bytes accessed | tf_op | source)
XLA Modules:
  0.0 46.2 jit_solution(6100218148890025820)
XLA Ops:
  0.0 0.9 %convert_element_type.9 = bf16[2,4,2,4,384]{4,3,2,1,0:T(4,128)(2,1)S(1)} convert(f32[2,4,2,4,384]{4,3,2,1,0:T(4,128)} %param.12) | non-fusion elementwise | flops 24576 | bytes 147456 | tf_op jit(solution)/shard_map/convert_element_type | solution.py:561
  0.9 0.0 copy-start.9
  0.9 0.5 %collective-permute-start = (bf16[8,8,384]{2,1,0:T(8,128)(2,1)S(1)}, bf16[8,8,384]{2,1,0:T(8,128)(2,1)S(1)}, u32[]{:S(2)}, u32[]{:S(2)}) collective-permute-start(bf16[8,8,384]{2,1,0:T(8,128)(2,1)S(1)} %reshape.20.own_ref), channel_id=1, source_target_pairs={{0,8},{8,0},{16,24},{24,16},{1,9},{9,1},{17,25},{25,17},{2,10},{10... | collective-permute-start | bytes 147464 | tf_op jit(solution)/shard_map/ppermute | solution.py:563
  1.5 2.6 %collective-permute-start.1 = (bf16[8,8,384]{2,1,0:T(8,128)(2,1)S(1)}, bf16[8,8,384]{2,1,0:T(8,128)(2,1)S(1)}, u32[]{:S(2)}, u32[]{:S(2)}) collective-permute-start(bf16[8,8,384]{2,1,0:T(8,128)(2,1)S(1)} %reshape.20.own_ref), channel_id=1, source_target_pairs={{0,16},{8,24},{16,0},{24,8},{1,17},{9,25},{17,1},{25,9},{2,18},{10... | collective-permute-start | bytes 147464 | tf_op jit(solution)/shard_map/ppermute | solution.py:563
  4.0 0.1 collective-permute-start.2
  4.1 0.0 copy-done.9
  4.1 0.0 copy-start
  4.1 0.9 %copy-done = f32[80,384]{1,0:T(8,128)S(1)} copy-done((f32[80,384]{1,0:T(8,128)S(1)}, f32[80,384]{1,0:T(8,128)}, u32[]{:S(2)}) %copy-start) | copy-done | bytes 122904
  5.0 3.1 %shard_map.118 = (f32[3,8,4,8,8,128]{5,4,3,2,1,0:T(8,128)S(1)}, f32[4,8,8,384]{3,2,1,0:T(8,128)S(1)}, bf16[384,768]{1,0:T(8,128)(2,1)S(1)}, bf16[384,768]{1,0:T(...) custom-call(s32[8]{0:T(128)} %steps_hbm.3, s32[8]{0:T(128)} %order_hbm.3, ...), custom_call_target="tpu_custom_call" | custom-call | flops 4000000000 | bytes 4000000 | tf_op jit(solution)/shard_map/pallas_call | solution.py:223
  8.1 0.0 copy-start.1
  8.2 0.8 %copy-done.1 = bf16[384,768]{1,0:T(8,128)(2,1)} copy-done((bf16[384,768]{1,0:T(8,128)(2,1)}, bf16[384,768]{1,0:T(8,128)(2,1)S(1)}, u32[]{:S(2)}) %copy-start.1) | copy-done | bytes 589848
  9.0 0.0 copy-start.3
  9.0 0.8 %copy-done.3 = bf16[384,768]{1,0:T(8,128)(2,1)} copy-done((bf16[384,768]{1,0:T(8,128)(2,1)}, bf16[384,768]{1,0:T(8,128)(2,1)S(1)}, u32[]{:S(2)}) %copy-start.3) | copy-done | bytes 589848
  9.8 0.0 copy-start.5
  9.8 0.8 %copy-done.5 = f32[4,8,8,384]{3,2,1,0:T(8,128)} copy-done((f32[4,8,8,384]{3,2,1,0:T(8,128)}, f32[4,8,8,384]{3,2,1,0:T(8,128)S(1)}, u32[]{:S(2)}) %copy-start.5) | copy-done | bytes 393240
  10.6 0.0 copy-start.7
  10.6 0.8 %copy-done.7 = bf16[384,768]{1,0:T(8,128)(2,1)} copy-done((bf16[384,768]{1,0:T(8,128)(2,1)}, bf16[384,768]{1,0:T(8,128)(2,1)S(1)}, u32[]{:S(2)}) %copy-start.7) | copy-done | bytes 589848
  11.4 0.1 pad_slice_fusion
  12.1 0.0 collective-permute-done.one_ref
  12.1 0.0 collective-permute-done.2.three_ref
  12.2 0.6 %fusion.2 = (bf16[3,8,384]{2,1,0:T(8,128)(2,1)}, bf16[3,8,384]{2,1,0:T(8,128)(2,1)}) fusion(bf16[8,8,384]{2,1,0:T(8,128)(2,1)S(1)} %collective-permute-done.2.three_ref, bf16[8,8,384]{2,1,0:T(8,128)(2,1)S(1)} %collective-permute-done.one_ref, pred[]{:T(512)S(6)} %eq.17, pred[]{:T(512)S(6)} %eq.16, pred[]{:T(512)S(6)} %eq.18), kind=kLoop, calls=%fused_computation.18 | loop fusion | flops 36864 | bytes 110595 | tf_op jit(solution)/shard_map/jit(_where)/select_n | solution.py:572
  12.8 0.7 %concatenate.19 = bf16[3,2,4,384]{3,2,1,0:T(4,128)(2,1)S(1)} reshape(bf16[3,8,384]{2,1,0:T(8,128)(2,1)} %get-tuple-element.30) | data formatting | bytes 36864 | tf_op jit(solution)/shard_map/concatenate | solution.py:574
  13.5 1.3 %concatenate.17 = bf16[3,2,4,384]{3,2,1,0:T(4,128)(2,1)} reshape(bf16[3,8,384]{2,1,0:T(8,128)(2,1)} %get-tuple-element.29) | data formatting | bytes 36864 | tf_op jit(solution)/shard_map/concatenate | solution.py:574
  14.8 0.9 %pad_maximum_fusion.8 = bf16[14,2,4,384]{3,2,1,0:T(4,128)(2,1)S(1)} fusion(bf16[3,2,4,384]{3,2,1,0:T(4,128)(2,1)S(1)} %concatenate.19, bf16[8,2,4,384]{3,2,1,0:T(4,128)(2,1)} %bitcast.13, bf16[3,2,4,384]{3,2,1,0:T(4,128)(2,1)} %concatenate.17), kind=kLoop, calls=%fused_computation.10 | loop fusion | flops 86016 | bytes 172032 | tf_op jit(solution)/shard_map/concatenate | solution.py:574
  15.7 0.1 broadcast_select_fusion.2
  15.8 0.7 %collective-permute-start.4 = (bf16[14,2,3,384]{3,2,1,0:T(4,128)(2,1)S(1)}, bf16[14,2,3,384]{3,2,1,0:T(4,128)(2,1)S(1)}, u32[]{:S(2)}, u32[]{:S(2)}) collective-permute-start(bf16[14,2,3,384]{3,2,1,0:T(4,128)(2,1)S(1)} %get-tuple-element.31), channel_id=1, source_target_pairs={{1,2},{2,1},{3,4},{4,3},{5,6},{6,5},{9,10},{10,9},{11,12},{12,11},... | collective-permute-start | bytes 193544 | tf_op jit(solution)/shard_map/ppermute | solution.py:23
  16.5 4.6 %collective-permute-start.3 = (bf16[14,2,3,384]{3,2,1,0:T(4,128)(2,1)S(1)}, bf16[14,2,3,384]{3,2,1,0:T(4,128)(2,1)S(1)}, u32[]{:S(2)}, u32[]{:S(2)}) collective-permute-start(bf16[14,2,3,384]{3,2,1,0:T(4,128)(2,1)S(1)} %get-tuple-element.32), channel_id=1, source_target_pairs={{0,1},{1,0},{2,3},{3,2},{4,5},{5,4},{6,7},{7,6},{8,9},{9,8},{10,11... | collective-permute-start | bytes 193544 | tf_op jit(solution)/shard_map/ppermute | solution.py:23
  21.1 0.0 collective-permute-done.1.two_ref
  21.1 0.0 copy-start.2
  21.1 1.1 %copy-done.2 = bf16[384,768]{1,0:T(8,128)(2,1)S(1)} copy-done((bf16[384,768]{1,0:T(8,128)(2,1)S(1)}, bf16[384,768]{1,0:T(8,128)(2,1)}, u32[]{:S(2)}) %copy-start.2) | copy-done | bytes 589848
  22.1 0.0 copy-start.4
  22.2 1.1 %copy-done.4 = bf16[384,768]{1,0:T(8,128)(2,1)S(1)} copy-done((bf16[384,768]{1,0:T(8,128)(2,1)S(1)}, bf16[384,768]{1,0:T(8,128)(2,1)}, u32[]{:S(2)}) %copy-start.4) | copy-done | bytes 589848
  23.2 0.0 copy-start.6
  23.2 1.0 %copy-done.6 = f32[4,8,8,384]{3,2,1,0:T(8,128)S(1)} copy-done((f32[4,8,8,384]{3,2,1,0:T(8,128)S(1)}, f32[4,8,8,384]{3,2,1,0:T(8,128)}, u32[]{:S(2)}) %copy-start.6) | copy-done | bytes 393240
  24.2 4.5 %shard_map.119 = bf16[8,4,2,4,384]{4,3,2,1,0:T(4,128)(2,1)} custom-call(bf16[8,8,384]{2,1,0:T(8,128)(2,1)S(1)} %reshape.20.own_ref, bf16[8,8,384]{2,1,0:T(8,128)(2,1)S(1)} %collective-permute-done.one_ref, bf16[8,8,384]{2,1,0:T(8,128)(2,1)S(1)} %collective-permute-done.1.two_ref, bf16[8,8,384]{2,1,0:T(8,128)(2,1)S(1)} %collective-permute-done.2.three_ref, ...), custom_call_target="tpu_custom_call" | custom-call | flops 4000000000 | bytes 4000000 | tf_op jit(solution)/shard_map/pallas_call | solution.py:355
  28.7 0.0 collective-permute-done.4
  28.7 0.0 collective-permute-done.3
  28.7 0.1 broadcast_select_fusion
  28.8 3.6 %all-to-all-start = ((bf16[8,4,2,4,384]{4,3,2,1,0:T(4,128)(2,1)}), bf16[8,4,2,4,384]{4,3,2,1,0:T(4,128)(2,1)S(1)}, u32[]{:S(2)}, u32[]{:S(2)}) async-start(bf16[8,4,2,4,384]{4,3,2,1,0:T(4,128)(2,1)} %shard_map.119), calls=%async_computation | async-start | bytes 393216 | tf_op jit(solution)/shard_map/all_to_all | solution.py:581
  32.4 1.1 %pad_maximum_fusion.4 = (bf16[14,2,8,384]{3,2,1,0:T(8,128)(2,1)S(1)}, bf16[14,2,8,384]{3,2,1,0:T(8,128)(2,1)S(1)}) fusion(bf16[14,2,3,384]{3,2,1,0:T(4,128)(2,1)S(1)} %get-tuple-element.20, bf16[14,2,3,384]{3,2,1,0:T(4,128)(2,1)S(1)} %get-tuple-element.19, bf16[3,2,4,384]{3,2,1,0:T(4,128)(2,1)S(1)} %concatenate.19, bf16[8,2,4,384]{3,2,1,0:T(4,128)(2,1)} %bitcast.14, ...), kind=kLoop, calls=%fused_computation.6 | loop fusion | flops 1720320 | bytes 559120 | tf_op jit(solution)/shard_map/concatenate | solution.py:582
  33.5 0.0 copy-start.8
  33.5 1.1 %copy-done.8 = bf16[384,768]{1,0:T(8,128)(2,1)S(1)} copy-done((bf16[384,768]{1,0:T(8,128)(2,1)S(1)}, bf16[384,768]{1,0:T(8,128)(2,1)}, u32[]{:S(2)}) %copy-start.8) | copy-done | bytes 589848
  34.6 10.8 %shard_map.120 = f32[8,2,4,384]{3,2,1,0:T(4,128)S(1)} custom-call(bf16[2,224,384]{2,1,0:T(8,128)(2,1)S(1)} %pad_maximum_fusion.window_ref, bf16[256,144]{1,0:T(8,128)(2,1)S(1)} %get-tuple-element.21.first_ref, bf16[384,768]{1,0:T(8,128)(2,1)S(1)} %copy-done.8, bf16[72,384]{1,0:T(8,128)(2,1)S(1)} %get-tuple-element.23.last_ref, f32[1]{0:T(128)S(6)} %copy.13.size_ref, ...), custom_call_target="tpu_custom_call" | custom-call | flops 10000000000 | bytes 2000000 | tf_op jit(solution)/shard_map/pallas_call | solution.py:526
  45.4 0.0 all-to-all-done
  45.4 0.1 convert_reduce_fusion
  45.5 0.7 %sub.3 = f32[2,4,2,4,384]{4,3,2,1,0:T(4,128)} subtract(f32[2,4,2,4,384]{4,3,2,1,0:T(4,128)S(1)} %bitcast.11, f32[2,4,2,4,384]{4,3,2,1,0:T(4,128)S(1)} %convert_reduce_fusion) | non-fusion elementwise | flops 24576 | bytes 294912 | tf_op jit(solution)/shard_map/sub | solution.py:588
  (3 shorter events, 0.1 us)
Async XLA Ops:
  0.9 3.2 %copy-start.9 = (bf16[2,4,2,4,384]{4,3,2,1,0:T(4,128)(2,1)}, bf16[2,4,2,4,384]{4,3,2,1,0:T(4,128)(2,1)S(1)}, u32[]{:S(2)}) copy-start(bf16[2,4,2,4,384]{4,3,2,1,0:T(4,128)(2,1)S(1)} %convert_element_type.9) | copy-start | bytes 147460
  0.9 11.2 %collective-permute-start = (bf16[8,8,384]{2,1,0:T(8,128)(2,1)S(1)}, bf16[8,8,384]{2,1,0:T(8,128)(2,1)S(1)}, u32[]{:S(2)}, u32[]{:S(2)}) collective-permute-start(bf16[8,8,384]{2,1,0:T(8,128)(2,1)S(1)} %reshape.20.own_ref), channel_id=1, source_target_pairs={{0,8},{8,0},{16,24},{24,16},{1,9},{9,1},{17,25},{25,17},{2,10},{10... | collective-permute-start | bytes 147464 | tf_op jit(solution)/shard_map/ppermute | solution.py:563
  1.5 19.6 %collective-permute-start.1 = (bf16[8,8,384]{2,1,0:T(8,128)(2,1)S(1)}, bf16[8,8,384]{2,1,0:T(8,128)(2,1)S(1)}, u32[]{:S(2)}, u32[]{:S(2)}) collective-permute-start(bf16[8,8,384]{2,1,0:T(8,128)(2,1)S(1)} %reshape.20.own_ref), channel_id=1, source_target_pairs={{0,16},{8,24},{16,0},{24,8},{1,17},{9,25},{17,1},{25,9},{2,18},{10... | collective-permute-start | bytes 147464 | tf_op jit(solution)/shard_map/ppermute | solution.py:563
  4.0 8.1 %collective-permute-start.2 = (bf16[8,8,384]{2,1,0:T(8,128)(2,1)S(1)}, bf16[8,8,384]{2,1,0:T(8,128)(2,1)S(1)}, u32[]{:S(2)}, u32[]{:S(2)}) collective-permute-start(bf16[8,8,384]{2,1,0:T(8,128)(2,1)S(1)} %reshape.20.own_ref), channel_id=1, source_target_pairs={{0,24},{8,16},{16,8},{24,0},{1,25},{9,17},{17,9},{25,1},{2,26},{10... | collective-permute-start | bytes 147464 | tf_op jit(solution)/shard_map/ppermute | solution.py:563
  4.1 0.9 %copy-start = (f32[80,384]{1,0:T(8,128)S(1)}, f32[80,384]{1,0:T(8,128)}, u32[]{:S(2)}) copy-start(f32[80,384]{1,0:T(8,128)} %constant.36.clone.factors_hbm) | copy-start | bytes 368644
  8.1 0.8 %copy-start.1 = (bf16[384,768]{1,0:T(8,128)(2,1)}, bf16[384,768]{1,0:T(8,128)(2,1)S(1)}, u32[]{:S(2)}) copy-start(bf16[384,768]{1,0:T(8,128)(2,1)S(1)} %get-tuple-element.17.high_ref) | copy-start | bytes 1769476
  9.0 0.8 %copy-start.3 = (bf16[384,768]{1,0:T(8,128)(2,1)}, bf16[384,768]{1,0:T(8,128)(2,1)S(1)}, u32[]{:S(2)}) copy-start(bf16[384,768]{1,0:T(8,128)(2,1)S(1)} %get-tuple-element.18.low_ref) | copy-start | bytes 1769476
  9.8 0.8 %copy-start.5 = (f32[4,8,8,384]{3,2,1,0:T(8,128)}, f32[4,8,8,384]{3,2,1,0:T(8,128)S(1)}, u32[]{:S(2)}) copy-start(f32[4,8,8,384]{3,2,1,0:T(8,128)S(1)} %get-tuple-element.16.stacked_ref) | copy-start | bytes 1179652
  10.6 0.8 %copy-start.7 = (bf16[384,768]{1,0:T(8,128)(2,1)}, bf16[384,768]{1,0:T(8,128)(2,1)S(1)}, u32[]{:S(2)}) copy-start(bf16[384,768]{1,0:T(8,128)(2,1)S(1)} %get-tuple-element.22.wide_ref) | copy-start | bytes 1769476
  15.8 12.9 %collective-permute-start.4 = (bf16[14,2,3,384]{3,2,1,0:T(4,128)(2,1)S(1)}, bf16[14,2,3,384]{3,2,1,0:T(4,128)(2,1)S(1)}, u32[]{:S(2)}, u32[]{:S(2)}) collective-permute-start(bf16[14,2,3,384]{3,2,1,0:T(4,128)(2,1)S(1)} %get-tuple-element.31), channel_id=1, source_target_pairs={{1,2},{2,1},{3,4},{4,3},{5,6},{6,5},{9,10},{10,9},{11,12},{12,11},... | collective-permute-start | bytes 193544 | tf_op jit(solution)/shard_map/ppermute | solution.py:23
  16.5 12.2 %collective-permute-start.3 = (bf16[14,2,3,384]{3,2,1,0:T(4,128)(2,1)S(1)}, bf16[14,2,3,384]{3,2,1,0:T(4,128)(2,1)S(1)}, u32[]{:S(2)}, u32[]{:S(2)}) collective-permute-start(bf16[14,2,3,384]{3,2,1,0:T(4,128)(2,1)S(1)} %get-tuple-element.32), channel_id=1, source_target_pairs={{0,1},{1,0},{2,3},{3,2},{4,5},{5,4},{6,7},{7,6},{8,9},{9,8},{10,11... | collective-permute-start | bytes 193544 | tf_op jit(solution)/shard_map/ppermute | solution.py:23
  21.1 1.1 %copy-start.2 = (bf16[384,768]{1,0:T(8,128)(2,1)S(1)}, bf16[384,768]{1,0:T(8,128)(2,1)}, u32[]{:S(2)}) copy-start(bf16[384,768]{1,0:T(8,128)(2,1)} %copy-done.1) | copy-start | bytes 1769476
  22.1 1.1 %copy-start.4 = (bf16[384,768]{1,0:T(8,128)(2,1)S(1)}, bf16[384,768]{1,0:T(8,128)(2,1)}, u32[]{:S(2)}) copy-start(bf16[384,768]{1,0:T(8,128)(2,1)} %copy-done.3) | copy-start | bytes 1769476
  23.2 1.0 %copy-start.6 = (f32[4,8,8,384]{3,2,1,0:T(8,128)S(1)}, f32[4,8,8,384]{3,2,1,0:T(8,128)}, u32[]{:S(2)}) copy-start(f32[4,8,8,384]{3,2,1,0:T(8,128)} %copy-done.5) | copy-start | bytes 1179652
  28.8 16.6 %all-to-all-start = ((bf16[8,4,2,4,384]{4,3,2,1,0:T(4,128)(2,1)}), bf16[8,4,2,4,384]{4,3,2,1,0:T(4,128)(2,1)S(1)}, u32[]{:S(2)}, u32[]{:S(2)}) async-start(bf16[8,4,2,4,384]{4,3,2,1,0:T(4,128)(2,1)} %shard_map.119), calls=%async_computation | async-start | bytes 393216 | tf_op jit(solution)/shard_map/all_to_all | solution.py:581
  33.5 1.1 %copy-start.8 = (bf16[384,768]{1,0:T(8,128)(2,1)S(1)}, bf16[384,768]{1,0:T(8,128)(2,1)}, u32[]{:S(2)}) copy-start(bf16[384,768]{1,0:T(8,128)(2,1)} %copy-done.7) | copy-start | bytes 1769476

commit v5 on v4

--- a/solution.py
+++ b/solution.py
@@ -3,7 +3,6 @@
 
 import jax
 import jax.numpy as jnp
-import numpy as np
 from jax import lax
 from jax.experimental import pallas as pl
 from jax.experimental.pallas import tpu as pltpu
@@ -30,15 +29,21 @@
     return [pltpu.with_memory_space_constraint(array, pltpu.HBM) for array in arrays]
 
 
-def dft_factors(columns):
+def fill_factors(factors_ref):
+    rows, columns = factors_ref.shape
     near = 16
-    index = np.arange(columns)
-    pieces = []
-    for rows in (near * np.arange(columns // near), np.arange(near)):
-        phase = (np.outer(rows, index) % columns) * (2.0 * math.pi / columns)
-        pieces += [np.cos(phase), np.sin(phase)]
-    far = np.concatenate(pieces[:2], axis=0) / math.sqrt(columns)
-    return np.concatenate([far] + pieces[2:], axis=0).astype(np.float32)
+    count = columns // near
+    half = count + near
+    row = lax.broadcasted_iota(jnp.int32, (half, columns), 0)
+    row = jnp.where(row < count, near * row, row - count).astype(jnp.float32)
+    phase = row * lax.broadcasted_iota(jnp.int32, (half, columns), 1).astype(jnp.float32)
+    phase = phase - columns * jnp.floor(phase * (1.0 / columns))
+    phase = phase * (2.0 * math.pi / columns)
+    scale = 1.0 / math.sqrt(columns)
+    for begin, wave in ((0, jnp.cos(phase)), (count, jnp.sin(phase))):
+        factors_ref[begin : begin + count, :] = scale * wave[:count]
+        begin = 2 * count + (0 if begin == 0 else near)
+        factors_ref[begin : begin + near, :] = wave[count:]
 
 
 def build_tables(factors_ref, high_ref, low_ref):
@@ -166,120 +171,147 @@
 
 
 def preparation_kernel(
-    steps_hbm, order_hbm, coil_hbm, kspace_hbm, factors_hbm, first_hbm, mid_hbm, last_hbm,
-    turned_ref, stacked_ref, high_ref, low_ref, first_ref, wide_ref, last_ref,
+    size_ref, steps_hbm, order_hbm, coil_hbm, kspace_hbm, first_hbm, mid_hbm, last_hbm,
+    turned_ref, scalars_ref,
+    stacked_out, high_out, low_out, first_out, wide_out, last_out,
     steps_ref, order_ref, coil_ref, kspace_ref, factors_ref, first_raw, mid_raw, last_raw,
-    first_sum, last_sum, sems, coil_sems,
+    first_sum, last_sum, stacked_ref, high_ref, low_ref, first_ref, wide_ref, last_ref,
+    sems, coil_sems, out_sems,
 ):
     all_positions, slices, coils, _, rows, columns = coil_ref.shape
     unit = columns // 8
+    block = coils * 2 * rows
     pairs = (
         (first_hbm, first_raw), (mid_hbm, mid_raw), (last_hbm, last_raw),
-        (factors_hbm, factors_ref), (steps_hbm, steps_ref), (order_hbm, order_ref),
-        (kspace_hbm, kspace_ref),
+        (steps_hbm, steps_ref), (order_hbm, order_ref), (kspace_hbm, kspace_ref),
     )
     copies = [pltpu.make_async_copy(src, dst, sems.at[i]) for i, (src, dst) in enumerate(pairs)]
     coil_copies = [
         pltpu.make_async_copy(coil_hbm.at[g], coil_ref.at[g], coil_sems.at[g])
         for g in range(all_positions)
     ]
-    for copy in copies[:6] + coil_copies + copies[6:]:
+    results = (
+        (first_ref, first_out), (wide_ref, wide_out), (last_ref, last_out),
+        (high_ref, high_out), (low_ref, low_out), (stacked_ref, stacked_out),
+    )
+    returns = [
+        pltpu.make_async_copy(src, dst, out_sems.at[i]) for i, (src, dst) in enumerate(results)
+    ]
+    for copy in copies[:5] + coil_copies + copies[5:]:
         copy.start()
+    fill_factors(factors_ref)
+    build_tables(factors_ref, high_ref, low_ref)
     for copy in copies[:3]:
         copy.wait()
     fill_weights(
         first_raw, mid_raw, last_raw, first_sum, last_sum, first_ref, wide_ref, last_ref
     )
-    copies[3].wait()
-    build_tables(factors_ref, high_ref, low_ref)
-    for copy in copies[4:6]:
+    for copy in returns[:5]:
+        copy.start()
+    for copy in copies[3:5]:
         copy.wait()
     for g in range(all_positions):
         shift = steps_ref[order_ref[g]] * unit
+        scalars_ref[g : g + 1, :] = jnp.full((1, 128), shift, jnp.int32).astype(jnp.float32)
         coil_copies[g].wait()
         for s in range(slices):
 
             def store_coil(j, value, s=s, g=g):
-                turned_ref[j, g, s] = value
+                turned_ref[j, g, s] = value.reshape(block, 128).astype(jnp.bfloat16)
 
             turned_tiles(stacked_parts(coil_ref[g, s].astype(jnp.float32)), shift, store_coil)
-    copies[6].wait()
+    scalars_ref[all_positions:, :] = jnp.full(
+        (scalars_ref.shape[0] - all_positions, 128), size_ref[0], jnp.float32
+    )
+    copies[5].wait()
     for s in range(slices):
         stacked_ref[s] = stacked_parts(kspace_ref[s])
+    returns[5].start()
+    for copy in returns:
+        copy.wait()
 
 
 def preparation(
-    coil_maps, measured_kspace, caipi_steps, band_order, weight_in, weight_mid, weight_out
+    step_size, coil_maps, measured_kspace, caipi_steps, band_order, weight_in, weight_mid, weight_out
 ):
     all_positions, slices, coils, _, rows, columns = coil_maps.shape
     channels = weight_mid.shape[0]
-    factors = jnp.asarray(dft_factors(columns))
     first = jnp.transpose(weight_in, (2, 3, 4, 1, 0))
     mid = jnp.transpose(weight_mid, (2, 3, 4, 0, 1))
     last = jnp.transpose(weight_out, (2, 3, 4, 0, 1))
     f32, bf16 = jnp.float32, jnp.bfloat16
     hbm = pl.BlockSpec(memory_space=pltpu.HBM)
     vmem = pl.BlockSpec(memory_space=pltpu.VMEM)
+    results = (
+        ((slices, coils, 2 * rows, columns), f32),
+        ((columns, 2 * columns), bf16),
+        ((columns, 2 * columns), bf16),
+        ((4 * channels, 144), bf16),
+        ((6 * channels, 12 * channels), bf16),
+        ((72, 6 * channels), bf16),
+    )
+    turned_shape = (columns // 128, all_positions, slices, coils * 2 * rows, 128)
     return pl.pallas_call(
         preparation_kernel,
         out_shape=(
-            jax.ShapeDtypeStruct((columns // 128, all_positions, slices, coils, 2 * rows, 128), f32),
-            jax.ShapeDtypeStruct((slices, coils, 2 * rows, columns), f32),
-            jax.ShapeDtypeStruct((columns, 2 * columns), bf16),
-            jax.ShapeDtypeStruct((columns, 2 * columns), bf16),
-            jax.ShapeDtypeStruct((4 * channels, 144), bf16),
-            jax.ShapeDtypeStruct((6 * channels, 12 * channels), bf16),
-            jax.ShapeDtypeStruct((72, 6 * channels), bf16),
-        ),
-        in_specs=[hbm] * 8,
-        out_specs=(vmem,) * 7,
+            jax.ShapeDtypeStruct(turned_shape, bf16),
+            jax.ShapeDtypeStruct((2 * all_positions, 128), f32),
+        )
+        + tuple(pltpu.HBM(shape, dtype) for shape, dtype in results),
+        in_specs=[pl.BlockSpec(memory_space=pltpu.SMEM)] + [hbm] * 7,
+        out_specs=(vmem,) * 2 + (hbm,) * 6,
         scratch_shapes=[
             pltpu.SMEM(caipi_steps.shape, jnp.int32),
             pltpu.SMEM(band_order.shape, jnp.int32),
             pltpu.VMEM(coil_maps.shape, bf16),
             pltpu.VMEM(measured_kspace.shape, f32),
-            pltpu.VMEM(factors.shape, f32),
+            pltpu.VMEM((2 * (columns // 16 + 16), columns), f32),
             pltpu.VMEM(first.shape, bf16),
             pltpu.VMEM(mid.shape, bf16),
             pltpu.VMEM(last.shape, bf16),
             pltpu.VMEM((256, 4 * channels), f32),
             pltpu.VMEM((72, 6 * channels), f32),
-            pltpu.SemaphoreType.DMA((7,)),
+        ]
+        + [pltpu.VMEM(shape, dtype) for shape, dtype in results]
+        + [
+            pltpu.SemaphoreType.DMA((6,)),
             pltpu.SemaphoreType.DMA((all_positions,)),
+            pltpu.SemaphoreType.DMA((6,)),
         ],
         compiler_params=pltpu.CompilerParams(vmem_limit_bytes=40 * 2**20),
         cost_estimate=pl.CostEstimate(
             flops=4 * 10**9, bytes_accessed=4 * 10**6, transcendentals=0
         ),
     )(
+        step_size,
         *in_hbm(caipi_steps, band_order, coil_maps, measured_kspace),
-        factors,
         *in_hbm(first, mid, last),
     )
 
 
 def consistency_kernel(
-    own_ref, one_ref, two_ref, three_ref, turned_ref, stacked_ref, high_ref, low_ref,
-    size_ref, steps_hbm, order_hbm, mask_hbm,
+    own_ref, one_ref, two_ref, three_ref, turned_ref, scalars_ref,
+    stacked_hbm, high_hbm, low_hbm, mask_hbm,
     out_ref,
-    steps_ref, order_ref, mask_ref, real_ref, imag_ref, field_ref, swap_ref, sum_ref,
+    stacked_ref, high_ref, low_ref, mask_ref, real_ref, imag_ref, field_ref, swap_ref, sum_ref,
     sems,
 ):
-    tiles, all_positions, slices, coils, doubled, _ = turned_ref.shape
-    rows, columns = doubled // 2, stacked_ref.shape[-1]
-    positions = all_positions // 4
-    unit = columns // 8
+    tiles, all_positions, slices, _, _ = turned_ref.shape
+    _, coils, doubled, columns = stacked_ref.shape
+    rows, positions = doubled // 2, all_positions // 4
     pairs = (
-        (steps_hbm, steps_ref), (order_hbm, order_ref), (mask_hbm, mask_ref),
+        (high_hbm, high_ref), (low_hbm, low_ref), (stacked_hbm, stacked_ref), (mask_hbm, mask_ref),
     )
     copies = [pltpu.make_async_copy(src, dst, sems.at[i]) for i, (src, dst) in enumerate(pairs)]
     for copy in copies:
         copy.start()
-    for copy in copies:
-        copy.wait()
+    size = scalars_ref[all_positions : all_positions + 1, :]
 
     def shift_of(g):
-        return steps_ref[order_ref[g]] * unit
+        return jnp.max(scalars_ref[pl.ds(g, 1), :]).astype(jnp.int32)
+
+    def coil_of(j, g, s):
+        return turned_ref[j, g, s].astype(jnp.float32).reshape(coils, doubled, 128)
 
     for x, ref in enumerate((own_ref, one_ref, two_ref, three_ref)):
         for p in range(positions):
@@ -300,7 +332,7 @@
             with_real = jnp.zeros((coils, 2 * rows, 128), jnp.float32)
             with_imag = jnp.zeros((coils, 2 * rows, 128), jnp.float32)
             for g in range(all_positions):
-                coil = turned_ref[j, g, s]
+                coil = coil_of(j, g, s)
                 with_real += coil * real_ref[j, g, s]
                 with_imag += coil * imag_ref[j, g, s]
             total = with_real + signed_swap(with_imag, -1.0, 1.0)
@@ -308,6 +340,8 @@
                 block, 128
             )
 
+    for copy in copies:
+        copy.wait()
     product = table_product(field_ref[...], high_ref, low_ref)
     grouped = (slices, coils, 2 * rows, columns)
     with_cos = product[:, :columns].reshape(grouped)
@@ -322,14 +356,13 @@
     field_ref[...] = back.reshape(slices * block, columns)
     swap_ref[...] = halves_swapped(back).reshape(slices * block, columns)
 
-    size = size_ref[0]
     for j in range(tiles):
         for s in range(slices):
             place = (slice(s * block, (s + 1) * block), slice(128 * j, 128 * (j + 1)))
             field = field_ref[place].reshape(coils, 2 * rows, 128)
             swapped = swap_ref[place].reshape(coils, 2 * rows, 128)
             for g in range(all_positions):
-                coil = turned_ref[j, g, s]
+                coil = coil_of(j, g, s)
                 straight = jnp.sum(coil * field, axis=0)
                 crossed = jnp.sum(coil * swapped, axis=0)
                 straight = straight + halves_swapped(straight)
@@ -340,52 +373,50 @@
 
     for g in range(all_positions):
         back_shift = lax.rem(columns - shift_of(g), columns)
-        turned = pltpu.roll(sum_ref[g], back_shift, 2).astype(jnp.bfloat16)
-        out_ref[g, :, 0] = turned[:, :rows]
-        out_ref[g, :, 1] = turned[:, rows:]
-
-
-def partial_consistency(images, prepared, size, sample_mask, caipi_steps, band_order):
-    tiles, all_positions, slices, coils, doubled, _ = prepared[0].shape
-    columns = sample_mask.shape[-1]
+        out_ref[g] = pltpu.roll(sum_ref[g], back_shift, 2).astype(jnp.bfloat16)
+
+
+def partial_consistency(images, prepared, sample_mask):
+    tiles, all_positions, slices, _, _ = prepared[0].shape
+    _, coils, doubled, columns = prepared[2].shape
     total = slices * coils * doubled
     hbm = pl.BlockSpec(memory_space=pltpu.HBM)
     vmem = pl.BlockSpec(memory_space=pltpu.VMEM)
     image_shape = (tiles, all_positions, slices, doubled, 128)
     return pl.pallas_call(
         consistency_kernel,
-        out_shape=jax.ShapeDtypeStruct(
-            (all_positions, slices, 2, doubled // 2, columns), jnp.bfloat16
-        ),
-        in_specs=[vmem] * 8 + [pl.BlockSpec(memory_space=pltpu.SMEM)] + [hbm] * 3,
+        out_shape=jax.ShapeDtypeStruct((all_positions, slices, doubled, columns), jnp.bfloat16),
+        in_specs=[vmem] * 6 + [hbm] * 4,
         out_specs=vmem,
         scratch_shapes=[
-            pltpu.SMEM(caipi_steps.shape, jnp.int32),
-            pltpu.SMEM(band_order.shape, jnp.int32),
+            pltpu.VMEM((slices, coils, doubled, columns), jnp.float32),
+            pltpu.VMEM((columns, 2 * columns), jnp.bfloat16),
+            pltpu.VMEM((columns, 2 * columns), jnp.bfloat16),
             pltpu.VMEM(sample_mask.shape, jnp.int32),
             pltpu.VMEM(image_shape, jnp.float32),
             pltpu.VMEM(image_shape, jnp.float32),
             pltpu.VMEM((total, columns), jnp.float32),
             pltpu.VMEM((total, columns), jnp.float32),
             pltpu.VMEM((all_positions, slices, doubled, columns), jnp.float32),
-            pltpu.SemaphoreType.DMA((3,)),
+            pltpu.SemaphoreType.DMA((4,)),
         ],
         compiler_params=pltpu.CompilerParams(vmem_limit_bytes=40 * 2**20),
         cost_estimate=pl.CostEstimate(
             flops=4 * 10**9, bytes_accessed=4 * 10**6, transcendentals=0
         ),
-    )(*images, *prepared, size, *in_hbm(caipi_steps, band_order, sample_mask))
+    )(*images, *prepared[:2], *in_hbm(*prepared[2:], sample_mask))
 
 
 def network_kernel(
-    window_ref, first_ref, wide_ref, last_ref, size_ref, image_hbm, noise_hbm,
+    window_ref, scalars_ref, first_hbm, wide_hbm, last_hbm, image_hbm, noise_hbm,
     out_ref,
-    image_ref, noise_ref, taps_ref, f1_ref, f2_ref, part_a, part_b, score_ref, sems,
+    first_ref, wide_ref, last_ref, image_ref, noise_ref, taps_ref, f1_ref, f2_ref, part_a, part_b, score_ref, sems,
 ):
     channels = first_ref.shape[0] // 4
     out_slices, _, rows, columns = out_ref.shape
     slices1, slices2 = out_slices + 4, out_slices + 2
     pairs = (
+        (first_hbm, first_ref), (wide_hbm, wide_ref), (last_hbm, last_ref),
         (image_hbm, image_ref), (noise_hbm, noise_ref),
     )
     copies = [pltpu.make_async_copy(src, dst, sems.at[i]) for i, (src, dst) in enumerate(pairs)]
@@ -405,6 +436,9 @@
         taps_ref[g, 0] = moved_right(base).astype(jnp.bfloat16)
         taps_ref[g, 1] = window_ref[g]
         taps_ref[g, 2] = moved_left(base).astype(jnp.bfloat16)
+
+    for copy in copies[:3]:
+        copy.wait()
 
     def first_layer(z):
         source = jnp.concatenate(
@@ -494,10 +528,11 @@
     second_layer(*waiting)
     third_product(waiting[0])
 
-    for copy in copies:
+    for copy in copies[3:]:
         copy.wait()
-    size = size_ref[0]
-    noise_scale = jnp.sqrt(jnp.full((1, columns), 2.0 * size, jnp.float32))
+    size = scalars_ref[scalars_ref.shape[0] - 1 :, :]
+    size = jnp.concatenate([size] * (columns // 128), axis=1)
+    noise_scale = jnp.sqrt(2.0 * size)
     for z in range(out_slices):
         taps = []
         for t in range(3):
@@ -516,7 +551,7 @@
             )
 
 
-def stepped_without_data(windows, weights, size, current_image, langevin_noise):
+def stepped_without_data(windows, scalars, weights, current_image, langevin_noise):
     channels = weights[0].shape[0] // 4
     slices0, columns = windows.shape[1] // 16, windows.shape[-1]
     out_slices = slices0 - 6
@@ -526,9 +561,10 @@
     return pl.pallas_call(
         network_kernel,
         out_shape=jax.ShapeDtypeStruct(local, jnp.float32),
-        in_specs=[vmem] * 4 + [pl.BlockSpec(memory_space=pltpu.SMEM)] + [hbm] * 2,
+        in_specs=[vmem] * 2 + [hbm] * 5,
         out_specs=vmem,
-        scratch_shapes=[
+        scratch_shapes=[pltpu.VMEM(weight.shape, weight.dtype) for weight in weights]
+        + [
             pltpu.VMEM(local, jnp.float32),
             pltpu.VMEM(local, jnp.float32),
             pltpu.VMEM((2, 3, slices0 * 16, columns), jnp.bfloat16),
@@ -537,17 +573,15 @@
             pltpu.VMEM((6 * channels, 2 * columns), jnp.float32),
             pltpu.VMEM((6 * channels, 2 * columns), jnp.float32),
             pltpu.VMEM((out_slices // 2 + 1, 72, 2 * columns), jnp.float32),
-            pltpu.SemaphoreType.DMA((2,)),
+            pltpu.SemaphoreType.DMA((5,)),
         ],
         compiler_params=pltpu.CompilerParams(vmem_limit_bytes=40 * 2**20),
         cost_estimate=pl.CostEstimate(
             flops=10**10, bytes_accessed=2 * 10**6, transcendentals=4 * 10**6
         ),
     )(
-        windows,
-        *weights,
-        size,
-        *in_hbm(current_image.reshape(local), langevin_noise.reshape(local)),
+        windows, scalars,
+        *in_hbm(*weights, current_image.reshape(local), langevin_noise.reshape(local)),
     ).reshape(current_image.shape)
 
 
@@ -562,8 +596,9 @@
     images = [own] + [
         lax.ppermute(own, "band", [(i, i ^ x) for i in range(bands)]) for x in range(1, 4)
     ]
-    turned, stacked, high, low, *weights = preparation(
-        coil_maps, measured_kspace, caipi_steps, band_order, weight_in, weight_mid, weight_out
+    turned, scalars, stacked, high, low, *weights = preparation(
+        step_size, coil_maps, measured_kspace, caipi_steps, band_order,
+        weight_in, weight_mid, weight_out,
     )
 
     odd = band % 2 == 1
@@ -575,7 +610,7 @@
     tall = tall.reshape(-1, 2, row_count, columns)
     below, above = exchanged_rows(tall, 3)
     partial_sums = partial_consistency(
-        images, (turned, stacked, high, low), step_size, sample_mask, caipi_steps, band_order
+        images, (turned, scalars, stacked, high, low), sample_mask
     )
     partial_sums, below, above = lax.optimization_barrier((partial_sums, below, above))
     swapped = lax.all_to_all(partial_sums, "band", split_axis=0, concat_axis=0, tiled=True)
@@ -583,9 +618,9 @@
     windows = jnp.stack(
         [field[:, :, 4 * g : 4 * g + 8].reshape(-1, columns) for g in range(2)], axis=0
     )
-    base = stepped_without_data(windows, weights, step_size, current_image, langevin_noise)
+    base = stepped_without_data(windows, scalars, weights, current_image, langevin_noise)
     pieces = swapped.reshape((-1, positions) + swapped.shape[1:]).astype(jnp.float32)
-    return base - jnp.sum(pieces, axis=0)
+    return base - jnp.sum(pieces, axis=0).reshape(base.shape)
 
 
 def solution(mesh):

time: 46.9 us -> 34.7 us (0.74)
  local copies, waits for them, and re-layouts: 10.5 us -> 0.15 us
  other arithmetic: 4.5 us -> 2.14 us
  Pallas kernels: 18.4 us -> 19.3 us
    unnamed x20 -> x0, local copies, waits for them, and re-layouts: 8.33 us -> none
    concatenate x2, local copies, waits for them, and re-layouts: 2.06 us -> 0.03 us  [per_device(): tall = jnp.concatenate([under, own, over], axis=0)]
    concatenate x1, other arithmetic: 1.12 us -> 0.24 us  [per_device(): jnp.concatenate([below, tall, above, jnp.zeros_like(above[:, :, :2])], ax...]
    pallas_call x1, Pallas kernels: 3.13 us -> 3.94 us  [preparation(): pl.pallas_call(preparation_kernel, out_shape=(jax.ShapeDtypeStruct(turned...]
    concatenate x1, other arithmetic: 0.86 us -> 0.07 us  [per_device(): tall = jnp.concatenate([under, own, over], axis=0)]
    select_n x1, other arithmetic: 0.62 us -> 0.01 us  [per_device(): under = jnp.where(band == 0, jnp.zeros_like(under), under)]
  transfers between devices with their start and end apart: 6 -> 6, of which waited for: 0 -> 0; matrix products, arithmetic and copies ran while one was open for 11% -> 2% of each run, Pallas kernels for 40% -> 56%
where the time goes in v5:
time: 34.7 us; the launch traced here: 34.3 us
  Pallas kernels  19.3 us (56%)
  starting transfers between devices  12 us (35%)
  other arithmetic  2.14 us (6%)
  between operations  0.8 us (2%)
    pallas_call x1, Pallas kernels, stepped_without_data(): pl.pallas_call(network_kernel, out_shape=jax.ShapeDtypeStruct(local, jnp....  10.5 us
    ppermute x2, starting transfers between devices, exchanged_rows(): arrived.append(lax.ppermute(sent, 'slab', route))  5.25 us
    pallas_call x1, Pallas kernels, partial_consistency(): pl.pallas_call(consistency_kernel, out_shape=jax.ShapeDtypeStruct((all_po...  4.82 us
    pallas_call x1, Pallas kernels, preparation(): pl.pallas_call(preparation_kernel, out_shape=(jax.ShapeDtypeStruct(turned...  3.94 us
    all_to_all x1, starting transfers between devices, per_device(): lax.all_to_all(partial_sums, 'band', split_axis=0, concat_axis=0, tiled=T...  3.56 us
    ppermute x3, starting transfers between devices, per_device(): lax.ppermute(own, 'band', [(i, i ^ x) for i in range(bands)])  3.15 us
    convert_element_type x1, other arithmetic, per_device(): current_image.astype(jnp.bfloat16)  0.91 us
  transfers between devices with their start and end apart: 6, of which 0 were waited for; matrix products, arithmetic and copies ran while one was open for 2% of the time, Pallas kernels for 56%

profile of v5, /device:TPU:0, one launch (start us, length us, event | category | flops | bytes accessed | tf_op | source)
XLA Modules:
  0.0 34.3 jit_solution(7230688897769746884)
XLA Ops:
  0.0 0.9 %convert_element_type.9 = bf16[2,4,2,4,384]{4,3,2,1,0:T(4,128)(2,1)S(1)} convert(f32[2,4,2,4,384]{4,3,2,1,0:T(4,128)} %param.11) | non-fusion elementwise | flops 24576 | bytes 147456 | tf_op jit(solution)/shard_map/convert_element_type | solution.py:595
  0.9 0.5 %collective-permute-start = (bf16[8,8,384]{2,1,0:T(8,128)(2,1)S(1)}, bf16[8,8,384]{2,1,0:T(8,128)(2,1)S(1)}, u32[]{:S(2)}, u32[]{:S(2)}) collective-permute-start(bf16[8,8,384]{2,1,0:T(8,128)(2,1)S(1)} %reshape.23.own_ref), channel_id=1, source_target_pairs={{0,8},{8,0},{16,24},{24,16},{1,9},{9,1},{17,25},{25,17},{2,10},{10... | collective-permute-start | bytes 147464 | tf_op jit(solution)/shard_map/ppermute | solution.py:597
  1.5 2.6 %collective-permute-start.1 = (bf16[8,8,384]{2,1,0:T(8,128)(2,1)S(1)}, bf16[8,8,384]{2,1,0:T(8,128)(2,1)S(1)}, u32[]{:S(2)}, u32[]{:S(2)}) collective-permute-start(bf16[8,8,384]{2,1,0:T(8,128)(2,1)S(1)} %reshape.23.own_ref), channel_id=1, source_target_pairs={{0,16},{8,24},{16,0},{24,8},{1,17},{9,25},{17,1},{25,9},{2,18},{10... | collective-permute-start | bytes 147464 | tf_op jit(solution)/shard_map/ppermute | solution.py:597
  4.0 0.1 collective-permute-start.2
  4.7 3.9 %shard_map.109 = (bf16[3,8,4,64,128]{4,3,2,1,0:T(8,128)(2,1)S(1)}, f32[16,128]{1,0:T(8,128)S(1)}, f32[4,8,8,384]{3,2,1,0:T(8,128)}, bf16[384,768]{1,0:T(8,128)(2...) custom-call(f32[1]{0:T(128)S(6)} %copy.12.size_ref, ...), custom_call_target="tpu_custom_call" | custom-call | flops 4000000000 | bytes 4000000 | tf_op jit(solution)/shard_map/pallas_call | solution.py:254
  8.7 0.1 pad_slice_fusion
  8.8 0.0 collective-permute-done.one_ref
  8.8 0.0 collective-permute-done.2.three_ref
  8.8 0.1 pad_maximum_fusion.8
  8.9 0.1 broadcast_select_fusion.2
  9.0 0.7 %collective-permute-start.4 = (bf16[14,2,3,384]{3,2,1,0:T(4,128)(2,1)S(1)}, bf16[14,2,3,384]{3,2,1,0:T(4,128)(2,1)S(1)}, u32[]{:S(2)}, u32[]{:S(2)}) collective-permute-start(bf16[14,2,3,384]{3,2,1,0:T(4,128)(2,1)S(1)} %get-tuple-element.33), channel_id=1, source_target_pairs={{1,2},{2,1},{3,4},{4,3},{5,6},{6,5},{9,10},{10,9},{11,12},{12,11},... | collective-permute-start | bytes 193544 | tf_op jit(solution)/shard_map/ppermute | solution.py:22
  9.7 4.6 %collective-permute-start.3 = (bf16[14,2,3,384]{3,2,1,0:T(4,128)(2,1)S(1)}, bf16[14,2,3,384]{3,2,1,0:T(4,128)(2,1)S(1)}, u32[]{:S(2)}, u32[]{:S(2)}) collective-permute-start(bf16[14,2,3,384]{3,2,1,0:T(4,128)(2,1)S(1)} %get-tuple-element.34), channel_id=1, source_target_pairs={{0,1},{1,0},{2,3},{3,2},{4,5},{5,4},{6,7},{7,6},{8,9},{9,8},{10,11... | collective-permute-start | bytes 193544 | tf_op jit(solution)/shard_map/ppermute | solution.py:22
  14.3 0.0 collective-permute-done.1.two_ref
  14.3 4.8 %shard_map.110 = bf16[8,4,8,384]{3,2,1,0:T(8,128)(2,1)} custom-call(bf16[8,8,384]{2,1,0:T(8,128)(2,1)S(1)} %reshape.23.own_ref, bf16[8,8,384]{2,1,0:T(8,128)(2,1)S(1)} %collective-permute-done.one_ref, bf16[8,8,384]{2,1,0:T(8,128)(2,1)S(1)} %collective-permute-done.1.two_ref, bf16[8,8,384]{2,1,0:T(8,128)(2,1)S(1)} %collective-permute-done.2.three_ref, ...), custom_call_target="tpu_custom_call" | custom-call | flops 4000000000 | bytes 4000000 | tf_op jit(solution)/shard_map/pallas_call | solution.py:386
  19.1 0.0 collective-permute-done.4
  19.1 0.0 collective-permute-done.3
  19.1 0.1 broadcast_select_fusion
  19.2 3.6 %all-to-all-start = ((bf16[8,4,8,384]{3,2,1,0:T(8,128)(2,1)}), bf16[8,4,8,384]{3,2,1,0:T(8,128)(2,1)S(1)}, u32[]{:S(2)}, u32[]{:S(2)}) async-start(bf16[8,4,8,384]{3,2,1,0:T(8,128)(2,1)} %shard_map.110), calls=%async_computation | async-start | bytes 393216 | tf_op jit(solution)/shard_map/all_to_all | solution.py:616
  22.8 0.2 pad_maximum_fusion.4
  23.1 10.5 %shard_map.111 = f32[8,2,4,384]{3,2,1,0:T(4,128)S(1)} custom-call(bf16[2,224,384]{2,1,0:T(8,128)(2,1)S(1)} %pad_maximum_fusion.window_ref, f32[16,128]{1,0:T(8,128)S(1)} %get-tuple-element.17.scalars_ref, bf16[256,144]{1,0:T(8,128)(2,1)} %get-tuple-element.23.first_hbm, bf16[384,768]{1,0:T(8,128)(2,1)} %get-tuple-element.24.wide_hbm, ...), custom_call_target="tpu_custom_call" | custom-call | flops 10000000000 | bytes 2000000 | tf_op jit(solution)/shard_map/pallas_call | solution.py:561
  33.6 0.0 all-to-all-done
  33.7 0.7 %sub.3 = f32[2,4,2,4,384]{4,3,2,1,0:T(4,128)} subtract(f32[2,4,2,4,384]{4,3,2,1,0:T(4,128)S(1)} %bitcast.13, f32[2,4,2,4,384]{4,3,2,1,0:T(4,128)S(1)} %reshape.27) | non-fusion elementwise | flops 24576 | bytes 294912 | tf_op jit(solution)/shard_map/sub | solution.py:623
  (8 shorter events, 0.2 us)
Async XLA Ops:
  0.9 7.8 %collective-permute-start = (bf16[8,8,384]{2,1,0:T(8,128)(2,1)S(1)}, bf16[8,8,384]{2,1,0:T(8,128)(2,1)S(1)}, u32[]{:S(2)}, u32[]{:S(2)}) collective-permute-start(bf16[8,8,384]{2,1,0:T(8,128)(2,1)S(1)} %reshape.23.own_ref), channel_id=1, source_target_pairs={{0,8},{8,0},{16,24},{24,16},{1,9},{9,1},{17,25},{25,17},{2,10},{10... | collective-permute-start | bytes 147464 | tf_op jit(solution)/shard_map/ppermute | solution.py:597
  1.5 12.8 %collective-permute-start.1 = (bf16[8,8,384]{2,1,0:T(8,128)(2,1)S(1)}, bf16[8,8,384]{2,1,0:T(8,128)(2,1)S(1)}, u32[]{:S(2)}, u32[]{:S(2)}) collective-permute-start(bf16[8,8,384]{2,1,0:T(8,128)(2,1)S(1)} %reshape.23.own_ref), channel_id=1, source_target_pairs={{0,16},{8,24},{16,0},{24,8},{1,17},{9,25},{17,1},{25,9},{2,18},{10... | collective-permute-start | bytes 147464 | tf_op jit(solution)/shard_map/ppermute | solution.py:597
  4.0 4.8 %collective-permute-start.2 = (bf16[8,8,384]{2,1,0:T(8,128)(2,1)S(1)}, bf16[8,8,384]{2,1,0:T(8,128)(2,1)S(1)}, u32[]{:S(2)}, u32[]{:S(2)}) collective-permute-start(bf16[8,8,384]{2,1,0:T(8,128)(2,1)S(1)} %reshape.23.own_ref), channel_id=1, source_target_pairs={{0,24},{8,16},{16,8},{24,0},{1,25},{9,17},{17,9},{25,1},{2,26},{10... | collective-permute-start | bytes 147464 | tf_op jit(solution)/shard_map/ppermute | solution.py:597
  9.0 10.1 %collective-permute-start.4 = (bf16[14,2,3,384]{3,2,1,0:T(4,128)(2,1)S(1)}, bf16[14,2,3,384]{3,2,1,0:T(4,128)(2,1)S(1)}, u32[]{:S(2)}, u32[]{:S(2)}) collective-permute-start(bf16[14,2,3,384]{3,2,1,0:T(4,128)(2,1)S(1)} %get-tuple-element.33), channel_id=1, source_target_pairs={{1,2},{2,1},{3,4},{4,3},{5,6},{6,5},{9,10},{10,9},{11,12},{12,11},... | collective-permute-start | bytes 193544 | tf_op jit(solution)/shard_map/ppermute | solution.py:22
  9.7 9.4 %collective-permute-start.3 = (bf16[14,2,3,384]{3,2,1,0:T(4,128)(2,1)S(1)}, bf16[14,2,3,384]{3,2,1,0:T(4,128)(2,1)S(1)}, u32[]{:S(2)}, u32[]{:S(2)}) collective-permute-start(bf16[14,2,3,384]{3,2,1,0:T(4,128)(2,1)S(1)} %get-tuple-element.34), channel_id=1, source_target_pairs={{0,1},{1,0},{2,3},{3,2},{4,5},{5,4},{6,7},{7,6},{8,9},{9,8},{10,11... | collective-permute-start | bytes 193544 | tf_op jit(solution)/shard_map/ppermute | solution.py:22
  19.2 14.4 %all-to-all-start = ((bf16[8,4,8,384]{3,2,1,0:T(8,128)(2,1)}), bf16[8,4,8,384]{3,2,1,0:T(8,128)(2,1)S(1)}, u32[]{:S(2)}, u32[]{:S(2)}) async-start(bf16[8,4,8,384]{3,2,1,0:T(8,128)(2,1)} %shard_map.110), calls=%async_computation | async-start | bytes 393216 | tf_op jit(solution)/shard_map/all_to_all | solution.py:616

commit v6 on v5

--- a/solution.py
+++ b/solution.py
@@ -29,6 +29,13 @@
     return [pltpu.with_memory_space_constraint(array, pltpu.HBM) for array in arrays]
 
 
+def series(square, coefficients):
+    total = jnp.full_like(square, coefficients[-1])
+    for coefficient in coefficients[-2::-1]:
+        total = total * square + coefficient
+    return total
+
+
 def fill_factors(factors_ref):
     rows, columns = factors_ref.shape
     near = 16
@@ -37,12 +44,17 @@
     row = lax.broadcasted_iota(jnp.int32, (half, columns), 0)
     row = jnp.where(row < count, near * row, row - count).astype(jnp.float32)
     phase = row * lax.broadcasted_iota(jnp.int32, (half, columns), 1).astype(jnp.float32)
-    phase = phase - columns * jnp.floor(phase * (1.0 / columns))
-    phase = phase * (2.0 * math.pi / columns)
+    phase = phase - columns * jnp.floor(phase * (1.0 / columns) + 0.5)
+    angle = phase * (math.pi / columns)
+    square = angle * angle
+    sine = angle * series(square, [(-1.0) ** k / math.factorial(2 * k + 1) for k in range(7)])
+    cosine = series(square, [(-1.0) ** k / math.factorial(2 * k) for k in range(8)])
     scale = 1.0 / math.sqrt(columns)
-    for begin, wave in ((0, jnp.cos(phase)), (count, jnp.sin(phase))):
+    waves = (1.0 - 2.0 * sine * sine, 2.0 * sine * cosine)
+    for part, wave in enumerate(waves):
+        begin = count * part
         factors_ref[begin : begin + count, :] = scale * wave[:count]
-        begin = 2 * count + (0 if begin == 0 else near)
+        begin = 2 * count + near * part
         factors_ref[begin : begin + near, :] = wave[count:]
 
 
@@ -171,252 +183,219 @@
 
 
 def preparation_kernel(
-    size_ref, steps_hbm, order_hbm, coil_hbm, kspace_hbm, first_hbm, mid_hbm, last_hbm,
-    turned_ref, scalars_ref,
-    stacked_out, high_out, low_out, first_out, wide_out, last_out,
-    steps_ref, order_ref, coil_ref, kspace_ref, factors_ref, first_raw, mid_raw, last_raw,
-    first_sum, last_sum, stacked_ref, high_ref, low_ref, first_ref, wide_ref, last_ref,
-    sems, coil_sems, out_sems,
+    size_ref, steps_hbm, order_hbm, coil_hbm,
+    turned_ref, scalars_ref, high_ref, low_ref,
+    steps_ref, order_ref, coil_ref, factors_ref, sems, coil_sems,
 ):
     all_positions, slices, coils, _, rows, columns = coil_ref.shape
     unit = columns // 8
     block = coils * 2 * rows
-    pairs = (
-        (first_hbm, first_raw), (mid_hbm, mid_raw), (last_hbm, last_raw),
-        (steps_hbm, steps_ref), (order_hbm, order_ref), (kspace_hbm, kspace_ref),
-    )
-    copies = [pltpu.make_async_copy(src, dst, sems.at[i]) for i, (src, dst) in enumerate(pairs)]
-    coil_copies = [
+    copies = [
+        pltpu.make_async_copy(steps_hbm, steps_ref, sems.at[0]),
+        pltpu.make_async_copy(order_hbm, order_ref, sems.at[1]),
+    ] + [
         pltpu.make_async_copy(coil_hbm.at[g], coil_ref.at[g], coil_sems.at[g])
         for g in range(all_positions)
     ]
-    results = (
-        (first_ref, first_out), (wide_ref, wide_out), (last_ref, last_out),
-        (high_ref, high_out), (low_ref, low_out), (stacked_ref, stacked_out),
-    )
-    returns = [
-        pltpu.make_async_copy(src, dst, out_sems.at[i]) for i, (src, dst) in enumerate(results)
-    ]
-    for copy in copies[:5] + coil_copies + copies[5:]:
+    for copy in copies:
         copy.start()
     fill_factors(factors_ref)
     build_tables(factors_ref, high_ref, low_ref)
-    for copy in copies[:3]:
-        copy.wait()
-    fill_weights(
-        first_raw, mid_raw, last_raw, first_sum, last_sum, first_ref, wide_ref, last_ref
-    )
-    for copy in returns[:5]:
-        copy.start()
-    for copy in copies[3:5]:
+    scalars_ref[all_positions:, :] = jnp.full(
+        (scalars_ref.shape[0] - all_positions, 128), size_ref[0], jnp.float32
+    )
+    for copy in copies:
         copy.wait()
     for g in range(all_positions):
         shift = steps_ref[order_ref[g]] * unit
         scalars_ref[g : g + 1, :] = jnp.full((1, 128), shift, jnp.int32).astype(jnp.float32)
-        coil_copies[g].wait()
         for s in range(slices):
 
             def store_coil(j, value, s=s, g=g):
                 turned_ref[j, g, s] = value.reshape(block, 128).astype(jnp.bfloat16)
 
             turned_tiles(stacked_parts(coil_ref[g, s].astype(jnp.float32)), shift, store_coil)
-    scalars_ref[all_positions:, :] = jnp.full(
-        (scalars_ref.shape[0] - all_positions, 128), size_ref[0], jnp.float32
-    )
-    copies[5].wait()
-    for s in range(slices):
-        stacked_ref[s] = stacked_parts(kspace_ref[s])
-    returns[5].start()
-    for copy in returns:
-        copy.wait()
-
-
-def preparation(
-    step_size, coil_maps, measured_kspace, caipi_steps, band_order, weight_in, weight_mid, weight_out
-):
+
+
+def preparation(step_size, coil_maps, caipi_steps, band_order):
     all_positions, slices, coils, _, rows, columns = coil_maps.shape
-    channels = weight_mid.shape[0]
-    first = jnp.transpose(weight_in, (2, 3, 4, 1, 0))
-    mid = jnp.transpose(weight_mid, (2, 3, 4, 0, 1))
-    last = jnp.transpose(weight_out, (2, 3, 4, 0, 1))
     f32, bf16 = jnp.float32, jnp.bfloat16
     hbm = pl.BlockSpec(memory_space=pltpu.HBM)
     vmem = pl.BlockSpec(memory_space=pltpu.VMEM)
-    results = (
-        ((slices, coils, 2 * rows, columns), f32),
-        ((columns, 2 * columns), bf16),
-        ((columns, 2 * columns), bf16),
-        ((4 * channels, 144), bf16),
-        ((6 * channels, 12 * channels), bf16),
-        ((72, 6 * channels), bf16),
-    )
     turned_shape = (columns // 128, all_positions, slices, coils * 2 * rows, 128)
     return pl.pallas_call(
         preparation_kernel,
         out_shape=(
             jax.ShapeDtypeStruct(turned_shape, bf16),
             jax.ShapeDtypeStruct((2 * all_positions, 128), f32),
-        )
-        + tuple(pltpu.HBM(shape, dtype) for shape, dtype in results),
-        in_specs=[pl.BlockSpec(memory_space=pltpu.SMEM)] + [hbm] * 7,
-        out_specs=(vmem,) * 2 + (hbm,) * 6,
+            jax.ShapeDtypeStruct((columns, 2 * columns), bf16),
+            jax.ShapeDtypeStruct((columns, 2 * columns), bf16),
+        ),
+        in_specs=[pl.BlockSpec(memory_space=pltpu.SMEM)] + [hbm] * 3,
+        out_specs=(vmem,) * 4,
         scratch_shapes=[
             pltpu.SMEM(caipi_steps.shape, jnp.int32),
             pltpu.SMEM(band_order.shape, jnp.int32),
             pltpu.VMEM(coil_maps.shape, bf16),
-            pltpu.VMEM(measured_kspace.shape, f32),
             pltpu.VMEM((2 * (columns // 16 + 16), columns), f32),
-            pltpu.VMEM(first.shape, bf16),
-            pltpu.VMEM(mid.shape, bf16),
-            pltpu.VMEM(last.shape, bf16),
-            pltpu.VMEM((256, 4 * channels), f32),
-            pltpu.VMEM((72, 6 * channels), f32),
-        ]
-        + [pltpu.VMEM(shape, dtype) for shape, dtype in results]
-        + [
-            pltpu.SemaphoreType.DMA((6,)),
+            pltpu.SemaphoreType.DMA((2,)),
             pltpu.SemaphoreType.DMA((all_positions,)),
-            pltpu.SemaphoreType.DMA((6,)),
         ],
         compiler_params=pltpu.CompilerParams(vmem_limit_bytes=40 * 2**20),
         cost_estimate=pl.CostEstimate(
             flops=4 * 10**9, bytes_accessed=4 * 10**6, transcendentals=0
         ),
-    )(
-        step_size,
-        *in_hbm(caipi_steps, band_order, coil_maps, measured_kspace),
-        *in_hbm(first, mid, last),
-    )
+    )(step_size, *in_hbm(caipi_steps, band_order, coil_maps))
 
 
 def consistency_kernel(
-    own_ref, one_ref, two_ref, three_ref, turned_ref, scalars_ref,
-    stacked_hbm, high_hbm, low_hbm, mask_hbm,
-    out_ref,
-    stacked_ref, high_ref, low_ref, mask_ref, real_ref, imag_ref, field_ref, swap_ref, sum_ref,
-    sems,
+    own_ref, one_ref, two_ref, three_ref, turned_ref, scalars_ref, high_ref, low_ref,
+    kspace_hbm, mask_hbm,
+    own_out, one_out, two_out, three_out,
+    kspace_ref, mask_ref, real_ref, imag_ref, field_ref, swap_ref, sum_ref, sems,
 ):
     tiles, all_positions, slices, _, _ = turned_ref.shape
-    _, coils, doubled, columns = stacked_ref.shape
-    rows, positions = doubled // 2, all_positions // 4
-    pairs = (
-        (high_hbm, high_ref), (low_hbm, low_ref), (stacked_hbm, stacked_ref), (mask_hbm, mask_ref),
-    )
-    copies = [pltpu.make_async_copy(src, dst, sems.at[i]) for i, (src, dst) in enumerate(pairs)]
+    _, coils, _, rows, columns = kspace_ref.shape
+    doubled, positions = 2 * rows, all_positions // 4
+    copies = [
+        pltpu.make_async_copy(kspace_hbm, kspace_ref, sems.at[0]),
+        pltpu.make_async_copy(mask_hbm, mask_ref, sems.at[1]),
+    ]
     for copy in copies:
         copy.start()
     size = scalars_ref[all_positions : all_positions + 1, :]
-
-    def shift_of(g):
-        return jnp.max(scalars_ref[pl.ds(g, 1), :]).astype(jnp.int32)
+    owners = []
+    for x in range(4):
+        first = lax.bitwise_xor(lax.axis_index("band"), jnp.int32(x)) * positions
+        for p in range(positions):
+            shift = jnp.max(scalars_ref[pl.ds(first + p, 1), :]).astype(jnp.int32)
+            owners.append((x, p, first + p, shift))
 
     def coil_of(j, g, s):
         return turned_ref[j, g, s].astype(jnp.float32).reshape(coils, doubled, 128)
 
-    for x, ref in enumerate((own_ref, one_ref, two_ref, three_ref)):
-        for p in range(positions):
-            g = lax.bitwise_xor(lax.axis_index("band"), jnp.int32(x)) * positions + p
-
-            def store_image(j, value, g=g):
-                other = halves_swapped(value)
-                top = upper_half(value)
-                real_ref[j, g] = jnp.where(top, value, other)
-                imag_ref[j, g] = jnp.where(top, other, value)
-
-            image = ref[p * slices : (p + 1) * slices].astype(jnp.float32)
-            turned_tiles(image, shift_of(g), store_image)
-
-    block = coils * 2 * rows
-    for j in range(tiles):
-        for s in range(slices):
-            with_real = jnp.zeros((coils, 2 * rows, 128), jnp.float32)
-            with_imag = jnp.zeros((coils, 2 * rows, 128), jnp.float32)
-            for g in range(all_positions):
-                coil = coil_of(j, g, s)
-                with_real += coil * real_ref[j, g, s]
-                with_imag += coil * imag_ref[j, g, s]
-            total = with_real + signed_swap(with_imag, -1.0, 1.0)
-            field_ref[s * block : (s + 1) * block, 128 * j : 128 * (j + 1)] = total.reshape(
-                block, 128
-            )
-
+    images = (own_ref, one_ref, two_ref, three_ref)
+    for k, (x, p, g, shift) in enumerate(owners):
+
+        def store_image(j, value, k=k):
+            other = halves_swapped(value)
+            top = upper_half(value)
+            real_ref[j, k] = jnp.where(top, value, other)
+            imag_ref[j, k] = jnp.where(top, other, value)
+
+        image = images[x][p * slices : (p + 1) * slices].astype(jnp.float32)
+        turned_tiles(image, shift, store_image)
     for copy in copies:
         copy.wait()
-    product = table_product(field_ref[...], high_ref, low_ref)
-    grouped = (slices, coils, 2 * rows, columns)
-    with_cos = product[:, :columns].reshape(grouped)
-    with_sin = product[:, columns:].reshape(grouped)
-    spectrum = with_cos + signed_swap(with_sin, 1.0, -1.0)
-    keep = mask_ref[...].astype(jnp.float32).reshape(slices, 1, 1, columns)
-    residual = keep * (spectrum - stacked_ref[...])
-    product = table_product(residual.reshape(slices * block, columns), high_ref, low_ref)
-    with_cos = product[:, :columns].reshape(grouped)
-    with_sin = product[:, columns:].reshape(grouped)
-    back = with_cos + signed_swap(with_sin, -1.0, 1.0)
-    field_ref[...] = back.reshape(slices * block, columns)
-    swap_ref[...] = halves_swapped(back).reshape(slices * block, columns)
-
-    for j in range(tiles):
-        for s in range(slices):
-            place = (slice(s * block, (s + 1) * block), slice(128 * j, 128 * (j + 1)))
-            field = field_ref[place].reshape(coils, 2 * rows, 128)
-            swapped = swap_ref[place].reshape(coils, 2 * rows, 128)
-            for g in range(all_positions):
-                coil = coil_of(j, g, s)
-                straight = jnp.sum(coil * field, axis=0)
-                crossed = jnp.sum(coil * swapped, axis=0)
-                straight = straight + halves_swapped(straight)
-                crossed = halves_swapped(crossed) - crossed
-                sum_ref[g, s, :, 128 * j : 128 * (j + 1)] = size * jnp.where(
-                    upper_half(straight), straight, crossed
+
+    block = coils * doubled
+    halves = [range(0, slices // 2), range(slices // 2, slices)]
+
+    def rows_of(half):
+        return slice(half[0] * block, (half[-1] + 1) * block)
+
+    def collapse(half):
+        for j in range(tiles):
+            for s in half:
+                with_real = jnp.zeros((coils, doubled, 128), jnp.float32)
+                with_imag = jnp.zeros((coils, doubled, 128), jnp.float32)
+                for k, (_, _, g, _) in enumerate(owners):
+                    coil = coil_of(j, g, s)
+                    with_real += coil * real_ref[j, k, s]
+                    with_imag += coil * imag_ref[j, k, s]
+                total = with_real + signed_swap(with_imag, -1.0, 1.0)
+                field_ref[s * block : (s + 1) * block, 128 * j : 128 * (j + 1)] = total.reshape(
+                    block, 128
                 )
 
-    for g in range(all_positions):
-        back_shift = lax.rem(columns - shift_of(g), columns)
-        out_ref[g] = pltpu.roll(sum_ref[g], back_shift, 2).astype(jnp.bfloat16)
-
-
-def partial_consistency(images, prepared, sample_mask):
+    def transformed(source, half, top, bottom):
+        product = table_product(source, high_ref, low_ref)
+        grouped = (len(half), coils, doubled, columns)
+        with_cos = product[:, :columns].reshape(grouped)
+        with_sin = product[:, columns:].reshape(grouped)
+        return with_cos + signed_swap(with_sin, top, bottom)
+
+    def project(half):
+        spectrum = transformed(field_ref[rows_of(half)], half, 1.0, -1.0)
+        keep = mask_ref[...].astype(jnp.float32)[half[0] : half[-1] + 1]
+        keep = keep.reshape(len(half), 1, 1, columns)
+        data = stacked_parts(kspace_ref[half[0] : half[-1] + 1])
+        residual = (keep * (spectrum - data)).reshape(len(half) * block, columns)
+        back = transformed(residual, half, -1.0, 1.0)
+        field_ref[rows_of(half)] = back.reshape(len(half) * block, columns)
+        swap_ref[rows_of(half)] = halves_swapped(back).reshape(len(half) * block, columns)
+
+    def combine(half):
+        for j in range(tiles):
+            for s in half:
+                place = (slice(s * block, (s + 1) * block), slice(128 * j, 128 * (j + 1)))
+                field = field_ref[place].reshape(coils, doubled, 128)
+                swapped = swap_ref[place].reshape(coils, doubled, 128)
+                for k, (_, _, g, _) in enumerate(owners):
+                    coil = coil_of(j, g, s)
+                    straight = jnp.sum(coil * field, axis=0)
+                    crossed = jnp.sum(coil * swapped, axis=0)
+                    straight = straight + halves_swapped(straight)
+                    crossed = halves_swapped(crossed) - crossed
+                    sum_ref[k, s, :, 128 * j : 128 * (j + 1)] = size * jnp.where(
+                        upper_half(straight), straight, crossed
+                    )
+
+    for half in halves:
+        collapse(half)
+    for half in halves:
+        project(half)
+    for half in halves:
+        combine(half)
+
+    outs = (own_out, one_out, two_out, three_out)
+    for k, (x, p, _, shift) in enumerate(owners):
+        back_shift = lax.rem(columns - shift, columns)
+        outs[x][p] = pltpu.roll(sum_ref[k], back_shift, 2).astype(jnp.bfloat16)
+
+
+def partial_consistency(images, prepared, measured_kspace, sample_mask):
     tiles, all_positions, slices, _, _ = prepared[0].shape
-    _, coils, doubled, columns = prepared[2].shape
+    _, coils, _, rows, columns = measured_kspace.shape
+    doubled = 2 * rows
     total = slices * coils * doubled
     hbm = pl.BlockSpec(memory_space=pltpu.HBM)
     vmem = pl.BlockSpec(memory_space=pltpu.VMEM)
     image_shape = (tiles, all_positions, slices, doubled, 128)
+    part = jax.ShapeDtypeStruct((all_positions // 4, slices, doubled, columns), jnp.bfloat16)
     return pl.pallas_call(
         consistency_kernel,
-        out_shape=jax.ShapeDtypeStruct((all_positions, slices, doubled, columns), jnp.bfloat16),
-        in_specs=[vmem] * 6 + [hbm] * 4,
-        out_specs=vmem,
+        out_shape=(part,) * 4,
+        in_specs=[vmem] * 8 + [hbm] * 2,
+        out_specs=(vmem,) * 4,
         scratch_shapes=[
-            pltpu.VMEM((slices, coils, doubled, columns), jnp.float32),
-            pltpu.VMEM((columns, 2 * columns), jnp.bfloat16),
-            pltpu.VMEM((columns, 2 * columns), jnp.bfloat16),
+            pltpu.VMEM(measured_kspace.shape, jnp.float32),
             pltpu.VMEM(sample_mask.shape, jnp.int32),
             pltpu.VMEM(image_shape, jnp.float32),
             pltpu.VMEM(image_shape, jnp.float32),
             pltpu.VMEM((total, columns), jnp.float32),
             pltpu.VMEM((total, columns), jnp.float32),
             pltpu.VMEM((all_positions, slices, doubled, columns), jnp.float32),
-            pltpu.SemaphoreType.DMA((4,)),
+            pltpu.SemaphoreType.DMA((2,)),
         ],
         compiler_params=pltpu.CompilerParams(vmem_limit_bytes=40 * 2**20),
         cost_estimate=pl.CostEstimate(
             flops=4 * 10**9, bytes_accessed=4 * 10**6, transcendentals=0
         ),
-    )(*images, *prepared[:2], *in_hbm(*prepared[2:], sample_mask))
+    )(*images, *prepared, *in_hbm(measured_kspace, sample_mask))
 
 
 def network_kernel(
-    window_ref, scalars_ref, first_hbm, wide_hbm, last_hbm, image_hbm, noise_hbm,
+    window_ref, scalars_ref, first_hbm, mid_hbm, last_hbm, image_hbm, noise_hbm,
     out_ref,
-    first_ref, wide_ref, last_ref, image_ref, noise_ref, taps_ref, f1_ref, f2_ref, part_a, part_b, score_ref, sems,
+    first_raw, mid_raw, last_raw, image_ref, noise_ref,
+    first_sum, last_sum, first_ref, wide_ref, last_ref, taps_ref, f1_ref, f2_ref, part_a, part_b, score_ref, sems,
 ):
-    channels = first_ref.shape[0] // 4
+    channels = mid_raw.shape[-1]
     out_slices, _, rows, columns = out_ref.shape
     slices1, slices2 = out_slices + 4, out_slices + 2
     pairs = (
-        (first_hbm, first_ref), (wide_hbm, wide_ref), (last_hbm, last_ref),
+        (first_hbm, first_raw), (mid_hbm, mid_raw), (last_hbm, last_raw),
         (image_hbm, image_ref), (noise_hbm, noise_ref),
     )
     copies = [pltpu.make_async_copy(src, dst, sems.at[i]) for i, (src, dst) in enumerate(pairs)]
@@ -439,6 +418,9 @@
 
     for copy in copies[:3]:
         copy.wait()
+    fill_weights(
+        first_raw, mid_raw, last_raw, first_sum, last_sum, first_ref, wide_ref, last_ref
+    )
 
     def first_layer(z):
         source = jnp.concatenate(
@@ -551,8 +533,13 @@
             )
 
 
-def stepped_without_data(windows, scalars, weights, current_image, langevin_noise):
-    channels = weights[0].shape[0] // 4
+def stepped_without_data(
+    windows, scalars, current_image, langevin_noise, weight_in, weight_mid, weight_out
+):
+    channels = weight_mid.shape[0]
+    first = jnp.transpose(weight_in, (2, 3, 4, 1, 0))
+    mid = jnp.transpose(weight_mid, (2, 3, 4, 0, 1))
+    last = jnp.transpose(weight_out, (2, 3, 4, 0, 1))
     slices0, columns = windows.shape[1] // 16, windows.shape[-1]
     out_slices = slices0 - 6
     local = (out_slices,) + current_image.shape[2:]
@@ -563,10 +550,17 @@
         out_shape=jax.ShapeDtypeStruct(local, jnp.float32),
         in_specs=[vmem] * 2 + [hbm] * 5,
         out_specs=vmem,
-        scratch_shapes=[pltpu.VMEM(weight.shape, weight.dtype) for weight in weights]
-        + [
+        scratch_shapes=[
+            pltpu.VMEM(first.shape, jnp.bfloat16),
+            pltpu.VMEM(mid.shape, jnp.bfloat16),
+            pltpu.VMEM(last.shape, jnp.bfloat16),
             pltpu.VMEM(local, jnp.float32),
             pltpu.VMEM(local, jnp.float32),
+            pltpu.VMEM((256, 4 * channels), jnp.float32),
+            pltpu.VMEM((72, 6 * channels), jnp.float32),
+            pltpu.VMEM((4 * channels, 144), jnp.bfloat16),
+            pltpu.VMEM((6 * channels, 12 * channels), jnp.bfloat16),
+            pltpu.VMEM((72, 6 * channels), jnp.bfloat16),
             pltpu.VMEM((2, 3, slices0 * 16, columns), jnp.bfloat16),
             pltpu.VMEM((out_slices + 4, 8 * channels, columns), jnp.bfloat16),
             pltpu.VMEM((out_slices + 2, 6 * channels, columns), jnp.bfloat16),
@@ -581,7 +575,7 @@
         ),
     )(
         windows, scalars,
-        *in_hbm(*weights, current_image.reshape(local), langevin_noise.reshape(local)),
+        *in_hbm(first, mid, last, current_image.reshape(local), langevin_noise.reshape(local)),
     ).reshape(current_image.shape)
 
 
@@ -593,13 +587,9 @@
     local_slices = positions * group_slices
     band, bands = lax.axis_index("band"), lax.axis_size("band")
     own = current_image.astype(jnp.bfloat16).reshape(local_slices, 2 * row_count, columns)
-    images = [own] + [
-        lax.ppermute(own, "band", [(i, i ^ x) for i in range(bands)]) for x in range(1, 4)
-    ]
-    turned, scalars, stacked, high, low, *weights = preparation(
-        step_size, coil_maps, measured_kspace, caipi_steps, band_order,
-        weight_in, weight_mid, weight_out,
-    )
+    routes = [[(i, i ^ x) for i in range(bands)] for x in range(1, 4)]
+    images = [own] + [lax.ppermute(own, "band", route) for route in routes]
+    prepared = preparation(step_size, coil_maps, caipi_steps, band_order)
 
     odd = band % 2 == 1
     under = jnp.where(odd, images[1], images[3])[local_slices - 3 :]
@@ -609,18 +599,20 @@
     tall = jnp.concatenate([under, own, over], axis=0)
     tall = tall.reshape(-1, 2, row_count, columns)
     below, above = exchanged_rows(tall, 3)
-    partial_sums = partial_consistency(
-        images, (turned, scalars, stacked, high, low), sample_mask
-    )
-    partial_sums, below, above = lax.optimization_barrier((partial_sums, below, above))
-    swapped = lax.all_to_all(partial_sums, "band", split_axis=0, concat_axis=0, tiled=True)
+    sums = partial_consistency(images, prepared, measured_kspace, sample_mask)
+    sums, below, above = lax.optimization_barrier((sums, below, above))
+    arrived = [lax.ppermute(part, "band", route) for part, route in zip(sums[1:], routes)]
     field = jnp.concatenate([below, tall, above, jnp.zeros_like(above[:, :, :2])], axis=2)
     windows = jnp.stack(
         [field[:, :, 4 * g : 4 * g + 8].reshape(-1, columns) for g in range(2)], axis=0
     )
-    base = stepped_without_data(windows, scalars, weights, current_image, langevin_noise)
-    pieces = swapped.reshape((-1, positions) + swapped.shape[1:]).astype(jnp.float32)
-    return base - jnp.sum(pieces, axis=0).reshape(base.shape)
+    base = stepped_without_data(
+        windows, prepared[1], current_image, langevin_noise, weight_in, weight_mid, weight_out
+    )
+    total = sums[0].astype(jnp.float32)
+    for part in arrived:
+        total = total + part.astype(jnp.float32)
+    return base - total.reshape(base.shape)
 
 
 def solution(mesh):

time: 34.7 us -> 30.9 us (0.89)
  Pallas kernels: 19.3 us -> 16.8 us
  starting transfers between devices: 12 us -> 10.1 us
  waiting for transfers between devices: 0.02 us -> 0.66 us
    all_to_all x1 -> x0, starting transfers between devices: 3.56 us -> none  [per_device(): lax.all_to_all(partial_sums, 'band', split_axis=0, concat_axis=0, tiled=T...]
    ppermute x3 -> x6, starting transfers between devices: 3.15 us -> 5.08 us  [the longest x3 3.15 us: per_device(): images = [own] + [lax.ppermute(own, 'band', route) for route in routes]]
    pallas_call x1, Pallas kernels: 3.94 us -> 2.24 us  [preparation(): pl.pallas_call(preparation_kernel, out_shape=(jax.ShapeDtypeStruct(turned...]
    pallas_call x1, Pallas kernels: 4.82 us -> 3.77 us  [partial_consistency(): pl.pallas_call(consistency_kernel, out_shape=(part,) * 4, in_specs=[vmem]...]
    ppermute x3 -> x6, waiting for transfers between devices: 0.01 us -> 0.65 us  [the longest x3 0.64 us: per_device(): images = [own] + [lax.ppermute(own, 'band', route) for route in routes]]
  transfers between devices with their start and end apart: 6 -> 8, of which waited for: 0 -> 1; matrix products, arithmetic and copies ran while one was open for 2% -> 2% of each run, Pallas kernels for 56% -> 55%
where the time goes in v6:
time: 30.9 us; the launch traced here: 30.6 us
  Pallas kernels  16.8 us (54%)
  starting transfers between devices  10.1 us (33%)
  other arithmetic  2.14 us (7%)
  between operations  0.8 us (3%)
  waiting for transfers between devices  0.66 us (2%)
    pallas_call x1, Pallas kernels, stepped_without_data(): pl.pallas_call(network_kernel, out_shape=jax.ShapeDtypeStruct(local, jnp....  10.8 us
    ppermute x2, starting transfers between devices, exchanged_rows(): arrived.append(lax.ppermute(sent, 'slab', route))  5.01 us
    pallas_call x1, Pallas kernels, partial_consistency(): pl.pallas_call(consistency_kernel, out_shape=(part,) * 4, in_specs=[vmem]...  3.77 us
    ppermute x3, starting transfers between devices, per_device(): images = [own] + [lax.ppermute(own, 'band', route) for route in routes]  3.15 us
    pallas_call x1, Pallas kernels, preparation(): pl.pallas_call(preparation_kernel, out_shape=(jax.ShapeDtypeStruct(turned...  2.24 us
    ppermute x3, starting transfers between devices, per_device(): lax.ppermute(part, 'band', route)  1.93 us
    convert_element_type x1, other arithmetic, per_device(): current_image.astype(jnp.bfloat16)  0.91 us
    sub x1, other arithmetic, per_device(): return base - total.reshape(base.shape)  0.67 us
  transfers between devices with their start and end apart: 8, of which 1 were waited for; matrix products, arithmetic and copies ran while one was open for 2% of the time, Pallas kernels for 55%

profile of v6, /device:TPU:0, one launch (start us, length us, event | category | flops | bytes accessed | tf_op | source)
XLA Modules:
  0.0 30.6 jit_solution(3462308428803358803)
XLA Ops:
  0.0 0.9 %convert_element_type.15 = bf16[2,4,2,4,384]{4,3,2,1,0:T(4,128)(2,1)S(1)} convert(f32[2,4,2,4,384]{4,3,2,1,0:T(4,128)} %param.11) | non-fusion elementwise | flops 24576 | bytes 147456 | tf_op jit(solution)/shard_map/convert_element_type | solution.py:589
  0.9 0.5 %collective-permute-start = (bf16[8,8,384]{2,1,0:T(8,128)(2,1)S(1)}, bf16[8,8,384]{2,1,0:T(8,128)(2,1)S(1)}, u32[]{:S(2)}, u32[]{:S(2)}) collective-permute-start(bf16[8,8,384]{2,1,0:T(8,128)(2,1)S(1)} %reshape.20.own_ref), channel_id=1, source_target_pairs={{0,8},{8,0},{16,24},{24,16},{1,9},{9,1},{17,25},{25,17},{2,10},{10... | collective-permute-start | bytes 147464 | tf_op jit(solution)/shard_map/ppermute | solution.py:591
  1.5 2.6 %collective-permute-start.1 = (bf16[8,8,384]{2,1,0:T(8,128)(2,1)S(1)}, bf16[8,8,384]{2,1,0:T(8,128)(2,1)S(1)}, u32[]{:S(2)}, u32[]{:S(2)}) collective-permute-start(bf16[8,8,384]{2,1,0:T(8,128)(2,1)S(1)} %reshape.20.own_ref), channel_id=1, source_target_pairs={{0,16},{8,24},{16,0},{24,8},{1,17},{9,25},{17,1},{25,9},{2,18},{10... | collective-permute-start | bytes 147464 | tf_op jit(solution)/shard_map/ppermute | solution.py:591
  4.0 0.1 collective-permute-start.2
  4.7 2.2 %shard_map.109 = (bf16[3,8,4,64,128]{4,3,2,1,0:T(8,128)(2,1)S(1)}, f32[16,128]{1,0:T(8,128)S(1)}, bf16[384,768]{1,0:T(8,128)(2,1)S(1)}, bf16[384,768]{1,0:T(8,128)(2,1)S(1)}) custom-call(f32[1]{0:T(128)S(6)} %copy.12.size_ref, s32[8]{0:T(128)} %steps_hbm.1, s32[8]{0:T(128)} %order_hbm.1, bf16[8,4,8,2,4,384]{5,4,3,2,1,0:T(4,128)(2,1)} %coil_hbm.1), custom_call_target="tpu_custom_call" | custom-call | flops 4000000000 | bytes 4000000 | tf_op jit(solution)/shard_map/pallas_call | solution.py:226
  7.0 0.1 pad_slice_fusion
  7.1 0.0 collective-permute-done.one_ref
  7.1 0.6 %collective-permute-done.2.three_ref = bf16[8,8,384]{2,1,0:T(8,128)(2,1)S(1)} collective-permute-done((bf16[8,8,384]{2,1,0:T(8,128)(2,1)S(1)}, bf16[8,8,384]{2,1,0:T(8,128)(2,1)S(1)}, u32[]{:S(2)}, u32[]{:S(2)}) %collective-permute-start.2) | collective-permute-done | bytes 49184 | tf_op jit(solution)/shard_map/ppermute | solution.py:591
  7.8 0.1 pad_maximum_fusion.8
  7.8 0.1 broadcast_select_fusion.2
  8.0 0.7 %collective-permute-start.4 = (bf16[14,2,3,384]{3,2,1,0:T(4,128)(2,1)S(1)}, bf16[14,2,3,384]{3,2,1,0:T(4,128)(2,1)S(1)}, u32[]{:S(2)}, u32[]{:S(2)}) collective-permute-start(bf16[14,2,3,384]{3,2,1,0:T(4,128)(2,1)S(1)} %get-tuple-element.39), channel_id=1, source_target_pairs={{1,2},{2,1},{3,4},{4,3},{5,6},{6,5},{9,10},{10,9},{11,12},{12,11},... | collective-permute-start | bytes 193544 | tf_op jit(solution)/shard_map/ppermute | solution.py:22
  8.6 4.3 %collective-permute-start.3 = (bf16[14,2,3,384]{3,2,1,0:T(4,128)(2,1)S(1)}, bf16[14,2,3,384]{3,2,1,0:T(4,128)(2,1)S(1)}, u32[]{:S(2)}, u32[]{:S(2)}) collective-permute-start(bf16[14,2,3,384]{3,2,1,0:T(4,128)(2,1)S(1)} %get-tuple-element.40), channel_id=1, source_target_pairs={{0,1},{1,0},{2,3},{3,2},{4,5},{5,4},{6,7},{7,6},{8,9},{9,8},{10,11... | collective-permute-start | bytes 193544 | tf_op jit(solution)/shard_map/ppermute | solution.py:22
  13.0 0.0 collective-permute-done.1.two_ref
  13.0 3.8 %shard_map.110 = (bf16[2,4,8,384]{3,2,1,0:T(8,128)(2,1)S(1)}, bf16[2,4,8,384]{3,2,1,0:T(8,128)(2,1)S(1)}, bf16[2,4,8,384]{3,2,1,0:T(8,128)(2,1)S(1)}, bf16[2,4,8,384]{3,2,1,0:T(8,128)(2,1)S(1)}) custom-call(bf16[8,8,384]{2,1,0:T(8,128)(2,1)S(1)} %reshape.20.own_ref, bf16[8,8,384]{2,1,0:T(8,128)(2,1)S(1)} %collective-permute-done.one_ref, ...), custom_call_target="tpu_custom_call" | custom-call | flops 4000000000 | bytes 4000000 | tf_op jit(solution)/shard_map/pallas_call | solution.py:366
  16.8 0.0 collective-permute-done.4
  16.8 0.0 collective-permute-done.3
  16.8 0.1 broadcast_select_fusion
  16.9 0.5 %collective-permute-start.7 = (bf16[2,4,8,384]{3,2,1,0:T(8,128)(2,1)S(1)}, bf16[2,4,8,384]{3,2,1,0:T(8,128)(2,1)S(1)}, u32[]{:S(2)}, u32[]{:S(2)}) collective-permute-start(bf16[2,4,8,384]{3,2,1,0:T(8,128)(2,1)S(1)} %get-tuple-element.32), channel_id=1, source_target_pairs={{0,24},{8,16},{16,8},{24,0},{1,25},{9,17},{17,9},{25,1},{2,26},{10... | collective-permute-start | bytes 147464 | tf_op jit(solution)/shard_map/ppermute | solution.py:604
  17.4 0.8 %collective-permute-start.6 = (bf16[2,4,8,384]{3,2,1,0:T(8,128)(2,1)S(1)}, bf16[2,4,8,384]{3,2,1,0:T(8,128)(2,1)S(1)}, u32[]{:S(2)}, u32[]{:S(2)}) collective-permute-start(bf16[2,4,8,384]{3,2,1,0:T(8,128)(2,1)S(1)} %get-tuple-element.31), channel_id=1, source_target_pairs={{0,16},{8,24},{16,0},{24,8},{1,17},{9,25},{17,1},{25,9},{2,18},{10... | collective-permute-start | bytes 147464 | tf_op jit(solution)/shard_map/ppermute | solution.py:604
  18.2 0.6 %collective-permute-start.5 = (bf16[2,4,8,384]{3,2,1,0:T(8,128)(2,1)S(1)}, bf16[2,4,8,384]{3,2,1,0:T(8,128)(2,1)S(1)}, u32[]{:S(2)}, u32[]{:S(2)}) collective-permute-start(bf16[2,4,8,384]{3,2,1,0:T(8,128)(2,1)S(1)} %get-tuple-element.30), channel_id=1, source_target_pairs={{0,8},{8,0},{16,24},{24,16},{1,9},{9,1},{17,25},{25,17},{2,10},{10... | collective-permute-start | bytes 147464 | tf_op jit(solution)/shard_map/ppermute | solution.py:604
  18.8 0.2 pad_maximum_fusion.4
  19.1 10.8 %shard_map.111 = f32[8,2,4,384]{3,2,1,0:T(4,128)S(1)} custom-call(bf16[2,224,384]{2,1,0:T(8,128)(2,1)S(1)} %pad_maximum_fusion.window_ref, f32[16,128]{1,0:T(8,128)S(1)} %get-tuple-element.20.scalars_ref, bf16[3,3,3,2,64]{4,3,2,1,0:T(2,128)(2,1)} %bitcast.19, bf16[3,3,3,64,64]{4,3,2,1,0:T(8,128)(2,1)} %bitcast.17, bf16[3,3,3,2,64]{4,3,2,1,0:T(2,128)(2,1)} %bitcast.20, ...), custom_call_target="tpu_custom_call" | custom-call | flops 10000000000 | bytes 2000000 | tf_op jit(solution)/shard_map/pallas_call | solution.py:548
  29.9 0.0 collective-permute-done.7
  29.9 0.0 collective-permute-done.6
  29.9 0.0 collective-permute-done.5
  30.0 0.7 %sub.3 = f32[2,4,2,4,384]{4,3,2,1,0:T(4,128)} subtract(f32[2,4,2,4,384]{4,3,2,1,0:T(4,128)S(1)} %bitcast.11, f32[2,4,2,4,384]{4,3,2,1,0:T(4,128)S(1)} %reshape.24) | non-fusion elementwise | flops 24576 | bytes 294912 | tf_op jit(solution)/shard_map/sub | solution.py:615
  (8 shorter events, 0.2 us)
Async XLA Ops:
  0.9 6.1 %collective-permute-start = (bf16[8,8,384]{2,1,0:T(8,128)(2,1)S(1)}, bf16[8,8,384]{2,1,0:T(8,128)(2,1)S(1)}, u32[]{:S(2)}, u32[]{:S(2)}) collective-permute-start(bf16[8,8,384]{2,1,0:T(8,128)(2,1)S(1)} %reshape.20.own_ref), channel_id=1, source_target_pairs={{0,8},{8,0},{16,24},{24,16},{1,9},{9,1},{17,25},{25,17},{2,10},{10... | collective-permute-start | bytes 147464 | tf_op jit(solution)/shard_map/ppermute | solution.py:591
  1.5 11.5 %collective-permute-start.1 = (bf16[8,8,384]{2,1,0:T(8,128)(2,1)S(1)}, bf16[8,8,384]{2,1,0:T(8,128)(2,1)S(1)}, u32[]{:S(2)}, u32[]{:S(2)}) collective-permute-start(bf16[8,8,384]{2,1,0:T(8,128)(2,1)S(1)} %reshape.20.own_ref), channel_id=1, source_target_pairs={{0,16},{8,24},{16,0},{24,8},{1,17},{9,25},{17,1},{25,9},{2,18},{10... | collective-permute-start | bytes 147464 | tf_op jit(solution)/shard_map/ppermute | solution.py:591
  4.0 3.7 %collective-permute-start.2 = (bf16[8,8,384]{2,1,0:T(8,128)(2,1)S(1)}, bf16[8,8,384]{2,1,0:T(8,128)(2,1)S(1)}, u32[]{:S(2)}, u32[]{:S(2)}) collective-permute-start(bf16[8,8,384]{2,1,0:T(8,128)(2,1)S(1)} %reshape.20.own_ref), channel_id=1, source_target_pairs={{0,24},{8,16},{16,8},{24,0},{1,25},{9,17},{17,9},{25,1},{2,26},{10... | collective-permute-start | bytes 147464 | tf_op jit(solution)/shard_map/ppermute | solution.py:591
  8.0 8.8 %collective-permute-start.4 = (bf16[14,2,3,384]{3,2,1,0:T(4,128)(2,1)S(1)}, bf16[14,2,3,384]{3,2,1,0:T(4,128)(2,1)S(1)}, u32[]{:S(2)}, u32[]{:S(2)}) collective-permute-start(bf16[14,2,3,384]{3,2,1,0:T(4,128)(2,1)S(1)} %get-tuple-element.39), channel_id=1, source_target_pairs={{1,2},{2,1},{3,4},{4,3},{5,6},{6,5},{9,10},{10,9},{11,12},{12,11},... | collective-permute-start | bytes 193544 | tf_op jit(solution)/shard_map/ppermute | solution.py:22
  8.6 8.1 %collective-permute-start.3 = (bf16[14,2,3,384]{3,2,1,0:T(4,128)(2,1)S(1)}, bf16[14,2,3,384]{3,2,1,0:T(4,128)(2,1)S(1)}, u32[]{:S(2)}, u32[]{:S(2)}) collective-permute-start(bf16[14,2,3,384]{3,2,1,0:T(4,128)(2,1)S(1)} %get-tuple-element.40), channel_id=1, source_target_pairs={{0,1},{1,0},{2,3},{3,2},{4,5},{5,4},{6,7},{7,6},{8,9},{9,8},{10,11... | collective-permute-start | bytes 193544 | tf_op jit(solution)/shard_map/ppermute | solution.py:22
  16.9 13.0 %collective-permute-start.7 = (bf16[2,4,8,384]{3,2,1,0:T(8,128)(2,1)S(1)}, bf16[2,4,8,384]{3,2,1,0:T(8,128)(2,1)S(1)}, u32[]{:S(2)}, u32[]{:S(2)}) collective-permute-start(bf16[2,4,8,384]{3,2,1,0:T(8,128)(2,1)S(1)} %get-tuple-element.32), channel_id=1, source_target_pairs={{0,24},{8,16},{16,8},{24,0},{1,25},{9,17},{17,9},{25,1},{2,26},{10... | collective-permute-start | bytes 147464 | tf_op jit(solution)/shard_map/ppermute | solution.py:604
  17.4 12.5 %collective-permute-start.6 = (bf16[2,4,8,384]{3,2,1,0:T(8,128)(2,1)S(1)}, bf16[2,4,8,384]{3,2,1,0:T(8,128)(2,1)S(1)}, u32[]{:S(2)}, u32[]{:S(2)}) collective-permute-start(bf16[2,4,8,384]{3,2,1,0:T(8,128)(2,1)S(1)} %get-tuple-element.31), channel_id=1, source_target_pairs={{0,16},{8,24},{16,0},{24,8},{1,17},{9,25},{17,1},{25,9},{2,18},{10... | collective-permute-start | bytes 147464 | tf_op jit(solution)/shard_map/ppermute | solution.py:604
  18.2 11.7 %collective-permute-start.5 = (bf16[2,4,8,384]{3,2,1,0:T(8,128)(2,1)S(1)}, bf16[2,4,8,384]{3,2,1,0:T(8,128)(2,1)S(1)}, u32[]{:S(2)}, u32[]{:S(2)}) collective-permute-start(bf16[2,4,8,384]{3,2,1,0:T(8,128)(2,1)S(1)} %get-tuple-element.30), channel_id=1, source_target_pairs={{0,8},{8,0},{16,24},{24,16},{1,9},{9,1},{17,25},{25,17},{2,10},{10... | collective-permute-start | bytes 147464 | tf_op jit(solution)/shard_map/ppermute | solution.py:604

commit v7 on v6

--- a/solution.py
+++ b/solution.py
@@ -250,9 +250,10 @@
 
 def consistency_kernel(
     own_ref, one_ref, two_ref, three_ref, turned_ref, scalars_ref, high_ref, low_ref,
-    kspace_hbm, mask_hbm,
-    own_out, one_out, two_out, three_out,
-    kspace_ref, mask_ref, real_ref, imag_ref, field_ref, swap_ref, sum_ref, sems,
+    kspace_hbm, mask_hbm, first_hbm, mid_hbm, last_hbm,
+    own_out, one_out, two_out, three_out, first_ref, wide_ref, last_ref,
+    kspace_ref, mask_ref, first_raw, mid_raw, last_raw, first_sum, last_sum,
+    real_ref, imag_ref, field_ref, swap_ref, sum_ref, sems,
 ):
     tiles, all_positions, slices, _, _ = turned_ref.shape
     _, coils, _, rows, columns = kspace_ref.shape
@@ -260,6 +261,9 @@
     copies = [
         pltpu.make_async_copy(kspace_hbm, kspace_ref, sems.at[0]),
         pltpu.make_async_copy(mask_hbm, mask_ref, sems.at[1]),
+        pltpu.make_async_copy(first_hbm, first_raw, sems.at[2]),
+        pltpu.make_async_copy(mid_hbm, mid_raw, sems.at[3]),
+        pltpu.make_async_copy(last_hbm, last_raw, sems.at[4]),
     ]
     for copy in copies:
         copy.start()
@@ -343,8 +347,11 @@
 
     for half in halves:
         collapse(half)
-    for half in halves:
-        project(half)
+    project(halves[0])
+    fill_weights(
+        first_raw, mid_raw, last_raw, first_sum, last_sum, first_ref, wide_ref, last_ref
+    )
+    project(halves[1])
     for half in halves:
         combine(half)
 
@@ -354,48 +361,64 @@
         outs[x][p] = pltpu.roll(sum_ref[k], back_shift, 2).astype(jnp.bfloat16)
 
 
-def partial_consistency(images, prepared, measured_kspace, sample_mask):
+def partial_consistency(
+    images, prepared, measured_kspace, sample_mask, weight_in, weight_mid, weight_out
+):
     tiles, all_positions, slices, _, _ = prepared[0].shape
     _, coils, _, rows, columns = measured_kspace.shape
+    channels = weight_mid.shape[0]
+    first = jnp.transpose(weight_in, (2, 3, 4, 1, 0))
+    mid = jnp.transpose(weight_mid, (2, 3, 4, 0, 1))
+    last = jnp.transpose(weight_out, (2, 3, 4, 0, 1))
     doubled = 2 * rows
     total = slices * coils * doubled
+    f32, bf16 = jnp.float32, jnp.bfloat16
     hbm = pl.BlockSpec(memory_space=pltpu.HBM)
     vmem = pl.BlockSpec(memory_space=pltpu.VMEM)
     image_shape = (tiles, all_positions, slices, doubled, 128)
-    part = jax.ShapeDtypeStruct((all_positions // 4, slices, doubled, columns), jnp.bfloat16)
-    return pl.pallas_call(
+    part = jax.ShapeDtypeStruct((all_positions // 4, slices, doubled, columns), bf16)
+    *sums, first, mid, last = pl.pallas_call(
         consistency_kernel,
-        out_shape=(part,) * 4,
-        in_specs=[vmem] * 8 + [hbm] * 2,
-        out_specs=(vmem,) * 4,
+        out_shape=(part,) * 4
+        + (
+            jax.ShapeDtypeStruct((4 * channels, 144), bf16),
+            jax.ShapeDtypeStruct((6 * channels, 12 * channels), bf16),
+            jax.ShapeDtypeStruct((72, 6 * channels), bf16),
+        ),
+        in_specs=[vmem] * 8 + [hbm] * 5,
+        out_specs=(vmem,) * 7,
         scratch_shapes=[
-            pltpu.VMEM(measured_kspace.shape, jnp.float32),
+            pltpu.VMEM(measured_kspace.shape, f32),
             pltpu.VMEM(sample_mask.shape, jnp.int32),
-            pltpu.VMEM(image_shape, jnp.float32),
-            pltpu.VMEM(image_shape, jnp.float32),
-            pltpu.VMEM((total, columns), jnp.float32),
-            pltpu.VMEM((total, columns), jnp.float32),
-            pltpu.VMEM((all_positions, slices, doubled, columns), jnp.float32),
-            pltpu.SemaphoreType.DMA((2,)),
+            pltpu.VMEM(first.shape, bf16),
+            pltpu.VMEM(mid.shape, bf16),
+            pltpu.VMEM(last.shape, bf16),
+            pltpu.VMEM((256, 4 * channels), f32),
+            pltpu.VMEM((72, 6 * channels), f32),
+            pltpu.VMEM(image_shape, f32),
+            pltpu.VMEM(image_shape, f32),
+            pltpu.VMEM((total, columns), f32),
+            pltpu.VMEM((total, columns), f32),
+            pltpu.VMEM((all_positions, slices, doubled, columns), f32),
+            pltpu.SemaphoreType.DMA((5,)),
         ],
         compiler_params=pltpu.CompilerParams(vmem_limit_bytes=40 * 2**20),
         cost_estimate=pl.CostEstimate(
             flops=4 * 10**9, bytes_accessed=4 * 10**6, transcendentals=0
         ),
-    )(*images, *prepared, *in_hbm(measured_kspace, sample_mask))
+    )(*images, *prepared, *in_hbm(measured_kspace, sample_mask, first, mid, last))
+    return sums, (first, mid, last)
 
 
 def network_kernel(
-    window_ref, scalars_ref, first_hbm, mid_hbm, last_hbm, image_hbm, noise_hbm,
+    window_ref, scalars_ref, first_ref, wide_ref, last_ref, image_hbm, noise_hbm,
     out_ref,
-    first_raw, mid_raw, last_raw, image_ref, noise_ref,
-    first_sum, last_sum, first_ref, wide_ref, last_ref, taps_ref, f1_ref, f2_ref, part_a, part_b, score_ref, sems,
+    image_ref, noise_ref, taps_ref, f1_ref, f2_ref, part_a, part_b, score_ref, sems,
 ):
-    channels = mid_raw.shape[-1]
+    channels = first_ref.shape[0] // 4
     out_slices, _, rows, columns = out_ref.shape
     slices1, slices2 = out_slices + 4, out_slices + 2
     pairs = (
-        (first_hbm, first_raw), (mid_hbm, mid_raw), (last_hbm, last_raw),
         (image_hbm, image_ref), (noise_hbm, noise_ref),
     )
     copies = [pltpu.make_async_copy(src, dst, sems.at[i]) for i, (src, dst) in enumerate(pairs)]
@@ -415,12 +438,6 @@
         taps_ref[g, 0] = moved_right(base).astype(jnp.bfloat16)
         taps_ref[g, 1] = window_ref[g]
         taps_ref[g, 2] = moved_left(base).astype(jnp.bfloat16)
-
-    for copy in copies[:3]:
-        copy.wait()
-    fill_weights(
-        first_raw, mid_raw, last_raw, first_sum, last_sum, first_ref, wide_ref, last_ref
-    )
 
     def first_layer(z):
         source = jnp.concatenate(
@@ -491,8 +508,31 @@
         source = jnp.concatenate([f2_ref[z], f2_ref[z + 1]], axis=1)
         score_ref[z // 2] = jnp.dot(last_ref[...], source, preferred_element_type=jnp.float32)
 
+    def finish(first_slice, end):
+        for z in range(max(first_slice, 0), end):
+            taps = []
+            for t in range(3):
+                total = None
+                for d in range(3):
+                    row, first = (3 * d + t) * 8, columns * ((z + d) % 2)
+                    piece = score_ref[(z + d) // 2, row : row + 8, first : first + columns]
+                    total = piece if total is None else total + piece
+                taps.append(total)
+            score = size * (moved_right(taps[0]) + taps[1] + moved_left(taps[2]))
+            for part in range(2):
+                out_ref[z, part] = (
+                    image_ref[z, part]
+                    + score[part * rows : (part + 1) * rows]
+                    + noise_scale * noise_ref[z, part]
+                )
+
     for z in range(4):
         first_layer(z)
+    for copy in copies:
+        copy.wait()
+    size = scalars_ref[scalars_ref.shape[0] - 1 :, :]
+    size = jnp.concatenate([size] * (columns // 128), axis=1)
+    noise_scale = jnp.sqrt(2.0 * size)
     waiting = None
     parts = (part_a, part_b)
     count = 0
@@ -505,41 +545,16 @@
                 second_layer(*waiting)
                 if waiting[1] == 2:
                     third_product(waiting[0])
+                    finish(waiting[0] - 2, waiting[0])
             waiting = (z, pair, parts[count % 2])
             count += 1
     second_layer(*waiting)
     third_product(waiting[0])
-
-    for copy in copies[3:]:
-        copy.wait()
-    size = scalars_ref[scalars_ref.shape[0] - 1 :, :]
-    size = jnp.concatenate([size] * (columns // 128), axis=1)
-    noise_scale = jnp.sqrt(2.0 * size)
-    for z in range(out_slices):
-        taps = []
-        for t in range(3):
-            total = None
-            for d in range(3):
-                row, first = (3 * d + t) * 8, columns * ((z + d) % 2)
-                piece = score_ref[(z + d) // 2, row : row + 8, first : first + columns]
-                total = piece if total is None else total + piece
-            taps.append(total)
-        score = size * (moved_right(taps[0]) + taps[1] + moved_left(taps[2]))
-        for part in range(2):
-            out_ref[z, part] = (
-                image_ref[z, part]
-                + score[part * rows : (part + 1) * rows]
-                + noise_scale * noise_ref[z, part]
-            )
-
-
-def stepped_without_data(
-    windows, scalars, current_image, langevin_noise, weight_in, weight_mid, weight_out
-):
-    channels = weight_mid.shape[0]
-    first = jnp.transpose(weight_in, (2, 3, 4, 1, 0))
-    mid = jnp.transpose(weight_mid, (2, 3, 4, 0, 1))
-    last = jnp.transpose(weight_out, (2, 3, 4, 0, 1))
+    finish(waiting[0] - 2, out_slices)
+
+
+def stepped_without_data(windows, scalars, weights, current_image, langevin_noise):
+    channels = weights[0].shape[0] // 4
     slices0, columns = windows.shape[1] // 16, windows.shape[-1]
     out_slices = slices0 - 6
     local = (out_slices,) + current_image.shape[2:]
@@ -548,34 +563,26 @@
     return pl.pallas_call(
         network_kernel,
         out_shape=jax.ShapeDtypeStruct(local, jnp.float32),
-        in_specs=[vmem] * 2 + [hbm] * 5,
+        in_specs=[vmem] * 5 + [hbm] * 2,
         out_specs=vmem,
         scratch_shapes=[
-            pltpu.VMEM(first.shape, jnp.bfloat16),
-            pltpu.VMEM(mid.shape, jnp.bfloat16),
-            pltpu.VMEM(last.shape, jnp.bfloat16),
             pltpu.VMEM(local, jnp.float32),
             pltpu.VMEM(local, jnp.float32),
-            pltpu.VMEM((256, 4 * channels), jnp.float32),
-            pltpu.VMEM((72, 6 * channels), jnp.float32),
-            pltpu.VMEM((4 * channels, 144), jnp.bfloat16),
-            pltpu.VMEM((6 * channels, 12 * channels), jnp.bfloat16),
-            pltpu.VMEM((72, 6 * channels), jnp.bfloat16),
             pltpu.VMEM((2, 3, slices0 * 16, columns), jnp.bfloat16),
             pltpu.VMEM((out_slices + 4, 8 * channels, columns), jnp.bfloat16),
             pltpu.VMEM((out_slices + 2, 6 * channels, columns), jnp.bfloat16),
             pltpu.VMEM((6 * channels, 2 * columns), jnp.float32),
             pltpu.VMEM((6 * channels, 2 * columns), jnp.float32),
             pltpu.VMEM((out_slices // 2 + 1, 72, 2 * columns), jnp.float32),
-            pltpu.SemaphoreType.DMA((5,)),
+            pltpu.SemaphoreType.DMA((2,)),
         ],
         compiler_params=pltpu.CompilerParams(vmem_limit_bytes=40 * 2**20),
         cost_estimate=pl.CostEstimate(
             flops=10**10, bytes_accessed=2 * 10**6, transcendentals=4 * 10**6
         ),
     )(
-        windows, scalars,
-        *in_hbm(first, mid, last, current_image.reshape(local), langevin_noise.reshape(local)),
+        windows, scalars, *weights,
+        *in_hbm(current_image.reshape(local), langevin_noise.reshape(local)),
     ).reshape(current_image.shape)
 
 
@@ -588,7 +595,8 @@
     band, bands = lax.axis_index("band"), lax.axis_size("band")
     own = current_image.astype(jnp.bfloat16).reshape(local_slices, 2 * row_count, columns)
     routes = [[(i, i ^ x) for i in range(bands)] for x in range(1, 4)]
-    images = [own] + [lax.ppermute(own, "band", route) for route in routes]
+    across = [lax.ppermute(own, "band", route) for route in routes[1:]]
+    images = [own, lax.ppermute(own, "band", routes[0])] + across
     prepared = preparation(step_size, coil_maps, caipi_steps, band_order)
 
     odd = band % 2 == 1
@@ -599,7 +607,9 @@
     tall = jnp.concatenate([under, own, over], axis=0)
     tall = tall.reshape(-1, 2, row_count, columns)
     below, above = exchanged_rows(tall, 3)
-    sums = partial_consistency(images, prepared, measured_kspace, sample_mask)
+    sums, weights = partial_consistency(
+        images, prepared, measured_kspace, sample_mask, weight_in, weight_mid, weight_out
+    )
     sums, below, above = lax.optimization_barrier((sums, below, above))
     arrived = [lax.ppermute(part, "band", route) for part, route in zip(sums[1:], routes)]
     field = jnp.concatenate([below, tall, above, jnp.zeros_like(above[:, :, :2])], axis=2)
@@ -607,7 +617,7 @@
         [field[:, :, 4 * g : 4 * g + 8].reshape(-1, columns) for g in range(2)], axis=0
     )
     base = stepped_without_data(
-        windows, prepared[1], current_image, langevin_noise, weight_in, weight_mid, weight_out
+        windows, prepared[1], weights, current_image, langevin_noise
     )
     total = sums[0].astype(jnp.float32)
     for part in arrived:

time: 30.9 us -> 31.5 us (1.019)
  Pallas kernels: 16.8 us -> 17.5 us
    pallas_call x1, Pallas kernels: 3.77 us -> 4.21 us  [partial_consistency(): pl.pallas_call(consistency_kernel, out_shape=(part,) * 4 + (jax.ShapeDtyp...]
  transfers between devices with their start and end apart: 8 -> 8, of which waited for: 1 -> 1; matrix products, arithmetic and copies ran while one was open for 2% -> 2% of each run, Pallas kernels for 55% -> 56%
where the time goes in v7:
time: 31.5 us; the launch traced here: 31.3 us
  Pallas kernels  17.5 us (56%)
  starting transfers between devices  10.1 us (32%)
  other arithmetic  2.14 us (7%)
  between operations  0.8 us (3%)
  waiting for transfers between devices  0.66 us (2%)
    pallas_call x1, Pallas kernels, stepped_without_data(): pl.pallas_call(network_kernel, out_shape=jax.ShapeDtypeStruct(local, jnp....  11 us
    ppermute x2, starting transfers between devices, exchanged_rows(): arrived.append(lax.ppermute(sent, 'slab', route))  5.01 us
    pallas_call x1, Pallas kernels, partial_consistency(): pl.pallas_call(consistency_kernel, out_shape=(part,) * 4 + (jax.ShapeDtyp...  4.21 us
    ppermute x2, starting transfers between devices, per_device(): across = [lax.ppermute(own, 'band', route) for route in routes[1:]]  2.63 us
    pallas_call x1, Pallas kernels, preparation(): pl.pallas_call(preparation_kernel, out_shape=(jax.ShapeDtypeStruct(turned...  2.24 us
    ppermute x3, starting transfers between devices, per_device(): lax.ppermute(part, 'band', route)  1.93 us
    convert_element_type x1, other arithmetic, per_device(): current_image.astype(jnp.bfloat16)  0.91 us
    sub x1, other arithmetic, per_device(): return base - total.reshape(base.shape)  0.67 us
  transfers between devices with their start and end apart: 8, of which 1 were waited for; matrix products, arithmetic and copies ran while one was open for 2% of the time, Pallas kernels for 56%

profile of v7, /device:TPU:0, one launch (start us, length us, event | category | flops | bytes accessed | tf_op | source)
XLA Modules:
  0.0 31.3 jit_solution(7748035893797029412)
XLA Ops:
  0.0 0.9 %convert_element_type.15 = bf16[2,4,2,4,384]{4,3,2,1,0:T(4,128)(2,1)S(1)} convert(f32[2,4,2,4,384]{4,3,2,1,0:T(4,128)} %param.11) | non-fusion elementwise | flops 24576 | bytes 147456 | tf_op jit(solution)/shard_map/convert_element_type | solution.py:596
  0.9 0.5 %collective-permute-start = (bf16[8,8,384]{2,1,0:T(8,128)(2,1)S(1)}, bf16[8,8,384]{2,1,0:T(8,128)(2,1)S(1)}, u32[]{:S(2)}, u32[]{:S(2)}) collective-permute-start(bf16[8,8,384]{2,1,0:T(8,128)(2,1)S(1)} %reshape.20.own_ref), channel_id=1, source_target_pairs={{0,8},{8,0},{16,24},{24,16},{1,9},{9,1},{17,25},{25,17},{2,10},{10... | collective-permute-start | bytes 147464 | tf_op jit(solution)/shard_map/ppermute | solution.py:599
  1.5 2.6 %collective-permute-start.1 = (bf16[8,8,384]{2,1,0:T(8,128)(2,1)S(1)}, bf16[8,8,384]{2,1,0:T(8,128)(2,1)S(1)}, u32[]{:S(2)}, u32[]{:S(2)}) collective-permute-start(bf16[8,8,384]{2,1,0:T(8,128)(2,1)S(1)} %reshape.20.own_ref), channel_id=1, source_target_pairs={{0,16},{8,24},{16,0},{24,8},{1,17},{9,25},{17,1},{25,9},{2,18},{10... | collective-permute-start | bytes 147464 | tf_op jit(solution)/shard_map/ppermute | solution.py:598
  4.0 0.1 collective-permute-start.2
  4.7 2.2 %shard_map.109 = (bf16[3,8,4,64,128]{4,3,2,1,0:T(8,128)(2,1)S(1)}, f32[16,128]{1,0:T(8,128)S(1)}, bf16[384,768]{1,0:T(8,128)(2,1)S(1)}, bf16[384,768]{1,0:T(8,128)(2,1)S(1)}) custom-call(f32[1]{0:T(128)S(6)} %copy.12.size_ref, s32[8]{0:T(128)} %steps_hbm.1, s32[8]{0:T(128)} %order_hbm.1, bf16[8,4,8,2,4,384]{5,4,3,2,1,0:T(4,128)(2,1)} %coil_hbm.1), custom_call_target="tpu_custom_call" | custom-call | flops 4000000000 | bytes 4000000 | tf_op jit(solution)/shard_map/pallas_call | solution.py:226
  7.0 0.1 pad_slice_fusion
  7.1 0.0 collective-permute-done.one_ref
  7.1 0.6 %collective-permute-done.2.three_ref = bf16[8,8,384]{2,1,0:T(8,128)(2,1)S(1)} collective-permute-done((bf16[8,8,384]{2,1,0:T(8,128)(2,1)S(1)}, bf16[8,8,384]{2,1,0:T(8,128)(2,1)S(1)}, u32[]{:S(2)}, u32[]{:S(2)}) %collective-permute-start.2) | collective-permute-done | bytes 49184 | tf_op jit(solution)/shard_map/ppermute | solution.py:598
  7.8 0.1 pad_maximum_fusion.8
  7.8 0.1 broadcast_select_fusion.2
  8.0 0.7 %collective-permute-start.4 = (bf16[14,2,3,384]{3,2,1,0:T(4,128)(2,1)S(1)}, bf16[14,2,3,384]{3,2,1,0:T(4,128)(2,1)S(1)}, u32[]{:S(2)}, u32[]{:S(2)}) collective-permute-start(bf16[14,2,3,384]{3,2,1,0:T(4,128)(2,1)S(1)} %get-tuple-element.45), channel_id=1, source_target_pairs={{1,2},{2,1},{3,4},{4,3},{5,6},{6,5},{9,10},{10,9},{11,12},{12,11},... | collective-permute-start | bytes 193544 | tf_op jit(solution)/shard_map/ppermute | solution.py:22
  8.6 4.3 %collective-permute-start.3 = (bf16[14,2,3,384]{3,2,1,0:T(4,128)(2,1)S(1)}, bf16[14,2,3,384]{3,2,1,0:T(4,128)(2,1)S(1)}, u32[]{:S(2)}, u32[]{:S(2)}) collective-permute-start(bf16[14,2,3,384]{3,2,1,0:T(4,128)(2,1)S(1)} %get-tuple-element.46), channel_id=1, source_target_pairs={{0,1},{1,0},{2,3},{3,2},{4,5},{5,4},{6,7},{7,6},{8,9},{9,8},{10,11... | collective-permute-start | bytes 193544 | tf_op jit(solution)/shard_map/ppermute | solution.py:22
  13.0 0.0 collective-permute-done.1.two_ref
  13.0 4.2 %shard_map.110 = (bf16[2,4,8,384]{3,2,1,0:T(8,128)(2,1)S(1)}, bf16[2,4,8,384]{3,2,1,0:T(8,128)(2,1)S(1)}, bf16[2,4,8,384]{3,2,1,0:T(8,128)(2,1)S(1)}, bf16[2,4,8...) custom-call(bf16[8,8,384]{2,1,0:T(8,128)(2,1)S(1)} %reshape.20.own_r, ...), custom_call_target="tpu_custom_call" | custom-call | flops 4000000000 | bytes 4000000 | tf_op jit(solution)/shard_map/pallas_call | solution.py:380
  17.2 0.0 collective-permute-done.4
  17.2 0.0 collective-permute-done.3
  17.2 0.1 broadcast_select_fusion
  17.3 0.5 %collective-permute-start.7 = (bf16[2,4,8,384]{3,2,1,0:T(8,128)(2,1)S(1)}, bf16[2,4,8,384]{3,2,1,0:T(8,128)(2,1)S(1)}, u32[]{:S(2)}, u32[]{:S(2)}) collective-permute-start(bf16[2,4,8,384]{3,2,1,0:T(8,128)(2,1)S(1)} %get-tuple-element.38), channel_id=1, source_target_pairs={{0,24},{8,16},{16,8},{24,0},{1,25},{9,17},{17,9},{25,1},{2,26},{10... | collective-permute-start | bytes 147464 | tf_op jit(solution)/shard_map/ppermute | solution.py:614
  17.8 0.7 %collective-permute-start.6 = (bf16[2,4,8,384]{3,2,1,0:T(8,128)(2,1)S(1)}, bf16[2,4,8,384]{3,2,1,0:T(8,128)(2,1)S(1)}, u32[]{:S(2)}, u32[]{:S(2)}) collective-permute-start(bf16[2,4,8,384]{3,2,1,0:T(8,128)(2,1)S(1)} %get-tuple-element.37), channel_id=1, source_target_pairs={{0,16},{8,24},{16,0},{24,8},{1,17},{9,25},{17,1},{25,9},{2,18},{10... | collective-permute-start | bytes 147464 | tf_op jit(solution)/shard_map/ppermute | solution.py:614
  18.6 0.6 %collective-permute-start.5 = (bf16[2,4,8,384]{3,2,1,0:T(8,128)(2,1)S(1)}, bf16[2,4,8,384]{3,2,1,0:T(8,128)(2,1)S(1)}, u32[]{:S(2)}, u32[]{:S(2)}) collective-permute-start(bf16[2,4,8,384]{3,2,1,0:T(8,128)(2,1)S(1)} %get-tuple-element.36), channel_id=1, source_target_pairs={{0,8},{8,0},{16,24},{24,16},{1,9},{9,1},{17,25},{25,17},{2,10},{10... | collective-permute-start | bytes 147464 | tf_op jit(solution)/shard_map/ppermute | solution.py:614
  19.2 0.2 pad_maximum_fusion.4
  19.5 11.0 %shard_map.111 = f32[8,2,4,384]{3,2,1,0:T(4,128)S(1)} custom-call(bf16[2,224,384]{2,1,0:T(8,128)(2,1)S(1)} %pad_maximum_fusion.window_ref, f32[16,128]{1,0:T(8,128)S(1)} %get-tuple-element.23.scalars_ref, bf16[256,144]{1,0:T(8,128)(2,1)S(1)} %get-tuple-element.32.first_ref, bf16[384,768]{1,0:T(8,128)(2,1)S(1)} %get-tuple-element.33.wide_ref, ...), custom_call_target="tpu_custom_call" | custom-call | flops 10000000000 | bytes 2000000 | tf_op jit(solution)/shard_map/pallas_call | solution.py:563
  30.5 0.0 collective-permute-done.7
  30.5 0.0 collective-permute-done.6
  30.5 0.0 collective-permute-done.5
  30.6 0.7 %sub.3 = f32[2,4,2,4,384]{4,3,2,1,0:T(4,128)} subtract(f32[2,4,2,4,384]{4,3,2,1,0:T(4,128)S(1)} %bitcast.11, f32[2,4,2,4,384]{4,3,2,1,0:T(4,128)S(1)} %reshape.24) | non-fusion elementwise | flops 24576 | bytes 294912 | tf_op jit(solution)/shard_map/sub | solution.py:625
  (8 shorter events, 0.2 us)
Async XLA Ops:
  0.9 6.1 %collective-permute-start = (bf16[8,8,384]{2,1,0:T(8,128)(2,1)S(1)}, bf16[8,8,384]{2,1,0:T(8,128)(2,1)S(1)}, u32[]{:S(2)}, u32[]{:S(2)}) collective-permute-start(bf16[8,8,384]{2,1,0:T(8,128)(2,1)S(1)} %reshape.20.own_ref), channel_id=1, source_target_pairs={{0,8},{8,0},{16,24},{24,16},{1,9},{9,1},{17,25},{25,17},{2,10},{10... | collective-permute-start | bytes 147464 | tf_op jit(solution)/shard_map/ppermute | solution.py:599
  1.5 11.5 %collective-permute-start.1 = (bf16[8,8,384]{2,1,0:T(8,128)(2,1)S(1)}, bf16[8,8,384]{2,1,0:T(8,128)(2,1)S(1)}, u32[]{:S(2)}, u32[]{:S(2)}) collective-permute-start(bf16[8,8,384]{2,1,0:T(8,128)(2,1)S(1)} %reshape.20.own_ref), channel_id=1, source_target_pairs={{0,16},{8,24},{16,0},{24,8},{1,17},{9,25},{17,1},{25,9},{2,18},{10... | collective-permute-start | bytes 147464 | tf_op jit(solution)/shard_map/ppermute | solution.py:598
  4.0 3.7 %collective-permute-start.2 = (bf16[8,8,384]{2,1,0:T(8,128)(2,1)S(1)}, bf16[8,8,384]{2,1,0:T(8,128)(2,1)S(1)}, u32[]{:S(2)}, u32[]{:S(2)}) collective-permute-start(bf16[8,8,384]{2,1,0:T(8,128)(2,1)S(1)} %reshape.20.own_ref), channel_id=1, source_target_pairs={{0,24},{8,16},{16,8},{24,0},{1,25},{9,17},{17,9},{25,1},{2,26},{10... | collective-permute-start | bytes 147464 | tf_op jit(solution)/shard_map/ppermute | solution.py:598
  8.0 9.2 %collective-permute-start.4 = (bf16[14,2,3,384]{3,2,1,0:T(4,128)(2,1)S(1)}, bf16[14,2,3,384]{3,2,1,0:T(4,128)(2,1)S(1)}, u32[]{:S(2)}, u32[]{:S(2)}) collective-permute-start(bf16[14,2,3,384]{3,2,1,0:T(4,128)(2,1)S(1)} %get-tuple-element.45), channel_id=1, source_target_pairs={{1,2},{2,1},{3,4},{4,3},{5,6},{6,5},{9,10},{10,9},{11,12},{12,11},... | collective-permute-start | bytes 193544 | tf_op jit(solution)/shard_map/ppermute | solution.py:22
  8.6 8.6 %collective-permute-start.3 = (bf16[14,2,3,384]{3,2,1,0:T(4,128)(2,1)S(1)}, bf16[14,2,3,384]{3,2,1,0:T(4,128)(2,1)S(1)}, u32[]{:S(2)}, u32[]{:S(2)}) collective-permute-start(bf16[14,2,3,384]{3,2,1,0:T(4,128)(2,1)S(1)} %get-tuple-element.46), channel_id=1, source_target_pairs={{0,1},{1,0},{2,3},{3,2},{4,5},{5,4},{6,7},{7,6},{8,9},{9,8},{10,11... | collective-permute-start | bytes 193544 | tf_op jit(solution)/shard_map/ppermute | solution.py:22
  17.3 13.2 %collective-permute-start.7 = (bf16[2,4,8,384]{3,2,1,0:T(8,128)(2,1)S(1)}, bf16[2,4,8,384]{3,2,1,0:T(8,128)(2,1)S(1)}, u32[]{:S(2)}, u32[]{:S(2)}) collective-permute-start(bf16[2,4,8,384]{3,2,1,0:T(8,128)(2,1)S(1)} %get-tuple-element.38), channel_id=1, source_target_pairs={{0,24},{8,16},{16,8},{24,0},{1,25},{9,17},{17,9},{25,1},{2,26},{10... | collective-permute-start | bytes 147464 | tf_op jit(solution)/shard_map/ppermute | solution.py:614
  17.8 12.7 %collective-permute-start.6 = (bf16[2,4,8,384]{3,2,1,0:T(8,128)(2,1)S(1)}, bf16[2,4,8,384]{3,2,1,0:T(8,128)(2,1)S(1)}, u32[]{:S(2)}, u32[]{:S(2)}) collective-permute-start(bf16[2,4,8,384]{3,2,1,0:T(8,128)(2,1)S(1)} %get-tuple-element.37), channel_id=1, source_target_pairs={{0,16},{8,24},{16,0},{24,8},{1,17},{9,25},{17,1},{25,9},{2,18},{10... | collective-permute-start | bytes 147464 | tf_op jit(solution)/shard_map/ppermute | solution.py:614
  18.6 12.0 %collective-permute-start.5 = (bf16[2,4,8,384]{3,2,1,0:T(8,128)(2,1)S(1)}, bf16[2,4,8,384]{3,2,1,0:T(8,128)(2,1)S(1)}, u32[]{:S(2)}, u32[]{:S(2)}) collective-permute-start(bf16[2,4,8,384]{3,2,1,0:T(8,128)(2,1)S(1)} %get-tuple-element.36), channel_id=1, source_target_pairs={{0,8},{8,0},{16,24},{24,16},{1,9},{9,1},{17,25},{25,17},{2,10},{10... | collective-permute-start | bytes 147464 | tf_op jit(solution)/shard_map/ppermute | solution.py:614

commit v8 on v6

--- a/solution.py
+++ b/solution.py
@@ -13,13 +13,13 @@
     count = lax.axis_size("slab")
     odd = lax.axis_index("slab") % 2 == 1
     head, tail = tall[:, :, :width, :], tall[:, :, tall.shape[2] - width :, :]
-    arrived = []
-    for first in range(2):
+    arrived = {}
+    for first in (1, 0):
         route = []
         for i in range(first, count - 1, 2):
             route += [(i, i + 1), (i + 1, i)]
         sent = jnp.where(odd, head, tail) if first == 0 else jnp.where(odd, tail, head)
-        arrived.append(lax.ppermute(sent, "slab", route))
+        arrived[first] = lax.ppermute(sent, "slab", route)
     below = jnp.where(odd, arrived[0], arrived[1])
     above = jnp.where(odd, arrived[1], arrived[0])
     return below, above
@@ -141,7 +141,9 @@
         store(lax.rem(j + whole, tiles), jnp.where(lane < part, moved[j - 1], moved[j]))
 
 
-def fill_weights(first_raw, mid_raw, last_raw, first_sum, last_sum, first_ref, wide_ref, last_ref):
+def fill_weights(
+    first_raw, mid_raw, last_raw, first_sum, last_sum, form_ref, first_ref, wide_ref, last_ref
+):
     channels = mid_raw.shape[-1]
     two = 2 * channels
     first_sum[...] = jnp.zeros_like(first_sum)
@@ -164,21 +166,26 @@
                         last_sum[row : row + 1, col : col + channels] = block[o : o + 1]
     first_ref[...] = first_sum[...].T[:, : first_ref.shape[1]].astype(jnp.bfloat16)
     last_ref[...] = last_sum[...].astype(jnp.bfloat16)
-    half_weight = jnp.bfloat16(0.5)
-    for t in range(3):
-        for r in range(2):
-            row = (t * 2 + r) * channels
-            for d in range(3):
+    for u in range(3):
+        for t in range(3):
+            low, mid, high = (0.5 * mid_raw[d, u, t].astype(jnp.float32) for d in range(3))
+            ends = 0.5 * (low + high)
+            forms = (low, ends + 0.5 * mid, ends - 0.5 * mid, high)
+            for k, form in enumerate(forms):
+                form_ref[k, t, u] = form.astype(jnp.bfloat16)
+    for k in range(4):
+        for t in range(3):
+            for r in range(2):
+                row = (t * 2 + r) * channels
                 for pair in range(2):
                     blocks = []
                     for q in (2 * pair, 2 * pair + 1):
                         if 0 <= q - r <= 2:
-                            blocks.append(mid_raw[d, q - r, t] * half_weight)
+                            blocks.append(form_ref[k, t, q - r])
                         else:
                             blocks.append(jnp.zeros((channels, channels), jnp.bfloat16))
-                    col = (d * 4 + 2 * pair) * channels
-                    wide_ref[row : row + channels, col : col + two] = jnp.concatenate(
-                        blocks, axis=1
+                    wide_ref[k, row : row + channels, two * pair : two * (pair + 1)] = (
+                        jnp.concatenate(blocks, axis=1)
                     )
 
 
@@ -389,7 +396,8 @@
     window_ref, scalars_ref, first_hbm, mid_hbm, last_hbm, image_hbm, noise_hbm,
     out_ref,
     first_raw, mid_raw, last_raw, image_ref, noise_ref,
-    first_sum, last_sum, first_ref, wide_ref, last_ref, taps_ref, f1_ref, f2_ref, part_a, part_b, score_ref, sems,
+    first_sum, last_sum, form_ref, first_ref, wide_ref, last_ref, taps_ref, f1_ref, form1_ref, f2_ref,
+    part_a, part_b, score_ref, sems,
 ):
     channels = mid_raw.shape[-1]
     out_slices, _, rows, columns = out_ref.shape
@@ -409,6 +417,7 @@
     low_slice, high_slice = inside("band", False), inside("band", True)
     low_row, high_row = inside("slab", False), inside("slab", True)
     four, two = 4 * channels, 2 * channels
+    parts = (part_a, part_b)
 
     for g in range(2):
         base = window_ref[g].astype(jnp.float32)
@@ -419,7 +428,7 @@
     for copy in copies[:3]:
         copy.wait()
     fill_weights(
-        first_raw, mid_raw, last_raw, first_sum, last_sum, first_ref, wide_ref, last_ref
+        first_raw, mid_raw, last_raw, first_sum, last_sum, form_ref, first_ref, wide_ref, last_ref
     )
 
     def first_layer(z):
@@ -448,30 +457,40 @@
                 value = value * factor
             f1_ref[z, r * channels : (r + 1) * channels, :] = value.astype(jnp.bfloat16)
 
-    def second_product(z, pair, part_ref):
+    def transform(z):
+        layers = [f1_ref[z + d] for d in range(4)]
+        forms = (
+            layers[0] - layers[2],
+            layers[1] + layers[2],
+            layers[2] - layers[1],
+            layers[1] - layers[3],
+        )
+        for k, form in enumerate(forms):
+            form1_ref[z // 2 % 2, k] = form
+
+    def second_product(z, k):
         source = jnp.concatenate(
-            [
-                f1_ref[z + a : z + a + 3, two * pair : two * pair + four, :].reshape(
-                    3 * four, columns
-                )
-                for a in range(2)
-            ],
+            [form1_ref[z // 2 % 2, k, two * pair : two * pair + four, :] for pair in range(3)],
             axis=1,
         )
-        part_ref[...] = jnp.dot(wide_ref[...], source, preferred_element_type=jnp.float32)
-
-    def second_layer(z, pair, part_ref):
-        for a in range(2):
-            first = columns * a
-            for r in range(2):
-                row = r * channels
-                half = (
-                    moved_right(part_ref[row : row + channels, first : first + columns])
-                    + part_ref[two + row : two + row + channels, first : first + columns]
-                    + moved_left(
-                        part_ref[four + row : four + row + channels, first : first + columns]
-                    )
+        parts[z // 2 % 2][k] = jnp.dot(
+            wide_ref[k], source, preferred_element_type=jnp.float32
+        )
+
+    def second_layer(z, pair):
+        part_ref = parts[z // 2 % 2]
+        lanes = slice(columns * pair, columns * (pair + 1))
+        for r in range(2):
+            sums = ([], [])
+            for t in range(3):
+                row = t * two + r * channels
+                one, two_, three, four_ = (
+                    part_ref[k, row : row + channels, lanes] for k in range(4)
                 )
+                sums[0].append(one + two_ + three)
+                sums[1].append(two_ - three - four_)
+            for a in range(2):
+                half = moved_right(sums[a][0]) + sums[a][1] + moved_left(sums[a][2])
                 value = half_silu(half)
                 factors = []
                 if z + a == 0:
@@ -493,22 +512,28 @@
 
     for z in range(4):
         first_layer(z)
-    waiting = None
-    parts = (part_a, part_b)
-    count = 0
+    transform(0)
     for z in range(0, slices2, 2):
-        for pair in range(3):
-            second_product(z, pair, parts[count % 2])
-            if pair < 2 and z + 4 + pair < slices1:
-                first_layer(z + 4 + pair)
-            if waiting is not None:
-                second_layer(*waiting)
-                if waiting[1] == 2:
-                    third_product(waiting[0])
-            waiting = (z, pair, parts[count % 2])
-            count += 1
-    second_layer(*waiting)
-    third_product(waiting[0])
+        later = z + 4
+        second_product(z, 0)
+        if later < slices1:
+            first_layer(later)
+        second_product(z, 1)
+        if later + 1 < slices1:
+            first_layer(later + 1)
+        second_product(z, 2)
+        if z > 0:
+            second_layer(z - 2, 0)
+            second_layer(z - 2, 1)
+        second_product(z, 3)
+        if z > 0:
+            second_layer(z - 2, 2)
+            third_product(z - 2)
+        if later < slices1:
+            transform(z + 2)
+    for pair in range(3):
+        second_layer(slices2 - 2, pair)
+    third_product(slices2 - 2)
 
     for copy in copies[3:]:
         copy.wait()
@@ -558,14 +583,16 @@
             pltpu.VMEM(local, jnp.float32),
             pltpu.VMEM((256, 4 * channels), jnp.float32),
             pltpu.VMEM((72, 6 * channels), jnp.float32),
+            pltpu.VMEM((4, 3, 3, channels, channels), jnp.bfloat16),
             pltpu.VMEM((4 * channels, 144), jnp.bfloat16),
-            pltpu.VMEM((6 * channels, 12 * channels), jnp.bfloat16),
+            pltpu.VMEM((4, 6 * channels, 4 * channels), jnp.bfloat16),
             pltpu.VMEM((72, 6 * channels), jnp.bfloat16),
             pltpu.VMEM((2, 3, slices0 * 16, columns), jnp.bfloat16),
             pltpu.VMEM((out_slices + 4, 8 * channels, columns), jnp.bfloat16),
+            pltpu.VMEM((2, 4, 8 * channels, columns), jnp.bfloat16),
             pltpu.VMEM((out_slices + 2, 6 * channels, columns), jnp.bfloat16),
-            pltpu.VMEM((6 * channels, 2 * columns), jnp.float32),
-            pltpu.VMEM((6 * channels, 2 * columns), jnp.float32),
+            pltpu.VMEM((4, 6 * channels, 3 * columns), jnp.float32),
+            pltpu.VMEM((4, 6 * channels, 3 * columns), jnp.float32),
             pltpu.VMEM((out_slices // 2 + 1, 72, 2 * columns), jnp.float32),
             pltpu.SemaphoreType.DMA((5,)),
         ],

time: 30.9 us -> 31.2 us (level)
    pallas_call x1, Pallas kernels: 10.8 us -> 11.1 us  [stepped_without_data(): pl.pallas_call(network_kernel, out_shape=jax.ShapeDtypeStruct(local, jnp....]
where the time goes in v8:
time: 31.2 us; the launch traced here: 31 us
  Pallas kernels  17.1 us (55%)
  starting transfers between devices  10.1 us (32%)
  other arithmetic  2.14 us (7%)
  between operations  0.8 us (3%)
  waiting for transfers between devices  0.66 us (2%)
    pallas_call x1, Pallas kernels, stepped_without_data(): pl.pallas_call(network_kernel, out_shape=jax.ShapeDtypeStruct(local, jnp....  11.1 us
    ppermute x2, starting transfers between devices, exchanged_rows(): arrived[first] = lax.ppermute(sent, 'slab', route)  5.01 us
    pallas_call x1, Pallas kernels, partial_consistency(): pl.pallas_call(consistency_kernel, out_shape=(part,) * 4, in_specs=[vmem]...  3.77 us
    ppermute x3, starting transfers between devices, per_device(): images = [own] + [lax.ppermute(own, 'band', route) for route in routes]  3.15 us
    pallas_call x1, Pallas kernels, preparation(): pl.pallas_call(preparation_kernel, out_shape=(jax.ShapeDtypeStruct(turned...  2.24 us
    ppermute x3, starting transfers between devices, per_device(): lax.ppermute(part, 'band', route)  1.93 us
    convert_element_type x1, other arithmetic, per_device(): current_image.astype(jnp.bfloat16)  0.91 us
    sub x1, other arithmetic, per_device(): return base - total.reshape(base.shape)  0.67 us
  transfers between devices with their start and end apart: 8, of which 1 were waited for; matrix products, arithmetic and copies ran while one was open for 2% of the time, Pallas kernels for 55%

profile of v8, /device:TPU:0, one launch (start us, length us, event | category | flops | bytes accessed | tf_op | source)
XLA Modules:
  0.0 31.0 jit_solution(13009616682826539180)
XLA Ops:
  0.0 0.9 %convert_element_type.15 = bf16[2,4,2,4,384]{4,3,2,1,0:T(4,128)(2,1)S(1)} convert(f32[2,4,2,4,384]{4,3,2,1,0:T(4,128)} %param.11) | non-fusion elementwise | flops 24576 | bytes 147456 | tf_op jit(solution)/shard_map/convert_element_type | solution.py:616
  0.9 0.5 %collective-permute-start = (bf16[8,8,384]{2,1,0:T(8,128)(2,1)S(1)}, bf16[8,8,384]{2,1,0:T(8,128)(2,1)S(1)}, u32[]{:S(2)}, u32[]{:S(2)}) collective-permute-start(bf16[8,8,384]{2,1,0:T(8,128)(2,1)S(1)} %reshape.20.own_ref), channel_id=1, source_target_pairs={{0,8},{8,0},{16,24},{24,16},{1,9},{9,1},{17,25},{25,17},{2,10},{10... | collective-permute-start | bytes 147464 | tf_op jit(solution)/shard_map/ppermute | solution.py:618
  1.5 2.6 %collective-permute-start.1 = (bf16[8,8,384]{2,1,0:T(8,128)(2,1)S(1)}, bf16[8,8,384]{2,1,0:T(8,128)(2,1)S(1)}, u32[]{:S(2)}, u32[]{:S(2)}) collective-permute-start(bf16[8,8,384]{2,1,0:T(8,128)(2,1)S(1)} %reshape.20.own_ref), channel_id=1, source_target_pairs={{0,16},{8,24},{16,0},{24,8},{1,17},{9,25},{17,1},{25,9},{2,18},{10... | collective-permute-start | bytes 147464 | tf_op jit(solution)/shard_map/ppermute | solution.py:618
  4.0 0.1 collective-permute-start.2
  4.7 2.2 %shard_map.109 = (bf16[3,8,4,64,128]{4,3,2,1,0:T(8,128)(2,1)S(1)}, f32[16,128]{1,0:T(8,128)S(1)}, bf16[384,768]{1,0:T(8,128)(2,1)S(1)}, bf16[384,768]{1,0:T(8,128)(2,1)S(1)}) custom-call(f32[1]{0:T(128)S(6)} %copy.12.size_ref, s32[8]{0:T(128)} %steps_hbm.1, s32[8]{0:T(128)} %order_hbm.1, bf16[8,4,8,2,4,384]{5,4,3,2,1,0:T(4,128)(2,1)} %coil_hbm.1), custom_call_target="tpu_custom_call" | custom-call | flops 4000000000 | bytes 4000000 | tf_op jit(solution)/shard_map/pallas_call | solution.py:233
  7.0 0.1 pad_slice_fusion
  7.1 0.0 collective-permute-done.one_ref
  7.1 0.6 %collective-permute-done.2.three_ref = bf16[8,8,384]{2,1,0:T(8,128)(2,1)S(1)} collective-permute-done((bf16[8,8,384]{2,1,0:T(8,128)(2,1)S(1)}, bf16[8,8,384]{2,1,0:T(8,128)(2,1)S(1)}, u32[]{:S(2)}, u32[]{:S(2)}) %collective-permute-start.2) | collective-permute-done | bytes 49184 | tf_op jit(solution)/shard_map/ppermute | solution.py:618
  7.8 0.1 pad_maximum_fusion.8
  7.8 0.1 broadcast_select_fusion.2
  8.0 0.7 %collective-permute-start.4 = (bf16[14,2,3,384]{3,2,1,0:T(4,128)(2,1)S(1)}, bf16[14,2,3,384]{3,2,1,0:T(4,128)(2,1)S(1)}, u32[]{:S(2)}, u32[]{:S(2)}) collective-permute-start(bf16[14,2,3,384]{3,2,1,0:T(4,128)(2,1)S(1)} %get-tuple-element.39), channel_id=1, source_target_pairs={{1,2},{2,1},{3,4},{4,3},{5,6},{6,5},{9,10},{10,9},{11,12},{12,11},... | collective-permute-start | bytes 193544 | tf_op jit(solution)/shard_map/ppermute | solution.py:22
  8.6 4.3 %collective-permute-start.3 = (bf16[14,2,3,384]{3,2,1,0:T(4,128)(2,1)S(1)}, bf16[14,2,3,384]{3,2,1,0:T(4,128)(2,1)S(1)}, u32[]{:S(2)}, u32[]{:S(2)}) collective-permute-start(bf16[14,2,3,384]{3,2,1,0:T(4,128)(2,1)S(1)} %get-tuple-element.40), channel_id=1, source_target_pairs={{0,1},{1,0},{2,3},{3,2},{4,5},{5,4},{6,7},{7,6},{8,9},{9,8},{10,11... | collective-permute-start | bytes 193544 | tf_op jit(solution)/shard_map/ppermute | solution.py:22
  13.0 0.0 collective-permute-done.1.two_ref
  13.0 3.8 %shard_map.110 = (bf16[2,4,8,384]{3,2,1,0:T(8,128)(2,1)S(1)}, bf16[2,4,8,384]{3,2,1,0:T(8,128)(2,1)S(1)}, bf16[2,4,8,384]{3,2,1,0:T(8,128)(2,1)S(1)}, bf16[2,4,8,384]{3,2,1,0:T(8,128)(2,1)S(1)}) custom-call(bf16[8,8,384]{2,1,0:T(8,128)(2,1)S(1)} %reshape.20.own_ref, bf16[8,8,384]{2,1,0:T(8,128)(2,1)S(1)} %collective-permute-done.one_ref, ...), custom_call_target="tpu_custom_call" | custom-call | flops 4000000000 | bytes 4000000 | tf_op jit(solution)/shard_map/pallas_call | solution.py:373
  16.8 0.0 collective-permute-done.4
  16.8 0.0 collective-permute-done.3
  16.8 0.1 broadcast_select_fusion
  16.9 0.5 %collective-permute-start.7 = (bf16[2,4,8,384]{3,2,1,0:T(8,128)(2,1)S(1)}, bf16[2,4,8,384]{3,2,1,0:T(8,128)(2,1)S(1)}, u32[]{:S(2)}, u32[]{:S(2)}) collective-permute-start(bf16[2,4,8,384]{3,2,1,0:T(8,128)(2,1)S(1)} %get-tuple-element.32), channel_id=1, source_target_pairs={{0,24},{8,16},{16,8},{24,0},{1,25},{9,17},{17,9},{25,1},{2,26},{10... | collective-permute-start | bytes 147464 | tf_op jit(solution)/shard_map/ppermute | solution.py:631
  17.4 0.8 %collective-permute-start.6 = (bf16[2,4,8,384]{3,2,1,0:T(8,128)(2,1)S(1)}, bf16[2,4,8,384]{3,2,1,0:T(8,128)(2,1)S(1)}, u32[]{:S(2)}, u32[]{:S(2)}) collective-permute-start(bf16[2,4,8,384]{3,2,1,0:T(8,128)(2,1)S(1)} %get-tuple-element.31), channel_id=1, source_target_pairs={{0,16},{8,24},{16,0},{24,8},{1,17},{9,25},{17,1},{25,9},{2,18},{10... | collective-permute-start | bytes 147464 | tf_op jit(solution)/shard_map/ppermute | solution.py:631
  18.2 0.6 %collective-permute-start.5 = (bf16[2,4,8,384]{3,2,1,0:T(8,128)(2,1)S(1)}, bf16[2,4,8,384]{3,2,1,0:T(8,128)(2,1)S(1)}, u32[]{:S(2)}, u32[]{:S(2)}) collective-permute-start(bf16[2,4,8,384]{3,2,1,0:T(8,128)(2,1)S(1)} %get-tuple-element.30), channel_id=1, source_target_pairs={{0,8},{8,0},{16,24},{24,16},{1,9},{9,1},{17,25},{25,17},{2,10},{10... | collective-permute-start | bytes 147464 | tf_op jit(solution)/shard_map/ppermute | solution.py:631
  18.8 0.2 pad_maximum_fusion.4
  19.1 11.1 %shard_map.111 = f32[8,2,4,384]{3,2,1,0:T(4,128)S(1)} custom-call(bf16[2,224,384]{2,1,0:T(8,128)(2,1)S(1)} %pad_maximum_fusion.window_ref, f32[16,128]{1,0:T(8,128)S(1)} %get-tuple-element.20.scalars_ref, bf16[3,3,3,2,64]{4,3,2,1,0:T(2,128)(2,1)} %bitcast.19, bf16[3,3,3,64,64]{4,3,2,1,0:T(8,128)(2,1)} %bitcast.17, bf16[3,3,3,2,64]{4,3,2,1,0:T(2,128)(2,1)} %bitcast.20, ...), custom_call_target="tpu_custom_call" | custom-call | flops 10000000000 | bytes 2000000 | tf_op jit(solution)/shard_map/pallas_call | solution.py:573
  30.2 0.0 collective-permute-done.7
  30.2 0.0 collective-permute-done.6
  30.2 0.0 collective-permute-done.5
  30.3 0.7 %sub.3 = f32[2,4,2,4,384]{4,3,2,1,0:T(4,128)} subtract(f32[2,4,2,4,384]{4,3,2,1,0:T(4,128)S(1)} %bitcast.11, f32[2,4,2,4,384]{4,3,2,1,0:T(4,128)S(1)} %reshape.24) | non-fusion elementwise | flops 24576 | bytes 294912 | tf_op jit(solution)/shard_map/sub | solution.py:642
  (8 shorter events, 0.2 us)
Async XLA Ops:
  0.9 6.1 %collective-permute-start = (bf16[8,8,384]{2,1,0:T(8,128)(2,1)S(1)}, bf16[8,8,384]{2,1,0:T(8,128)(2,1)S(1)}, u32[]{:S(2)}, u32[]{:S(2)}) collective-permute-start(bf16[8,8,384]{2,1,0:T(8,128)(2,1)S(1)} %reshape.20.own_ref), channel_id=1, source_target_pairs={{0,8},{8,0},{16,24},{24,16},{1,9},{9,1},{17,25},{25,17},{2,10},{10... | collective-permute-start | bytes 147464 | tf_op jit(solution)/shard_map/ppermute | solution.py:618
  1.5 11.5 %collective-permute-start.1 = (bf16[8,8,384]{2,1,0:T(8,128)(2,1)S(1)}, bf16[8,8,384]{2,1,0:T(8,128)(2,1)S(1)}, u32[]{:S(2)}, u32[]{:S(2)}) collective-permute-start(bf16[8,8,384]{2,1,0:T(8,128)(2,1)S(1)} %reshape.20.own_ref), channel_id=1, source_target_pairs={{0,16},{8,24},{16,0},{24,8},{1,17},{9,25},{17,1},{25,9},{2,18},{10... | collective-permute-start | bytes 147464 | tf_op jit(solution)/shard_map/ppermute | solution.py:618
  4.0 3.7 %collective-permute-start.2 = (bf16[8,8,384]{2,1,0:T(8,128)(2,1)S(1)}, bf16[8,8,384]{2,1,0:T(8,128)(2,1)S(1)}, u32[]{:S(2)}, u32[]{:S(2)}) collective-permute-start(bf16[8,8,384]{2,1,0:T(8,128)(2,1)S(1)} %reshape.20.own_ref), channel_id=1, source_target_pairs={{0,24},{8,16},{16,8},{24,0},{1,25},{9,17},{17,9},{25,1},{2,26},{10... | collective-permute-start | bytes 147464 | tf_op jit(solution)/shard_map/ppermute | solution.py:618
  8.0 8.8 %collective-permute-start.4 = (bf16[14,2,3,384]{3,2,1,0:T(4,128)(2,1)S(1)}, bf16[14,2,3,384]{3,2,1,0:T(4,128)(2,1)S(1)}, u32[]{:S(2)}, u32[]{:S(2)}) collective-permute-start(bf16[14,2,3,384]{3,2,1,0:T(4,128)(2,1)S(1)} %get-tuple-element.39), channel_id=1, source_target_pairs={{1,2},{2,1},{3,4},{4,3},{5,6},{6,5},{9,10},{10,9},{11,12},{12,11},... | collective-permute-start | bytes 193544 | tf_op jit(solution)/shard_map/ppermute | solution.py:22
  8.6 8.1 %collective-permute-start.3 = (bf16[14,2,3,384]{3,2,1,0:T(4,128)(2,1)S(1)}, bf16[14,2,3,384]{3,2,1,0:T(4,128)(2,1)S(1)}, u32[]{:S(2)}, u32[]{:S(2)}) collective-permute-start(bf16[14,2,3,384]{3,2,1,0:T(4,128)(2,1)S(1)} %get-tuple-element.40), channel_id=1, source_target_pairs={{0,1},{1,0},{2,3},{3,2},{4,5},{5,4},{6,7},{7,6},{8,9},{9,8},{10,11... | collective-permute-start | bytes 193544 | tf_op jit(solution)/shard_map/ppermute | solution.py:22
  16.9 13.3 %collective-permute-start.7 = (bf16[2,4,8,384]{3,2,1,0:T(8,128)(2,1)S(1)}, bf16[2,4,8,384]{3,2,1,0:T(8,128)(2,1)S(1)}, u32[]{:S(2)}, u32[]{:S(2)}) collective-permute-start(bf16[2,4,8,384]{3,2,1,0:T(8,128)(2,1)S(1)} %get-tuple-element.32), channel_id=1, source_target_pairs={{0,24},{8,16},{16,8},{24,0},{1,25},{9,17},{17,9},{25,1},{2,26},{10... | collective-permute-start | bytes 147464 | tf_op jit(solution)/shard_map/ppermute | solution.py:631
  17.4 12.8 %collective-permute-start.6 = (bf16[2,4,8,384]{3,2,1,0:T(8,128)(2,1)S(1)}, bf16[2,4,8,384]{3,2,1,0:T(8,128)(2,1)S(1)}, u32[]{:S(2)}, u32[]{:S(2)}) collective-permute-start(bf16[2,4,8,384]{3,2,1,0:T(8,128)(2,1)S(1)} %get-tuple-element.31), channel_id=1, source_target_pairs={{0,16},{8,24},{16,0},{24,8},{1,17},{9,25},{17,1},{25,9},{2,18},{10... | collective-permute-start | bytes 147464 | tf_op jit(solution)/shard_map/ppermute | solution.py:631
  18.2 12.1 %collective-permute-start.5 = (bf16[2,4,8,384]{3,2,1,0:T(8,128)(2,1)S(1)}, bf16[2,4,8,384]{3,2,1,0:T(8,128)(2,1)S(1)}, u32[]{:S(2)}, u32[]{:S(2)}) collective-permute-start(bf16[2,4,8,384]{3,2,1,0:T(8,128)(2,1)S(1)} %get-tuple-element.30), channel_id=1, source_target_pairs={{0,8},{8,0},{16,24},{24,16},{1,9},{9,1},{17,25},{25,17},{2,10},{10... | collective-permute-start | bytes 147464 | tf_op jit(solution)/shard_map/ppermute | solution.py:631

commit v9 on v6

--- a/solution.py
+++ b/solution.py
@@ -98,8 +98,8 @@
     )
 
 
-def half_silu(half):
-    return half + half * jnp.tanh(half)
+def silu(value):
+    return value * pl.reciprocal(1.0 + jnp.exp(-value), approx=True)
 
 
 def table_product(source, high_ref, low_ref):
@@ -149,7 +149,7 @@
     for d in range(3):
         for u in range(3):
             for t in range(3):
-                block = first_raw[d, u, t].astype(jnp.float32) * 0.5
+                block = first_raw[d, u, t].astype(jnp.float32)
                 for i in range(2):
                     for r in range(4):
                         row = (t * 3 + d) * 16 + i * 8 + u + r
@@ -164,7 +164,6 @@
                         last_sum[row : row + 1, col : col + channels] = block[o : o + 1]
     first_ref[...] = first_sum[...].T[:, : first_ref.shape[1]].astype(jnp.bfloat16)
     last_ref[...] = last_sum[...].astype(jnp.bfloat16)
-    half_weight = jnp.bfloat16(0.5)
     for t in range(3):
         for r in range(2):
             row = (t * 2 + r) * channels
@@ -173,7 +172,7 @@
                     blocks = []
                     for q in (2 * pair, 2 * pair + 1):
                         if 0 <= q - r <= 2:
-                            blocks.append(mid_raw[d, q - r, t] * half_weight)
+                            blocks.append(mid_raw[d, q - r, t])
                         else:
                             blocks.append(jnp.zeros((channels, channels), jnp.bfloat16))
                     col = (d * 4 + 2 * pair) * channels
@@ -434,7 +433,7 @@
         for r in range(8):
             begin = (r % 4) * channels
             first = columns * (r // 4)
-            value = half_silu(half[begin : begin + channels, first : first + columns])
+            value = silu(half[begin : begin + channels, first : first + columns])
             factors = []
             if z < 2:
                 factors.append(low_slice)
@@ -472,7 +471,7 @@
                         part_ref[four + row : four + row + channels, first : first + columns]
                     )
                 )
-                value = half_silu(half)
+                value = silu(half)
                 factors = []
                 if z + a == 0:
                     factors.append(low_slice)

time: 30.9 us -> 31.3 us (1.013)
  Pallas kernels: 16.8 us -> 17.2 us
    pallas_call x1, Pallas kernels: 10.8 us -> 11.2 us  [stepped_without_data(): pl.pallas_call(network_kernel, out_shape=jax.ShapeDtypeStruct(local, jnp....]
where the time goes in v9:
time: 31.3 us; the launch traced here: 31 us
  Pallas kernels  17.2 us (55%)
  starting transfers between devices  10.1 us (32%)
  other arithmetic  2.14 us (7%)
  between operations  0.8 us (3%)
  waiting for transfers between devices  0.66 us (2%)
    pallas_call x1, Pallas kernels, stepped_without_data(): pl.pallas_call(network_kernel, out_shape=jax.ShapeDtypeStruct(local, jnp....  11.2 us
    ppermute x2, starting transfers between devices, exchanged_rows(): arrived.append(lax.ppermute(sent, 'slab', route))  5.01 us
    pallas_call x1, Pallas kernels, partial_consistency(): pl.pallas_call(consistency_kernel, out_shape=(part,) * 4, in_specs=[vmem]...  3.77 us
    ppermute x3, starting transfers between devices, per_device(): images = [own] + [lax.ppermute(own, 'band', route) for route in routes]  3.15 us
    pallas_call x1, Pallas kernels, preparation(): pl.pallas_call(preparation_kernel, out_shape=(jax.ShapeDtypeStruct(turned...  2.24 us
    ppermute x3, starting transfers between devices, per_device(): lax.ppermute(part, 'band', route)  1.93 us
    convert_element_type x1, other arithmetic, per_device(): current_image.astype(jnp.bfloat16)  0.91 us
    sub x1, other arithmetic, per_device(): return base - total.reshape(base.shape)  0.67 us
  transfers between devices with their start and end apart: 8, of which 1 were waited for; matrix products, arithmetic and copies ran while one was open for 2% of the time, Pallas kernels for 55%

profile of v9, /device:TPU:0, one launch (start us, length us, event | category | flops | bytes accessed | tf_op | source)
XLA Modules:
  0.0 31.0 jit_solution(11365166529330249344)
XLA Ops:
  0.0 0.9 %convert_element_type.15 = bf16[2,4,2,4,384]{4,3,2,1,0:T(4,128)(2,1)S(1)} convert(f32[2,4,2,4,384]{4,3,2,1,0:T(4,128)} %param.11) | non-fusion elementwise | flops 24576 | bytes 147456 | tf_op jit(solution)/shard_map/convert_element_type | solution.py:588
  0.9 0.5 %collective-permute-start = (bf16[8,8,384]{2,1,0:T(8,128)(2,1)S(1)}, bf16[8,8,384]{2,1,0:T(8,128)(2,1)S(1)}, u32[]{:S(2)}, u32[]{:S(2)}) collective-permute-start(bf16[8,8,384]{2,1,0:T(8,128)(2,1)S(1)} %reshape.20.own_ref), channel_id=1, source_target_pairs={{0,8},{8,0},{16,24},{24,16},{1,9},{9,1},{17,25},{25,17},{2,10},{10... | collective-permute-start | bytes 147464 | tf_op jit(solution)/shard_map/ppermute | solution.py:590
  1.5 2.6 %collective-permute-start.1 = (bf16[8,8,384]{2,1,0:T(8,128)(2,1)S(1)}, bf16[8,8,384]{2,1,0:T(8,128)(2,1)S(1)}, u32[]{:S(2)}, u32[]{:S(2)}) collective-permute-start(bf16[8,8,384]{2,1,0:T(8,128)(2,1)S(1)} %reshape.20.own_ref), channel_id=1, source_target_pairs={{0,16},{8,24},{16,0},{24,8},{1,17},{9,25},{17,1},{25,9},{2,18},{10... | collective-permute-start | bytes 147464 | tf_op jit(solution)/shard_map/ppermute | solution.py:590
  4.0 0.1 collective-permute-start.2
  4.7 2.2 %shard_map.109 = (bf16[3,8,4,64,128]{4,3,2,1,0:T(8,128)(2,1)S(1)}, f32[16,128]{1,0:T(8,128)S(1)}, bf16[384,768]{1,0:T(8,128)(2,1)S(1)}, bf16[384,768]{1,0:T(8,128)(2,1)S(1)}) custom-call(f32[1]{0:T(128)S(6)} %copy.12.size_ref, s32[8]{0:T(128)} %steps_hbm.1, s32[8]{0:T(128)} %order_hbm.1, bf16[8,4,8,2,4,384]{5,4,3,2,1,0:T(4,128)(2,1)} %coil_hbm.1), custom_call_target="tpu_custom_call" | custom-call | flops 4000000000 | bytes 4000000 | tf_op jit(solution)/shard_map/pallas_call | solution.py:225
  7.0 0.1 pad_slice_fusion
  7.1 0.0 collective-permute-done.one_ref
  7.1 0.6 %collective-permute-done.2.three_ref = bf16[8,8,384]{2,1,0:T(8,128)(2,1)S(1)} collective-permute-done((bf16[8,8,384]{2,1,0:T(8,128)(2,1)S(1)}, bf16[8,8,384]{2,1,0:T(8,128)(2,1)S(1)}, u32[]{:S(2)}, u32[]{:S(2)}) %collective-permute-start.2) | collective-permute-done | bytes 49184 | tf_op jit(solution)/shard_map/ppermute | solution.py:590
  7.8 0.1 pad_maximum_fusion.8
  7.8 0.1 broadcast_select_fusion.2
  8.0 0.7 %collective-permute-start.4 = (bf16[14,2,3,384]{3,2,1,0:T(4,128)(2,1)S(1)}, bf16[14,2,3,384]{3,2,1,0:T(4,128)(2,1)S(1)}, u32[]{:S(2)}, u32[]{:S(2)}) collective-permute-start(bf16[14,2,3,384]{3,2,1,0:T(4,128)(2,1)S(1)} %get-tuple-element.39), channel_id=1, source_target_pairs={{1,2},{2,1},{3,4},{4,3},{5,6},{6,5},{9,10},{10,9},{11,12},{12,11},... | collective-permute-start | bytes 193544 | tf_op jit(solution)/shard_map/ppermute | solution.py:22
  8.6 4.3 %collective-permute-start.3 = (bf16[14,2,3,384]{3,2,1,0:T(4,128)(2,1)S(1)}, bf16[14,2,3,384]{3,2,1,0:T(4,128)(2,1)S(1)}, u32[]{:S(2)}, u32[]{:S(2)}) collective-permute-start(bf16[14,2,3,384]{3,2,1,0:T(4,128)(2,1)S(1)} %get-tuple-element.40), channel_id=1, source_target_pairs={{0,1},{1,0},{2,3},{3,2},{4,5},{5,4},{6,7},{7,6},{8,9},{9,8},{10,11... | collective-permute-start | bytes 193544 | tf_op jit(solution)/shard_map/ppermute | solution.py:22
  13.0 0.0 collective-permute-done.1.two_ref
  13.0 3.8 %shard_map.110 = (bf16[2,4,8,384]{3,2,1,0:T(8,128)(2,1)S(1)}, bf16[2,4,8,384]{3,2,1,0:T(8,128)(2,1)S(1)}, bf16[2,4,8,384]{3,2,1,0:T(8,128)(2,1)S(1)}, bf16[2,4,8,384]{3,2,1,0:T(8,128)(2,1)S(1)}) custom-call(bf16[8,8,384]{2,1,0:T(8,128)(2,1)S(1)} %reshape.20.own_ref, bf16[8,8,384]{2,1,0:T(8,128)(2,1)S(1)} %collective-permute-done.one_ref, ...), custom_call_target="tpu_custom_call" | custom-call | flops 4000000000 | bytes 4000000 | tf_op jit(solution)/shard_map/pallas_call | solution.py:365
  16.8 0.0 collective-permute-done.4
  16.8 0.0 collective-permute-done.3
  16.8 0.1 broadcast_select_fusion
  16.9 0.5 %collective-permute-start.7 = (bf16[2,4,8,384]{3,2,1,0:T(8,128)(2,1)S(1)}, bf16[2,4,8,384]{3,2,1,0:T(8,128)(2,1)S(1)}, u32[]{:S(2)}, u32[]{:S(2)}) collective-permute-start(bf16[2,4,8,384]{3,2,1,0:T(8,128)(2,1)S(1)} %get-tuple-element.32), channel_id=1, source_target_pairs={{0,24},{8,16},{16,8},{24,0},{1,25},{9,17},{17,9},{25,1},{2,26},{10... | collective-permute-start | bytes 147464 | tf_op jit(solution)/shard_map/ppermute | solution.py:603
  17.4 0.8 %collective-permute-start.6 = (bf16[2,4,8,384]{3,2,1,0:T(8,128)(2,1)S(1)}, bf16[2,4,8,384]{3,2,1,0:T(8,128)(2,1)S(1)}, u32[]{:S(2)}, u32[]{:S(2)}) collective-permute-start(bf16[2,4,8,384]{3,2,1,0:T(8,128)(2,1)S(1)} %get-tuple-element.31), channel_id=1, source_target_pairs={{0,16},{8,24},{16,0},{24,8},{1,17},{9,25},{17,1},{25,9},{2,18},{10... | collective-permute-start | bytes 147464 | tf_op jit(solution)/shard_map/ppermute | solution.py:603
  18.2 0.6 %collective-permute-start.5 = (bf16[2,4,8,384]{3,2,1,0:T(8,128)(2,1)S(1)}, bf16[2,4,8,384]{3,2,1,0:T(8,128)(2,1)S(1)}, u32[]{:S(2)}, u32[]{:S(2)}) collective-permute-start(bf16[2,4,8,384]{3,2,1,0:T(8,128)(2,1)S(1)} %get-tuple-element.30), channel_id=1, source_target_pairs={{0,8},{8,0},{16,24},{24,16},{1,9},{9,1},{17,25},{25,17},{2,10},{10... | collective-permute-start | bytes 147464 | tf_op jit(solution)/shard_map/ppermute | solution.py:603
  18.8 0.2 pad_maximum_fusion.4
  19.1 11.2 %shard_map.111 = f32[8,2,4,384]{3,2,1,0:T(4,128)S(1)} custom-call(bf16[2,224,384]{2,1,0:T(8,128)(2,1)S(1)} %pad_maximum_fusion.window_ref, f32[16,128]{1,0:T(8,128)S(1)} %get-tuple-element.20.scalars_ref, bf16[3,3,3,2,64]{4,3,2,1,0:T(2,128)(2,1)} %bitcast.19, bf16[3,3,3,64,64]{4,3,2,1,0:T(8,128)(2,1)} %bitcast.17, bf16[3,3,3,2,64]{4,3,2,1,0:T(2,128)(2,1)} %bitcast.20, ...), custom_call_target="tpu_custom_call" | custom-call | flops 10000000000 | bytes 2000000 | tf_op jit(solution)/shard_map/pallas_call | solution.py:547
  30.3 0.0 collective-permute-done.7
  30.3 0.0 collective-permute-done.6
  30.3 0.0 collective-permute-done.5
  30.4 0.7 %sub.3 = f32[2,4,2,4,384]{4,3,2,1,0:T(4,128)} subtract(f32[2,4,2,4,384]{4,3,2,1,0:T(4,128)S(1)} %bitcast.11, f32[2,4,2,4,384]{4,3,2,1,0:T(4,128)S(1)} %reshape.24) | non-fusion elementwise | flops 24576 | bytes 294912 | tf_op jit(solution)/shard_map/sub | solution.py:614
  (8 shorter events, 0.2 us)
Async XLA Ops:
  0.9 6.1 %collective-permute-start = (bf16[8,8,384]{2,1,0:T(8,128)(2,1)S(1)}, bf16[8,8,384]{2,1,0:T(8,128)(2,1)S(1)}, u32[]{:S(2)}, u32[]{:S(2)}) collective-permute-start(bf16[8,8,384]{2,1,0:T(8,128)(2,1)S(1)} %reshape.20.own_ref), channel_id=1, source_target_pairs={{0,8},{8,0},{16,24},{24,16},{1,9},{9,1},{17,25},{25,17},{2,10},{10... | collective-permute-start | bytes 147464 | tf_op jit(solution)/shard_map/ppermute | solution.py:590
  1.5 11.5 %collective-permute-start.1 = (bf16[8,8,384]{2,1,0:T(8,128)(2,1)S(1)}, bf16[8,8,384]{2,1,0:T(8,128)(2,1)S(1)}, u32[]{:S(2)}, u32[]{:S(2)}) collective-permute-start(bf16[8,8,384]{2,1,0:T(8,128)(2,1)S(1)} %reshape.20.own_ref), channel_id=1, source_target_pairs={{0,16},{8,24},{16,0},{24,8},{1,17},{9,25},{17,1},{25,9},{2,18},{10... | collective-permute-start | bytes 147464 | tf_op jit(solution)/shard_map/ppermute | solution.py:590
  4.0 3.7 %collective-permute-start.2 = (bf16[8,8,384]{2,1,0:T(8,128)(2,1)S(1)}, bf16[8,8,384]{2,1,0:T(8,128)(2,1)S(1)}, u32[]{:S(2)}, u32[]{:S(2)}) collective-permute-start(bf16[8,8,384]{2,1,0:T(8,128)(2,1)S(1)} %reshape.20.own_ref), channel_id=1, source_target_pairs={{0,24},{8,16},{16,8},{24,0},{1,25},{9,17},{17,9},{25,1},{2,26},{10... | collective-permute-start | bytes 147464 | tf_op jit(solution)/shard_map/ppermute | solution.py:590
  8.0 8.8 %collective-permute-start.4 = (bf16[14,2,3,384]{3,2,1,0:T(4,128)(2,1)S(1)}, bf16[14,2,3,384]{3,2,1,0:T(4,128)(2,1)S(1)}, u32[]{:S(2)}, u32[]{:S(2)}) collective-permute-start(bf16[14,2,3,384]{3,2,1,0:T(4,128)(2,1)S(1)} %get-tuple-element.39), channel_id=1, source_target_pairs={{1,2},{2,1},{3,4},{4,3},{5,6},{6,5},{9,10},{10,9},{11,12},{12,11},... | collective-permute-start | bytes 193544 | tf_op jit(solution)/shard_map/ppermute | solution.py:22
  8.6 8.1 %collective-permute-start.3 = (bf16[14,2,3,384]{3,2,1,0:T(4,128)(2,1)S(1)}, bf16[14,2,3,384]{3,2,1,0:T(4,128)(2,1)S(1)}, u32[]{:S(2)}, u32[]{:S(2)}) collective-permute-start(bf16[14,2,3,384]{3,2,1,0:T(4,128)(2,1)S(1)} %get-tuple-element.40), channel_id=1, source_target_pairs={{0,1},{1,0},{2,3},{3,2},{4,5},{5,4},{6,7},{7,6},{8,9},{9,8},{10,11... | collective-permute-start | bytes 193544 | tf_op jit(solution)/shard_map/ppermute | solution.py:22
  16.9 13.4 %collective-permute-start.7 = (bf16[2,4,8,384]{3,2,1,0:T(8,128)(2,1)S(1)}, bf16[2,4,8,384]{3,2,1,0:T(8,128)(2,1)S(1)}, u32[]{:S(2)}, u32[]{:S(2)}) collective-permute-start(bf16[2,4,8,384]{3,2,1,0:T(8,128)(2,1)S(1)} %get-tuple-element.32), channel_id=1, source_target_pairs={{0,24},{8,16},{16,8},{24,0},{1,25},{9,17},{17,9},{25,1},{2,26},{10... | collective-permute-start | bytes 147464 | tf_op jit(solution)/shard_map/ppermute | solution.py:603
  17.4 12.9 %collective-permute-start.6 = (bf16[2,4,8,384]{3,2,1,0:T(8,128)(2,1)S(1)}, bf16[2,4,8,384]{3,2,1,0:T(8,128)(2,1)S(1)}, u32[]{:S(2)}, u32[]{:S(2)}) collective-permute-start(bf16[2,4,8,384]{3,2,1,0:T(8,128)(2,1)S(1)} %get-tuple-element.31), channel_id=1, source_target_pairs={{0,16},{8,24},{16,0},{24,8},{1,17},{9,25},{17,1},{25,9},{2,18},{10... | collective-permute-start | bytes 147464 | tf_op jit(solution)/shard_map/ppermute | solution.py:603
  18.2 12.1 %collective-permute-start.5 = (bf16[2,4,8,384]{3,2,1,0:T(8,128)(2,1)S(1)}, bf16[2,4,8,384]{3,2,1,0:T(8,128)(2,1)S(1)}, u32[]{:S(2)}, u32[]{:S(2)}) collective-permute-start(bf16[2,4,8,384]{3,2,1,0:T(8,128)(2,1)S(1)} %get-tuple-element.30), channel_id=1, source_target_pairs={{0,8},{8,0},{16,24},{24,16},{1,9},{9,1},{17,25},{25,17},{2,10},{10... | collective-permute-start | bytes 147464 | tf_op jit(solution)/shard_map/ppermute | solution.py:603

commit v10 on v6

--- a/solution.py
+++ b/solution.py
@@ -141,11 +141,9 @@
         store(lax.rem(j + whole, tiles), jnp.where(lane < part, moved[j - 1], moved[j]))
 
 
-def fill_weights(first_raw, mid_raw, last_raw, first_sum, last_sum, first_ref, wide_ref, last_ref):
-    channels = mid_raw.shape[-1]
-    two = 2 * channels
+def fill_first(first_raw, first_sum, first_ref):
+    channels = first_raw.shape[-1]
     first_sum[...] = jnp.zeros_like(first_sum)
-    last_sum[...] = jnp.zeros_like(last_sum)
     for d in range(3):
         for u in range(3):
             for t in range(3):
@@ -156,13 +154,22 @@
                         first_sum[row : row + 1, r * channels : (r + 1) * channels] = block[
                             i : i + 1
                         ]
+    first_ref[...] = first_sum[...].T[:, : first_ref.shape[1]].astype(jnp.bfloat16)
+
+
+def fill_others(mid_raw, last_raw, last_sum, wide_ref, last_ref):
+    channels = mid_raw.shape[-1]
+    two = 2 * channels
+    last_sum[...] = jnp.zeros_like(last_sum)
+    for d in range(3):
+        for u in range(3):
+            for t in range(3):
                 block = last_raw[d, u, t].astype(jnp.float32)
                 for o in range(2):
                     for r in range(4):
                         row = (d * 3 + t) * 8 + o * 4 + r
                         col = (r + u) * channels
                         last_sum[row : row + 1, col : col + channels] = block[o : o + 1]
-    first_ref[...] = first_sum[...].T[:, : first_ref.shape[1]].astype(jnp.bfloat16)
     last_ref[...] = last_sum[...].astype(jnp.bfloat16)
     half_weight = jnp.bfloat16(0.5)
     for t in range(3):
@@ -418,9 +425,7 @@
 
     for copy in copies[:3]:
         copy.wait()
-    fill_weights(
-        first_raw, mid_raw, last_raw, first_sum, last_sum, first_ref, wide_ref, last_ref
-    )
+    fill_first(first_raw, first_sum, first_ref)
 
     def first_layer(z):
         source = jnp.concatenate(
@@ -491,6 +496,7 @@
         source = jnp.concatenate([f2_ref[z], f2_ref[z + 1]], axis=1)
         score_ref[z // 2] = jnp.dot(last_ref[...], source, preferred_element_type=jnp.float32)
 
+    fill_others(mid_raw, last_raw, last_sum, wide_ref, last_ref)
     for z in range(4):
         first_layer(z)
     waiting = None
@@ -602,7 +608,7 @@
     sums = partial_consistency(images, prepared, measured_kspace, sample_mask)
     sums, below, above = lax.optimization_barrier((sums, below, above))
     arrived = [lax.ppermute(part, "band", route) for part, route in zip(sums[1:], routes)]
-    field = jnp.concatenate([below, tall, above, jnp.zeros_like(above[:, :, :2])], axis=2)
+    field = jnp.concatenate([below, tall, above, above[:, :, :2]], axis=2)
     windows = jnp.stack(
         [field[:, :, 4 * g : 4 * g + 8].reshape(-1, columns) for g in range(2)], axis=0
     )

time: 30.9 us -> 31 us (level)
  no operation moved by 1% of the time
where the time goes in v10:
time: 31 us; the launch traced here: 30.7 us
  Pallas kernels  16.8 us (54%)
  starting transfers between devices  10.1 us (33%)
  other arithmetic  2.18 us (7%)
  between operations  0.84 us (3%)
  waiting for transfers between devices  0.71 us (2%)
    pallas_call x1, Pallas kernels, stepped_without_data(): pl.pallas_call(network_kernel, out_shape=jax.ShapeDtypeStruct(local, jnp....  10.8 us
    ppermute x2, starting transfers between devices, exchanged_rows(): arrived.append(lax.ppermute(sent, 'slab', route))  5.01 us
    pallas_call x1, Pallas kernels, partial_consistency(): pl.pallas_call(consistency_kernel, out_shape=(part,) * 4, in_specs=[vmem]...  3.77 us
    ppermute x3, starting transfers between devices, per_device(): images = [own] + [lax.ppermute(own, 'band', route) for route in routes]  3.15 us
    pallas_call x1, Pallas kernels, preparation(): pl.pallas_call(preparation_kernel, out_shape=(jax.ShapeDtypeStruct(turned...  2.24 us
    ppermute x3, starting transfers between devices, per_device(): lax.ppermute(part, 'band', route)  1.93 us
    convert_element_type x1, other arithmetic, per_device(): current_image.astype(jnp.bfloat16)  0.91 us
    ppermute x3, waiting for transfers between devices, per_device(): images = [own] + [lax.ppermute(own, 'band', route) for route in routes]  0.7 us
  transfers between devices with their start and end apart: 8, of which 1 were waited for; matrix products, arithmetic and copies ran while one was open for 2% of the time, Pallas kernels for 55%

profile of v10, /device:TPU:0, one launch (start us, length us, event | category | flops | bytes accessed | tf_op | source)
XLA Modules:
  0.0 30.7 jit_solution(3959325861364201603)
XLA Ops:
  0.0 0.9 %convert_element_type.15 = bf16[2,4,2,4,384]{4,3,2,1,0:T(4,128)(2,1)S(1)} convert(f32[2,4,2,4,384]{4,3,2,1,0:T(4,128)} %param.11) | non-fusion elementwise | flops 24576 | bytes 147456 | tf_op jit(solution)/shard_map/convert_element_type | solution.py:595
  0.9 0.5 %collective-permute-start = (bf16[8,8,384]{2,1,0:T(8,128)(2,1)S(1)}, bf16[8,8,384]{2,1,0:T(8,128)(2,1)S(1)}, u32[]{:S(2)}, u32[]{:S(2)}) collective-permute-start(bf16[8,8,384]{2,1,0:T(8,128)(2,1)S(1)} %reshape.20.own_ref), channel_id=1, source_target_pairs={{0,8},{8,0},{16,24},{24,16},{1,9},{9,1},{17,25},{25,17},{2,10},{10... | collective-permute-start | bytes 147464 | tf_op jit(solution)/shard_map/ppermute | solution.py:597
  1.5 2.6 %collective-permute-start.1 = (bf16[8,8,384]{2,1,0:T(8,128)(2,1)S(1)}, bf16[8,8,384]{2,1,0:T(8,128)(2,1)S(1)}, u32[]{:S(2)}, u32[]{:S(2)}) collective-permute-start(bf16[8,8,384]{2,1,0:T(8,128)(2,1)S(1)} %reshape.20.own_ref), channel_id=1, source_target_pairs={{0,16},{8,24},{16,0},{24,8},{1,17},{9,25},{17,1},{25,9},{2,18},{10... | collective-permute-start | bytes 147464 | tf_op jit(solution)/shard_map/ppermute | solution.py:597
  4.0 0.1 collective-permute-start.2
  4.7 2.2 %shard_map.109 = (bf16[3,8,4,64,128]{4,3,2,1,0:T(8,128)(2,1)S(1)}, f32[16,128]{1,0:T(8,128)S(1)}, bf16[384,768]{1,0:T(8,128)(2,1)S(1)}, bf16[384,768]{1,0:T(8,128)(2,1)S(1)}) custom-call(f32[1]{0:T(128)S(6)} %copy.12.size_ref, s32[8]{0:T(128)} %steps_hbm.1, s32[8]{0:T(128)} %order_hbm.1, bf16[8,4,8,2,4,384]{5,4,3,2,1,0:T(4,128)(2,1)} %coil_hbm.1), custom_call_target="tpu_custom_call" | custom-call | flops 4000000000 | bytes 4000000 | tf_op jit(solution)/shard_map/pallas_call | solution.py:233
  7.0 0.0 collective-permute-done.one_ref
  7.0 0.7 %collective-permute-done.2.three_ref = bf16[8,8,384]{2,1,0:T(8,128)(2,1)S(1)} collective-permute-done((bf16[8,8,384]{2,1,0:T(8,128)(2,1)S(1)}, bf16[8,8,384]{2,1,0:T(8,128)(2,1)S(1)}, u32[]{:S(2)}, u32[]{:S(2)}) %collective-permute-start.2) | collective-permute-done | bytes 49184 | tf_op jit(solution)/shard_map/ppermute | solution.py:597
  7.8 0.1 pad_maximum_fusion.9
  7.8 0.1 broadcast_select_fusion.2
  8.0 0.7 %collective-permute-start.4 = (bf16[14,2,3,384]{3,2,1,0:T(4,128)(2,1)S(1)}, bf16[14,2,3,384]{3,2,1,0:T(4,128)(2,1)S(1)}, u32[]{:S(2)}, u32[]{:S(2)}) collective-permute-start(bf16[14,2,3,384]{3,2,1,0:T(4,128)(2,1)S(1)} %get-tuple-element.39), channel_id=1, source_target_pairs={{1,2},{2,1},{3,4},{4,3},{5,6},{6,5},{9,10},{10,9},{11,12},{12,11},... | collective-permute-start | bytes 193544 | tf_op jit(solution)/shard_map/ppermute | solution.py:22
  8.6 4.3 %collective-permute-start.3 = (bf16[14,2,3,384]{3,2,1,0:T(4,128)(2,1)S(1)}, bf16[14,2,3,384]{3,2,1,0:T(4,128)(2,1)S(1)}, u32[]{:S(2)}, u32[]{:S(2)}) collective-permute-start(bf16[14,2,3,384]{3,2,1,0:T(4,128)(2,1)S(1)} %get-tuple-element.40), channel_id=1, source_target_pairs={{0,1},{1,0},{2,3},{3,2},{4,5},{5,4},{6,7},{7,6},{8,9},{9,8},{10,11... | collective-permute-start | bytes 193544 | tf_op jit(solution)/shard_map/ppermute | solution.py:22
  13.0 0.0 collective-permute-done.1.two_ref
  13.0 3.8 %shard_map.110 = (bf16[2,4,8,384]{3,2,1,0:T(8,128)(2,1)S(1)}, bf16[2,4,8,384]{3,2,1,0:T(8,128)(2,1)S(1)}, bf16[2,4,8,384]{3,2,1,0:T(8,128)(2,1)S(1)}, bf16[2,4,8,384]{3,2,1,0:T(8,128)(2,1)S(1)}) custom-call(bf16[8,8,384]{2,1,0:T(8,128)(2,1)S(1)} %reshape.20.own_ref, bf16[8,8,384]{2,1,0:T(8,128)(2,1)S(1)} %collective-permute-done.one_ref, ...), custom_call_target="tpu_custom_call" | custom-call | flops 4000000000 | bytes 4000000 | tf_op jit(solution)/shard_map/pallas_call | solution.py:373
  16.8 0.0 collective-permute-done.4
  16.8 0.0 collective-permute-done.3
  16.8 0.1 broadcast_select_fusion
  16.9 0.5 %collective-permute-start.7 = (bf16[2,4,8,384]{3,2,1,0:T(8,128)(2,1)S(1)}, bf16[2,4,8,384]{3,2,1,0:T(8,128)(2,1)S(1)}, u32[]{:S(2)}, u32[]{:S(2)}) collective-permute-start(bf16[2,4,8,384]{3,2,1,0:T(8,128)(2,1)S(1)} %get-tuple-element.32), channel_id=1, source_target_pairs={{0,24},{8,16},{16,8},{24,0},{1,25},{9,17},{17,9},{25,1},{2,26},{10... | collective-permute-start | bytes 147464 | tf_op jit(solution)/shard_map/ppermute | solution.py:610
  17.4 0.8 %collective-permute-start.6 = (bf16[2,4,8,384]{3,2,1,0:T(8,128)(2,1)S(1)}, bf16[2,4,8,384]{3,2,1,0:T(8,128)(2,1)S(1)}, u32[]{:S(2)}, u32[]{:S(2)}) collective-permute-start(bf16[2,4,8,384]{3,2,1,0:T(8,128)(2,1)S(1)} %get-tuple-element.31), channel_id=1, source_target_pairs={{0,16},{8,24},{16,0},{24,8},{1,17},{9,25},{17,1},{25,9},{2,18},{10... | collective-permute-start | bytes 147464 | tf_op jit(solution)/shard_map/ppermute | solution.py:610
  18.2 0.6 %collective-permute-start.5 = (bf16[2,4,8,384]{3,2,1,0:T(8,128)(2,1)S(1)}, bf16[2,4,8,384]{3,2,1,0:T(8,128)(2,1)S(1)}, u32[]{:S(2)}, u32[]{:S(2)}) collective-permute-start(bf16[2,4,8,384]{3,2,1,0:T(8,128)(2,1)S(1)} %get-tuple-element.30), channel_id=1, source_target_pairs={{0,8},{8,0},{16,24},{24,16},{1,9},{9,1},{17,25},{25,17},{2,10},{10... | collective-permute-start | bytes 147464 | tf_op jit(solution)/shard_map/ppermute | solution.py:610
  18.8 0.3 pad_maximum_fusion.5
  19.2 10.8 %shard_map.111 = f32[8,2,4,384]{3,2,1,0:T(4,128)S(1)} custom-call(bf16[2,224,384]{2,1,0:T(8,128)(2,1)S(1)} %pad_maximum_fusion.window_ref, f32[16,128]{1,0:T(8,128)S(1)} %get-tuple-element.20.scalars_ref, bf16[3,3,3,2,64]{4,3,2,1,0:T(2,128)(2,1)} %bitcast.19, bf16[3,3,3,64,64]{4,3,2,1,0:T(8,128)(2,1)} %bitcast.17, bf16[3,3,3,2,64]{4,3,2,1,0:T(2,128)(2,1)} %bitcast.20, ...), custom_call_target="tpu_custom_call" | custom-call | flops 10000000000 | bytes 2000000 | tf_op jit(solution)/shard_map/pallas_call | solution.py:554
  29.9 0.0 collective-permute-done.7
  30.0 0.0 collective-permute-done.6
  30.0 0.0 collective-permute-done.5
  30.0 0.7 %sub.3 = f32[2,4,2,4,384]{4,3,2,1,0:T(4,128)} subtract(f32[2,4,2,4,384]{4,3,2,1,0:T(4,128)S(1)} %bitcast.11, f32[2,4,2,4,384]{4,3,2,1,0:T(4,128)S(1)} %reshape.24) | non-fusion elementwise | flops 24576 | bytes 294912 | tf_op jit(solution)/shard_map/sub | solution.py:621
  (8 shorter events, 0.2 us)
Async XLA Ops:
  0.9 6.1 %collective-permute-start = (bf16[8,8,384]{2,1,0:T(8,128)(2,1)S(1)}, bf16[8,8,384]{2,1,0:T(8,128)(2,1)S(1)}, u32[]{:S(2)}, u32[]{:S(2)}) collective-permute-start(bf16[8,8,384]{2,1,0:T(8,128)(2,1)S(1)} %reshape.20.own_ref), channel_id=1, source_target_pairs={{0,8},{8,0},{16,24},{24,16},{1,9},{9,1},{17,25},{25,17},{2,10},{10... | collective-permute-start | bytes 147464 | tf_op jit(solution)/shard_map/ppermute | solution.py:597
  1.5 11.5 %collective-permute-start.1 = (bf16[8,8,384]{2,1,0:T(8,128)(2,1)S(1)}, bf16[8,8,384]{2,1,0:T(8,128)(2,1)S(1)}, u32[]{:S(2)}, u32[]{:S(2)}) collective-permute-start(bf16[8,8,384]{2,1,0:T(8,128)(2,1)S(1)} %reshape.20.own_ref), channel_id=1, source_target_pairs={{0,16},{8,24},{16,0},{24,8},{1,17},{9,25},{17,1},{25,9},{2,18},{10... | collective-permute-start | bytes 147464 | tf_op jit(solution)/shard_map/ppermute | solution.py:597
  4.0 3.7 %collective-permute-start.2 = (bf16[8,8,384]{2,1,0:T(8,128)(2,1)S(1)}, bf16[8,8,384]{2,1,0:T(8,128)(2,1)S(1)}, u32[]{:S(2)}, u32[]{:S(2)}) collective-permute-start(bf16[8,8,384]{2,1,0:T(8,128)(2,1)S(1)} %reshape.20.own_ref), channel_id=1, source_target_pairs={{0,24},{8,16},{16,8},{24,0},{1,25},{9,17},{17,9},{25,1},{2,26},{10... | collective-permute-start | bytes 147464 | tf_op jit(solution)/shard_map/ppermute | solution.py:597
  8.0 8.8 %collective-permute-start.4 = (bf16[14,2,3,384]{3,2,1,0:T(4,128)(2,1)S(1)}, bf16[14,2,3,384]{3,2,1,0:T(4,128)(2,1)S(1)}, u32[]{:S(2)}, u32[]{:S(2)}) collective-permute-start(bf16[14,2,3,384]{3,2,1,0:T(4,128)(2,1)S(1)} %get-tuple-element.39), channel_id=1, source_target_pairs={{1,2},{2,1},{3,4},{4,3},{5,6},{6,5},{9,10},{10,9},{11,12},{12,11},... | collective-permute-start | bytes 193544 | tf_op jit(solution)/shard_map/ppermute | solution.py:22
  8.6 8.1 %collective-permute-start.3 = (bf16[14,2,3,384]{3,2,1,0:T(4,128)(2,1)S(1)}, bf16[14,2,3,384]{3,2,1,0:T(4,128)(2,1)S(1)}, u32[]{:S(2)}, u32[]{:S(2)}) collective-permute-start(bf16[14,2,3,384]{3,2,1,0:T(4,128)(2,1)S(1)} %get-tuple-element.40), channel_id=1, source_target_pairs={{0,1},{1,0},{2,3},{3,2},{4,5},{5,4},{6,7},{7,6},{8,9},{9,8},{10,11... | collective-permute-start | bytes 193544 | tf_op jit(solution)/shard_map/ppermute | solution.py:22
  16.9 13.0 %collective-permute-start.7 = (bf16[2,4,8,384]{3,2,1,0:T(8,128)(2,1)S(1)}, bf16[2,4,8,384]{3,2,1,0:T(8,128)(2,1)S(1)}, u32[]{:S(2)}, u32[]{:S(2)}) collective-permute-start(bf16[2,4,8,384]{3,2,1,0:T(8,128)(2,1)S(1)} %get-tuple-element.32), channel_id=1, source_target_pairs={{0,24},{8,16},{16,8},{24,0},{1,25},{9,17},{17,9},{25,1},{2,26},{10... | collective-permute-start | bytes 147464 | tf_op jit(solution)/shard_map/ppermute | solution.py:610
  17.4 12.5 %collective-permute-start.6 = (bf16[2,4,8,384]{3,2,1,0:T(8,128)(2,1)S(1)}, bf16[2,4,8,384]{3,2,1,0:T(8,128)(2,1)S(1)}, u32[]{:S(2)}, u32[]{:S(2)}) collective-permute-start(bf16[2,4,8,384]{3,2,1,0:T(8,128)(2,1)S(1)} %get-tuple-element.31), channel_id=1, source_target_pairs={{0,16},{8,24},{16,0},{24,8},{1,17},{9,25},{17,1},{25,9},{2,18},{10... | collective-permute-start | bytes 147464 | tf_op jit(solution)/shard_map/ppermute | solution.py:610
  18.2 11.8 %collective-permute-start.5 = (bf16[2,4,8,384]{3,2,1,0:T(8,128)(2,1)S(1)}, bf16[2,4,8,384]{3,2,1,0:T(8,128)(2,1)S(1)}, u32[]{:S(2)}, u32[]{:S(2)}) collective-permute-start(bf16[2,4,8,384]{3,2,1,0:T(8,128)(2,1)S(1)} %get-tuple-element.30), channel_id=1, source_target_pairs={{0,8},{8,0},{16,24},{24,16},{1,9},{9,1},{17,25},{25,17},{2,10},{10... | collective-permute-start | bytes 147464 | tf_op jit(solution)/shard_map/ppermute | solution.py:610

commit v11 on v6

--- a/solution.py
+++ b/solution.py
@@ -341,12 +341,12 @@
                         upper_half(straight), straight, crossed
                     )
 
-    for half in halves:
-        collapse(half)
-    for half in halves:
-        project(half)
-    for half in halves:
-        combine(half)
+    collapse(halves[0])
+    project(halves[0])
+    collapse(halves[1])
+    combine(halves[0])
+    project(halves[1])
+    combine(halves[1])
 
     outs = (own_out, one_out, two_out, three_out)
     for k, (x, p, _, shift) in enumerate(owners):

time: 30.9 us -> 30.9 us (level)
  no operation moved by 1% of the time
where the time goes in v11:
time: 30.9 us; the launch traced here: 30.6 us
  Pallas kernels  16.8 us (54%)
  starting transfers between devices  10.1 us (33%)
  other arithmetic  2.14 us (7%)
  between operations  0.8 us (3%)
  waiting for transfers between devices  0.66 us (2%)
    pallas_call x1, Pallas kernels, stepped_without_data(): pl.pallas_call(network_kernel, out_shape=jax.ShapeDtypeStruct(local, jnp....  10.8 us
    ppermute x2, starting transfers between devices, exchanged_rows(): arrived.append(lax.ppermute(sent, 'slab', route))  5.01 us
    pallas_call x1, Pallas kernels, partial_consistency(): pl.pallas_call(consistency_kernel, out_shape=(part,) * 4, in_specs=[vmem]...  3.77 us
    ppermute x3, starting transfers between devices, per_device(): images = [own] + [lax.ppermute(own, 'band', route) for route in routes]  3.15 us
    pallas_call x1, Pallas kernels, preparation(): pl.pallas_call(preparation_kernel, out_shape=(jax.ShapeDtypeStruct(turned...  2.24 us
    ppermute x3, starting transfers between devices, per_device(): lax.ppermute(part, 'band', route)  1.93 us
    convert_element_type x1, other arithmetic, per_device(): current_image.astype(jnp.bfloat16)  0.91 us
    sub x1, other arithmetic, per_device(): return base - total.reshape(base.shape)  0.67 us
  transfers between devices with their start and end apart: 8, of which 1 were waited for; matrix products, arithmetic and copies ran while one was open for 2% of the time, Pallas kernels for 55%

profile of v11, /device:TPU:0, one launch (start us, length us, event | category | flops | bytes accessed | tf_op | source)
XLA Modules:
  0.0 30.6 jit_solution(3462308428803358803)
XLA Ops:
  0.0 0.9 %convert_element_type.15 = bf16[2,4,2,4,384]{4,3,2,1,0:T(4,128)(2,1)S(1)} convert(f32[2,4,2,4,384]{4,3,2,1,0:T(4,128)} %param.11) | non-fusion elementwise | flops 24576 | bytes 147456 | tf_op jit(solution)/shard_map/convert_element_type | solution.py:589
  0.9 0.5 %collective-permute-start = (bf16[8,8,384]{2,1,0:T(8,128)(2,1)S(1)}, bf16[8,8,384]{2,1,0:T(8,128)(2,1)S(1)}, u32[]{:S(2)}, u32[]{:S(2)}) collective-permute-start(bf16[8,8,384]{2,1,0:T(8,128)(2,1)S(1)} %reshape.20.own_ref), channel_id=1, source_target_pairs={{0,8},{8,0},{16,24},{24,16},{1,9},{9,1},{17,25},{25,17},{2,10},{10... | collective-permute-start | bytes 147464 | tf_op jit(solution)/shard_map/ppermute | solution.py:591
  1.5 2.6 %collective-permute-start.1 = (bf16[8,8,384]{2,1,0:T(8,128)(2,1)S(1)}, bf16[8,8,384]{2,1,0:T(8,128)(2,1)S(1)}, u32[]{:S(2)}, u32[]{:S(2)}) collective-permute-start(bf16[8,8,384]{2,1,0:T(8,128)(2,1)S(1)} %reshape.20.own_ref), channel_id=1, source_target_pairs={{0,16},{8,24},{16,0},{24,8},{1,17},{9,25},{17,1},{25,9},{2,18},{10... | collective-permute-start | bytes 147464 | tf_op jit(solution)/shard_map/ppermute | solution.py:591
  4.0 0.1 collective-permute-start.2
  4.7 2.2 %shard_map.109 = (bf16[3,8,4,64,128]{4,3,2,1,0:T(8,128)(2,1)S(1)}, f32[16,128]{1,0:T(8,128)S(1)}, bf16[384,768]{1,0:T(8,128)(2,1)S(1)}, bf16[384,768]{1,0:T(8,128)(2,1)S(1)}) custom-call(f32[1]{0:T(128)S(6)} %copy.12.size_ref, s32[8]{0:T(128)} %steps_hbm.1, s32[8]{0:T(128)} %order_hbm.1, bf16[8,4,8,2,4,384]{5,4,3,2,1,0:T(4,128)(2,1)} %coil_hbm.1), custom_call_target="tpu_custom_call" | custom-call | flops 4000000000 | bytes 4000000 | tf_op jit(solution)/shard_map/pallas_call | solution.py:226
  7.0 0.1 pad_slice_fusion
  7.1 0.0 collective-permute-done.one_ref
  7.1 0.6 %collective-permute-done.2.three_ref = bf16[8,8,384]{2,1,0:T(8,128)(2,1)S(1)} collective-permute-done((bf16[8,8,384]{2,1,0:T(8,128)(2,1)S(1)}, bf16[8,8,384]{2,1,0:T(8,128)(2,1)S(1)}, u32[]{:S(2)}, u32[]{:S(2)}) %collective-permute-start.2) | collective-permute-done | bytes 49184 | tf_op jit(solution)/shard_map/ppermute | solution.py:591
  7.8 0.1 pad_maximum_fusion.8
  7.8 0.1 broadcast_select_fusion.2
  8.0 0.7 %collective-permute-start.4 = (bf16[14,2,3,384]{3,2,1,0:T(4,128)(2,1)S(1)}, bf16[14,2,3,384]{3,2,1,0:T(4,128)(2,1)S(1)}, u32[]{:S(2)}, u32[]{:S(2)}) collective-permute-start(bf16[14,2,3,384]{3,2,1,0:T(4,128)(2,1)S(1)} %get-tuple-element.39), channel_id=1, source_target_pairs={{1,2},{2,1},{3,4},{4,3},{5,6},{6,5},{9,10},{10,9},{11,12},{12,11},... | collective-permute-start | bytes 193544 | tf_op jit(solution)/shard_map/ppermute | solution.py:22
  8.6 4.3 %collective-permute-start.3 = (bf16[14,2,3,384]{3,2,1,0:T(4,128)(2,1)S(1)}, bf16[14,2,3,384]{3,2,1,0:T(4,128)(2,1)S(1)}, u32[]{:S(2)}, u32[]{:S(2)}) collective-permute-start(bf16[14,2,3,384]{3,2,1,0:T(4,128)(2,1)S(1)} %get-tuple-element.40), channel_id=1, source_target_pairs={{0,1},{1,0},{2,3},{3,2},{4,5},{5,4},{6,7},{7,6},{8,9},{9,8},{10,11... | collective-permute-start | bytes 193544 | tf_op jit(solution)/shard_map/ppermute | solution.py:22
  13.0 0.0 collective-permute-done.1.two_ref
  13.0 3.8 %shard_map.110 = (bf16[2,4,8,384]{3,2,1,0:T(8,128)(2,1)S(1)}, bf16[2,4,8,384]{3,2,1,0:T(8,128)(2,1)S(1)}, bf16[2,4,8,384]{3,2,1,0:T(8,128)(2,1)S(1)}, bf16[2,4,8,384]{3,2,1,0:T(8,128)(2,1)S(1)}) custom-call(bf16[8,8,384]{2,1,0:T(8,128)(2,1)S(1)} %reshape.20.own_ref, bf16[8,8,384]{2,1,0:T(8,128)(2,1)S(1)} %collective-permute-done.one_ref, ...), custom_call_target="tpu_custom_call" | custom-call | flops 4000000000 | bytes 4000000 | tf_op jit(solution)/shard_map/pallas_call | solution.py:366
  16.8 0.0 collective-permute-done.4
  16.8 0.0 collective-permute-done.3
  16.8 0.1 broadcast_select_fusion
  16.9 0.5 %collective-permute-start.7 = (bf16[2,4,8,384]{3,2,1,0:T(8,128)(2,1)S(1)}, bf16[2,4,8,384]{3,2,1,0:T(8,128)(2,1)S(1)}, u32[]{:S(2)}, u32[]{:S(2)}) collective-permute-start(bf16[2,4,8,384]{3,2,1,0:T(8,128)(2,1)S(1)} %get-tuple-element.32), channel_id=1, source_target_pairs={{0,24},{8,16},{16,8},{24,0},{1,25},{9,17},{17,9},{25,1},{2,26},{10... | collective-permute-start | bytes 147464 | tf_op jit(solution)/shard_map/ppermute | solution.py:604
  17.4 0.8 %collective-permute-start.6 = (bf16[2,4,8,384]{3,2,1,0:T(8,128)(2,1)S(1)}, bf16[2,4,8,384]{3,2,1,0:T(8,128)(2,1)S(1)}, u32[]{:S(2)}, u32[]{:S(2)}) collective-permute-start(bf16[2,4,8,384]{3,2,1,0:T(8,128)(2,1)S(1)} %get-tuple-element.31), channel_id=1, source_target_pairs={{0,16},{8,24},{16,0},{24,8},{1,17},{9,25},{17,1},{25,9},{2,18},{10... | collective-permute-start | bytes 147464 | tf_op jit(solution)/shard_map/ppermute | solution.py:604
  18.2 0.6 %collective-permute-start.5 = (bf16[2,4,8,384]{3,2,1,0:T(8,128)(2,1)S(1)}, bf16[2,4,8,384]{3,2,1,0:T(8,128)(2,1)S(1)}, u32[]{:S(2)}, u32[]{:S(2)}) collective-permute-start(bf16[2,4,8,384]{3,2,1,0:T(8,128)(2,1)S(1)} %get-tuple-element.30), channel_id=1, source_target_pairs={{0,8},{8,0},{16,24},{24,16},{1,9},{9,1},{17,25},{25,17},{2,10},{10... | collective-permute-start | bytes 147464 | tf_op jit(solution)/shard_map/ppermute | solution.py:604
  18.8 0.2 pad_maximum_fusion.4
  19.1 10.8 %shard_map.111 = f32[8,2,4,384]{3,2,1,0:T(4,128)S(1)} custom-call(bf16[2,224,384]{2,1,0:T(8,128)(2,1)S(1)} %pad_maximum_fusion.window_ref, f32[16,128]{1,0:T(8,128)S(1)} %get-tuple-element.20.scalars_ref, bf16[3,3,3,2,64]{4,3,2,1,0:T(2,128)(2,1)} %bitcast.19, bf16[3,3,3,64,64]{4,3,2,1,0:T(8,128)(2,1)} %bitcast.17, bf16[3,3,3,2,64]{4,3,2,1,0:T(2,128)(2,1)} %bitcast.20, ...), custom_call_target="tpu_custom_call" | custom-call | flops 10000000000 | bytes 2000000 | tf_op jit(solution)/shard_map/pallas_call | solution.py:548
  29.9 0.0 collective-permute-done.7
  29.9 0.0 collective-permute-done.6
  29.9 0.0 collective-permute-done.5
  30.0 0.7 %sub.3 = f32[2,4,2,4,384]{4,3,2,1,0:T(4,128)} subtract(f32[2,4,2,4,384]{4,3,2,1,0:T(4,128)S(1)} %bitcast.11, f32[2,4,2,4,384]{4,3,2,1,0:T(4,128)S(1)} %reshape.24) | non-fusion elementwise | flops 24576 | bytes 294912 | tf_op jit(solution)/shard_map/sub | solution.py:615
  (8 shorter events, 0.2 us)
Async XLA Ops:
  0.9 6.1 %collective-permute-start = (bf16[8,8,384]{2,1,0:T(8,128)(2,1)S(1)}, bf16[8,8,384]{2,1,0:T(8,128)(2,1)S(1)}, u32[]{:S(2)}, u32[]{:S(2)}) collective-permute-start(bf16[8,8,384]{2,1,0:T(8,128)(2,1)S(1)} %reshape.20.own_ref), channel_id=1, source_target_pairs={{0,8},{8,0},{16,24},{24,16},{1,9},{9,1},{17,25},{25,17},{2,10},{10... | collective-permute-start | bytes 147464 | tf_op jit(solution)/shard_map/ppermute | solution.py:591
  1.5 11.5 %collective-permute-start.1 = (bf16[8,8,384]{2,1,0:T(8,128)(2,1)S(1)}, bf16[8,8,384]{2,1,0:T(8,128)(2,1)S(1)}, u32[]{:S(2)}, u32[]{:S(2)}) collective-permute-start(bf16[8,8,384]{2,1,0:T(8,128)(2,1)S(1)} %reshape.20.own_ref), channel_id=1, source_target_pairs={{0,16},{8,24},{16,0},{24,8},{1,17},{9,25},{17,1},{25,9},{2,18},{10... | collective-permute-start | bytes 147464 | tf_op jit(solution)/shard_map/ppermute | solution.py:591
  4.0 3.7 %collective-permute-start.2 = (bf16[8,8,384]{2,1,0:T(8,128)(2,1)S(1)}, bf16[8,8,384]{2,1,0:T(8,128)(2,1)S(1)}, u32[]{:S(2)}, u32[]{:S(2)}) collective-permute-start(bf16[8,8,384]{2,1,0:T(8,128)(2,1)S(1)} %reshape.20.own_ref), channel_id=1, source_target_pairs={{0,24},{8,16},{16,8},{24,0},{1,25},{9,17},{17,9},{25,1},{2,26},{10... | collective-permute-start | bytes 147464 | tf_op jit(solution)/shard_map/ppermute | solution.py:591
  8.0 8.8 %collective-permute-start.4 = (bf16[14,2,3,384]{3,2,1,0:T(4,128)(2,1)S(1)}, bf16[14,2,3,384]{3,2,1,0:T(4,128)(2,1)S(1)}, u32[]{:S(2)}, u32[]{:S(2)}) collective-permute-start(bf16[14,2,3,384]{3,2,1,0:T(4,128)(2,1)S(1)} %get-tuple-element.39), channel_id=1, source_target_pairs={{1,2},{2,1},{3,4},{4,3},{5,6},{6,5},{9,10},{10,9},{11,12},{12,11},... | collective-permute-start | bytes 193544 | tf_op jit(solution)/shard_map/ppermute | solution.py:22
  8.6 8.1 %collective-permute-start.3 = (bf16[14,2,3,384]{3,2,1,0:T(4,128)(2,1)S(1)}, bf16[14,2,3,384]{3,2,1,0:T(4,128)(2,1)S(1)}, u32[]{:S(2)}, u32[]{:S(2)}) collective-permute-start(bf16[14,2,3,384]{3,2,1,0:T(4,128)(2,1)S(1)} %get-tuple-element.40), channel_id=1, source_target_pairs={{0,1},{1,0},{2,3},{3,2},{4,5},{5,4},{6,7},{7,6},{8,9},{9,8},{10,11... | collective-permute-start | bytes 193544 | tf_op jit(solution)/shard_map/ppermute | solution.py:22
  16.9 13.0 %collective-permute-start.7 = (bf16[2,4,8,384]{3,2,1,0:T(8,128)(2,1)S(1)}, bf16[2,4,8,384]{3,2,1,0:T(8,128)(2,1)S(1)}, u32[]{:S(2)}, u32[]{:S(2)}) collective-permute-start(bf16[2,4,8,384]{3,2,1,0:T(8,128)(2,1)S(1)} %get-tuple-element.32), channel_id=1, source_target_pairs={{0,24},{8,16},{16,8},{24,0},{1,25},{9,17},{17,9},{25,1},{2,26},{10... | collective-permute-start | bytes 147464 | tf_op jit(solution)/shard_map/ppermute | solution.py:604
  17.4 12.5 %collective-permute-start.6 = (bf16[2,4,8,384]{3,2,1,0:T(8,128)(2,1)S(1)}, bf16[2,4,8,384]{3,2,1,0:T(8,128)(2,1)S(1)}, u32[]{:S(2)}, u32[]{:S(2)}) collective-permute-start(bf16[2,4,8,384]{3,2,1,0:T(8,128)(2,1)S(1)} %get-tuple-element.31), channel_id=1, source_target_pairs={{0,16},{8,24},{16,0},{24,8},{1,17},{9,25},{17,1},{25,9},{2,18},{10... | collective-permute-start | bytes 147464 | tf_op jit(solution)/shard_map/ppermute | solution.py:604
  18.2 11.7 %collective-permute-start.5 = (bf16[2,4,8,384]{3,2,1,0:T(8,128)(2,1)S(1)}, bf16[2,4,8,384]{3,2,1,0:T(8,128)(2,1)S(1)}, u32[]{:S(2)}, u32[]{:S(2)}) collective-permute-start(bf16[2,4,8,384]{3,2,1,0:T(8,128)(2,1)S(1)} %get-tuple-element.30), channel_id=1, source_target_pairs={{0,8},{8,0},{16,24},{24,16},{1,9},{9,1},{17,25},{25,17},{2,10},{10... | collective-permute-start | bytes 147464 | tf_op jit(solution)/shard_map/ppermute | solution.py:604
